TPU v7x, 32 devices: a whole 2x2x4 slice. The times are simulated.
32 devices in a mesh: dp: 4 (over y, x), fsdp: 8 (over z, core).
Axes of the slice: x: 2, y: 2, z: 4, core: 2. Of those that a mesh axis runs over, the one named last changes fastest.
Arguments:
- tokens: bfloat16 [64, 64, 1536], P(('dp', 'fsdp')), may hold values from -6 to 6
- cotangent: bfloat16 [64, 64, 1536], P(('dp', 'fsdp')), may hold values from -6 to 6
- lengths: int32 [64], P(('dp', 'fsdp')), may hold values from 16 to 64, as said below
- in_proj: float32 [1536, 3072], P(None, ('dp', 'fsdp')), may hold values from -0.15625 to 0.15625
- out_proj: float32 [1536, 1536], P(None, ('dp', 'fsdp')), may hold values from -0.875 to 0.875
- gate_up: float32 [2, 1536, 4096], P(None, None, ('dp', 'fsdp')), may hold values from -0.15625 to 0.15625
- down_proj: float32 [4096, 1536], P(('dp', 'fsdp')), may hold values from -0.09375 to 0.09375
- gains_pair: float32 [2, 1536], P(None, ('dp', 'fsdp')), may hold values from 0.5 to 1.5
- in_proj_mom: float32 [1536, 3072], P(None, ('dp', 'fsdp')), may hold values from -96 to 96
- out_proj_mom: float32 [1536, 1536], P(None, ('dp', 'fsdp')), may hold values from -96 to 96
- gate_up_mom: float32 [2, 1536, 4096], P(None, None, ('dp', 'fsdp')), may hold values from -96 to 96
- down_proj_mom: float32 [4096, 1536], P(('dp', 'fsdp')), may hold values from -96 to 96
- gains_mom: float32 [2, 1536], P(None, ('dp', 'fsdp')), may hold values from -96 to 96
- in_proj_avg: float32 [1536, 3072], P(None, ('dp', 'fsdp')), may hold values from -0.15625 to 0.15625
- out_proj_avg: float32 [1536, 1536], P(None, ('dp', 'fsdp')), may hold values from -0.875 to 0.875
- gate_up_avg: float32 [2, 1536, 4096], P(None, None, ('dp', 'fsdp')), may hold values from -0.15625 to 0.15625
- down_proj_avg: float32 [4096, 1536], P(('dp', 'fsdp')), may hold values from -0.09375 to 0.09375
- gains_avg: float32 [2, 1536], P(None, ('dp', 'fsdp')), may hold values from 0.5 to 1.5
Outputs:
- output: bfloat16 [64, 64, 1536], P(('dp', 'fsdp'))
- input_grad: float32 [64, 64, 1536], P(('dp', 'fsdp'))
- in_proj_grad: float32 [1536, 3072], P(None, ('dp', 'fsdp'))
- in_proj_mom_new: float32 [1536, 3072], P(None, ('dp', 'fsdp'))
- in_proj_new: float32 [1536, 3072], P(None, ('dp', 'fsdp'))
- in_proj_avg_new: float32 [1536, 3072], P(None, ('dp', 'fsdp'))
- in_proj_copy: bfloat16 [1536, 3072], P(None, ('dp', 'fsdp'))
- out_proj_grad: float32 [1536, 1536], P(None, ('dp', 'fsdp'))
- out_proj_mom_new: float32 [1536, 1536], P(None, ('dp', 'fsdp'))
- out_proj_new: float32 [1536, 1536], P(None, ('dp', 'fsdp'))
- out_proj_avg_new: float32 [1536, 1536], P(None, ('dp', 'fsdp'))
- out_proj_copy: bfloat16 [1536, 1536], P(None, ('dp', 'fsdp'))
- gate_up_grad: float32 [2, 1536, 4096], P(None, None, ('dp', 'fsdp'))
- gate_up_mom_new: float32 [2, 1536, 4096], P(None, None, ('dp', 'fsdp'))
- gate_up_new: float32 [2, 1536, 4096], P(None, None, ('dp', 'fsdp'))
- gate_up_avg_new: float32 [2, 1536, 4096], P(None, None, ('dp', 'fsdp'))
- gate_up_copy: bfloat16 [2, 1536, 4096], P(None, None, ('dp', 'fsdp'))
- down_proj_grad: float32 [4096, 1536], P(('dp', 'fsdp'))
- down_proj_mom_new: float32 [4096, 1536], P(('dp', 'fsdp'))
- down_proj_new: float32 [4096, 1536], P(('dp', 'fsdp'))
- down_proj_avg_new: float32 [4096, 1536], P(('dp', 'fsdp'))
- down_proj_copy: bfloat16 [4096, 1536], P(('dp', 'fsdp'))
- gains_grad: float32 [2, 1536], P(None, ('dp', 'fsdp'))
- gains_mom_new: float32 [2, 1536], P(None, ('dp', 'fsdp'))
- gains_new: float32 [2, 1536], P(None, ('dp', 'fsdp'))
- gains_avg_new: float32 [2, 1536], P(None, ('dp', 'fsdp'))
- gains_copy: bfloat16 [2, 1536], P(None, ('dp', 'fsdp'))
Inputs may be any that keep to these rules, and one draw needn't show every extreme that they name: `lengths`: valid tokens of each slot, counted from its start; both ends are reached.
All inputs are finite; a program needn't handle non-finite values.
Results may differ from a plain program's by a relative error of at most 0.014.
The roundings to bfloat16 on the way count: a program that leaves them out, or rounds other values in their place, can miss the bound.
Values may be sent and summed in bfloat16 or wider, within the bound.
No kernel may reach another device: no remote copies, remote signals or barrier semaphores. Data moves between devices by JAX's collectives and lax.ppermute only.
A program may use at most 512 MiB of HBM per device.

v0:
```python
import math

import jax
import jax.numpy as jnp
from jax import lax
from jax.sharding import PartitionSpec as P

D = 1536
HEADS = 16
KV_HEADS = 8
HEAD_DIM = 96


EPS = 1e-05
THETA = 10000.0
MASKED = -1e30
MOMENTUM_RATE = 0.9
AVERAGE_RATE = 0.75
RATE_BASE = 0.1
LEFT_ROWS = (((0,), (0,)), ((), ()))
RIGHT_ROWS = (((1,), (1,)), ((), ()))


def rotary_tables(seq_len):
    positions = jnp.arange(seq_len, dtype=jnp.float32)
    halves = jnp.arange(HEAD_DIM // 2, dtype=jnp.float32)
    frequencies = jnp.power(THETA, -2.0 * halves / HEAD_DIM)
    angles = positions[:, None] * frequencies[None, :]
    return (jnp.cos(angles), jnp.sin(angles))


def rotate(values, cos_table, sine_table):
    half_width = values.shape[-1] // 2
    first_half = values[..., :half_width]
    second_half = values[..., half_width:]
    cos_part = cos_table[:, None, :]
    sine_part = sine_table[:, None, :]
    return jnp.concatenate(
        [
            first_half * cos_part - second_half * sine_part,
            second_half * cos_part + first_half * sine_part,
        ],
        axis=-1,
    )


def rotate_back(values, cos_table, sine_table):
    half_width = values.shape[-1] // 2
    first_half = values[..., :half_width]
    second_half = values[..., half_width:]
    cos_part = cos_table[:, None, :]
    sine_part = sine_table[:, None, :]
    return jnp.concatenate(
        [
            first_half * cos_part + second_half * sine_part,
            second_half * cos_part - first_half * sine_part,
        ],
        axis=-1,
    )


def rms_scale(values):
    return lax.rsqrt(jnp.mean(values * values, axis=-1, keepdims=True) + EPS)


def gather_weights(qkv_low, out_low, gate_low, down_low, gain_low):
    return (
        lax.all_gather(qkv_low, ("dp", "fsdp"), axis=1, tiled=True),
        lax.all_gather(out_low, ("dp", "fsdp"), axis=1, tiled=True),
        lax.all_gather(gate_low, ("dp", "fsdp"), axis=2, tiled=True),
        lax.all_gather(down_low, ("dp", "fsdp"), axis=0, tiled=True),
        lax.all_gather(gain_low, ("dp", "fsdp"), axis=1, tiled=True),
    )


def reduce_grads(grad_qkv, grad_out, grad_gate, grad_down, grad_gain):
    return (
        lax.psum_scatter(grad_qkv, ("dp", "fsdp"), scatter_dimension=0, tiled=True),
        lax.psum_scatter(grad_out, ("dp", "fsdp"), scatter_dimension=0, tiled=True),
        lax.psum_scatter(grad_gate, ("dp", "fsdp"), scatter_dimension=0, tiled=True),
        lax.psum_scatter(grad_down, ("dp", "fsdp"), scatter_dimension=0, tiled=True),
        lax.psum_scatter(grad_gain, ("dp", "fsdp"), scatter_dimension=0, tiled=True),
    )


def fetch_weights(qkv_low, out_low, gate_low, down_low, gain_low):
    whole = gather_weights(qkv_low, out_low, gate_low, down_low, gain_low)
    return ((whole[0], whole[1], whole[4]), (whole[2], whole[3]))


def attention_forward(inputs_low, length, attn):
    in_full, out_full, gain_full = attn
    seq_len = inputs_low.shape[0]
    kv_width = KV_HEADS * HEAD_DIM
    groups = HEADS // KV_HEADS
    inv_root = HEAD_DIM ** (-0.5)
    inputs = inputs_low.astype(jnp.float32)
    positions = jnp.arange(seq_len)
    is_valid = positions < length
    gain_pair = gain_full.astype(jnp.float32)
    scale_one = rms_scale(inputs)
    unit_one = inputs * scale_one
    normed_one = (unit_one * gain_pair[0]).astype(jnp.bfloat16)
    projected = jnp.dot(normed_one, in_full, preferred_element_type=jnp.float32)
    cos_table, sine_table = rotary_tables(seq_len)
    queries = rotate(
        projected[:, :D].reshape(seq_len, HEADS, HEAD_DIM), cos_table, sine_table
    ).astype(jnp.bfloat16)
    queries = queries.reshape(seq_len, KV_HEADS, groups, HEAD_DIM)
    key_rows = rotate(
        projected[:, D : D + kv_width].reshape(seq_len, KV_HEADS, HEAD_DIM), cos_table, sine_table
    ).astype(jnp.bfloat16)
    value_rows = (
        projected[:, D + kv_width :].reshape(seq_len, KV_HEADS, HEAD_DIM).astype(jnp.bfloat16)
    )
    scores = (
        jnp.einsum("skgd,tkd->kgst", queries, key_rows, preferred_element_type=jnp.float32)
        * inv_root
    )
    allowed = (positions[None, :] <= positions[:, None]) & is_valid[None, :]
    masked = jnp.where(allowed, scores, MASKED)
    row_max = jnp.max(masked, axis=-1, keepdims=True)
    exps = jnp.exp(masked - row_max)
    probabilities = exps / jnp.sum(exps, axis=-1, keepdims=True)
    prob_low = probabilities.astype(jnp.bfloat16)
    attended = jnp.einsum(
        "kgst,tkd->skgd", prob_low, value_rows, preferred_element_type=jnp.float32
    )
    attended = attended.reshape(seq_len, D).astype(jnp.bfloat16)
    hidden = inputs + jnp.dot(attended, out_full, preferred_element_type=jnp.float32)
    scale_two = rms_scale(hidden)
    unit_two = hidden * scale_two
    normed_two = (unit_two * gain_pair[1]).astype(jnp.bfloat16)
    saved = (
        is_valid,
        gain_pair,
        scale_one,
        unit_one,
        normed_one,
        queries,
        key_rows,
        value_rows,
        probabilities,
        prob_low,
        attended,
        scale_two,
        unit_two,
    )
    return (hidden, normed_two, saved)


def mlp_forward(normed_rows, gate_w, down_w):
    gate_part = jnp.dot(normed_rows, gate_w[0], preferred_element_type=jnp.float32)
    up_part = jnp.dot(normed_rows, gate_w[1], preferred_element_type=jnp.float32)
    sigmoid_gate = jax.nn.sigmoid(gate_part)
    silu_gate = gate_part * sigmoid_gate
    active = (silu_gate * up_part).astype(jnp.bfloat16)
    partial_out = jnp.dot(active, down_w, preferred_element_type=jnp.float32)
    return (partial_out, (gate_part, up_part, sigmoid_gate, silu_gate, active))


def mlp_backward(normed_rows, upstream_rows, kept, gate_w, down_w):
    gate_part, up_part, sigmoid_gate, silu_gate, active = kept
    grad_down = lax.dot_general(
        active, upstream_rows, LEFT_ROWS, preferred_element_type=jnp.float32
    )
    grad_active = lax.dot_general(
        upstream_rows, down_w, RIGHT_ROWS, preferred_element_type=jnp.float32
    )
    grad_gate = (
        grad_active * up_part * sigmoid_gate * (1.0 + gate_part * (1.0 - sigmoid_gate))
    ).astype(jnp.bfloat16)
    grad_up = (grad_active * silu_gate).astype(jnp.bfloat16)
    grad_gate_up = jnp.stack(
        [
            lax.dot_general(grad_gate, normed_rows, LEFT_ROWS, preferred_element_type=jnp.float32),
            lax.dot_general(grad_up, normed_rows, LEFT_ROWS, preferred_element_type=jnp.float32),
        ],
        axis=1,
    )
    grad_normed_two = lax.dot_general(
        grad_gate, gate_w[0], RIGHT_ROWS, preferred_element_type=jnp.float32
    ) + lax.dot_general(grad_up, gate_w[1], RIGHT_ROWS, preferred_element_type=jnp.float32)
    return (grad_normed_two, grad_gate_up, grad_down)


def attention_backward(saved, grad_normed_two, upstream, attn):
    in_full, out_full, gain_full = attn
    (
        is_valid,
        gain_pair,
        scale_one,
        unit_one,
        normed_one,
        queries,
        key_rows,
        value_rows,
        probabilities,
        prob_low,
        attended,
        scale_two,
        unit_two,
    ) = saved
    seq_len = upstream.shape[0]
    kv_width = KV_HEADS * HEAD_DIM
    groups = HEADS // KV_HEADS
    inv_root = HEAD_DIM ** (-0.5)
    gain_two = jnp.sum(grad_normed_two * unit_two, axis=0)
    scaled_two = grad_normed_two * gain_pair[1]
    grad_hidden = upstream.astype(jnp.float32) + scale_two * (
        scaled_two - unit_two * jnp.mean(scaled_two * unit_two, axis=-1, keepdims=True)
    )
    grad_branch = grad_hidden.astype(jnp.bfloat16)
    grad_out = lax.dot_general(grad_branch, attended, LEFT_ROWS, preferred_element_type=jnp.float32)
    grad_attended = lax.dot_general(
        grad_branch, out_full, RIGHT_ROWS, preferred_element_type=jnp.float32
    ).astype(jnp.bfloat16)
    grad_attended = grad_attended.reshape(seq_len, KV_HEADS, groups, HEAD_DIM)
    grad_values = jnp.einsum(
        "kgst,skgd->tkd", prob_low, grad_attended, preferred_element_type=jnp.float32
    )
    grad_probs = jnp.einsum(
        "skgd,tkd->kgst", grad_attended, value_rows, preferred_element_type=jnp.float32
    )
    grad_scores = probabilities * (
        grad_probs - jnp.sum(probabilities * grad_probs, axis=-1, keepdims=True)
    )
    grad_scores = grad_scores.astype(jnp.bfloat16)
    grad_queries = (
        jnp.einsum("kgst,tkd->skgd", grad_scores, key_rows, preferred_element_type=jnp.float32)
        * inv_root
    )
    grad_keys = (
        jnp.einsum("kgst,skgd->tkd", grad_scores, queries, preferred_element_type=jnp.float32)
        * inv_root
    )
    cos_table, sine_table = rotary_tables(seq_len)
    grad_query_pre = rotate_back(
        grad_queries.reshape(seq_len, HEADS, HEAD_DIM), cos_table, sine_table
    ).reshape(seq_len, D)
    grad_key_pre = rotate_back(grad_keys, cos_table, sine_table).reshape(seq_len, kv_width)
    grad_proj = jnp.concatenate(
        [grad_query_pre, grad_key_pre, grad_values.reshape(seq_len, kv_width)], axis=1
    ).astype(jnp.bfloat16)
    grad_in = lax.dot_general(grad_proj, normed_one, LEFT_ROWS, preferred_element_type=jnp.float32)
    grad_normed_one = lax.dot_general(
        grad_proj, in_full, RIGHT_ROWS, preferred_element_type=jnp.float32
    )
    gain_one = jnp.sum(grad_normed_one * unit_one, axis=0)
    scaled_one = grad_normed_one * gain_pair[0]
    grad_inputs = grad_hidden + scale_one * (
        scaled_one - unit_one * jnp.mean(scaled_one * unit_one, axis=-1, keepdims=True)
    )
    grad_gains = jnp.stack([gain_one, gain_two], axis=1)
    return ((grad_in, grad_out, grad_gains), grad_inputs)


def update(weight, gradient, moment, average, step_rate):
    moment_new = MOMENTUM_RATE * moment + gradient
    weight_new = weight - step_rate * (gradient + MOMENTUM_RATE * moment_new)
    average_new = AVERAGE_RATE * average + (1.0 - AVERAGE_RATE) * weight_new
    return (gradient, moment_new, weight_new, average_new, weight_new.astype(jnp.bfloat16))


def on_device(
    tokens,
    cotangent,
    lengths,
    in_proj,
    out_proj,
    gate_up,
    down_proj,
    gains_pair,
    in_proj_mom,
    out_proj_mom,
    gate_up_mom,
    down_proj_mom,
    gains_mom,
    in_proj_avg,
    out_proj_avg,
    gate_up_avg,
    down_proj_avg,
    gains_avg,
):
    qkv_low = in_proj.astype(jnp.bfloat16)
    out_low = out_proj.astype(jnp.bfloat16)
    gate_low = gate_up.astype(jnp.bfloat16)
    down_low = down_proj.astype(jnp.bfloat16)
    gain_low = gains_pair.astype(jnp.bfloat16)
    devices = lax.axis_size("dp") * lax.axis_size("fsdp")
    micro_count = tokens.shape[0]
    step_rate = RATE_BASE / math.sqrt(micro_count * devices * tokens.shape[1])
    attn_totals = None
    mlp_totals = None
    produced_all = []
    grad_inputs_all = []
    for micro_index in range(micro_count):
        attn, mlp = fetch_weights(qkv_low, out_low, gate_low, down_low, gain_low)
        hidden, normed_two, saved = attention_forward(
            tokens[micro_index], lengths[micro_index], attn
        )
        is_valid = saved[0]
        partial_out, kept = mlp_forward(normed_two, mlp[0], mlp[1])
        result = hidden + partial_out
        produced = jnp.where(is_valid[:, None], result, 0.0).astype(jnp.bfloat16)
        attn, mlp = fetch_weights(qkv_low, out_low, gate_low, down_low, gain_low)
        upstream_low = cotangent[micro_index]
        upstream = jnp.where(is_valid[:, None], upstream_low, jnp.zeros_like(upstream_low))
        grad_normed_two, grad_gate_up, grad_down = mlp_backward(
            normed_two, upstream, kept, mlp[0], mlp[1]
        )
        attn_grads, grad_inputs = attention_backward(saved, grad_normed_two, upstream, attn)
        mlp_grads = (grad_gate_up, grad_down)
        attn_totals = (
            attn_grads
            if attn_totals is None
            else tuple((earlier + later for earlier, later in zip(attn_totals, attn_grads)))
        )
        mlp_totals = (
            mlp_grads
            if mlp_totals is None
            else tuple((earlier + later for earlier, later in zip(mlp_totals, mlp_grads)))
        )
        produced_all.append(produced)
        grad_inputs_all.append(grad_inputs)
    reduced = reduce_grads(
        attn_totals[0], attn_totals[1], mlp_totals[0], mlp_totals[1], attn_totals[2]
    )
    grad_qkv = jnp.transpose(reduced[0])
    grad_outw = jnp.transpose(reduced[1])
    grad_gate = jnp.transpose(reduced[2], (1, 2, 0))
    grad_gain = jnp.transpose(reduced[4])
    in_g, in_m, in_w, in_a, in_c = update(in_proj, grad_qkv, in_proj_mom, in_proj_avg, step_rate)
    out_g, out_m, out_w, out_a, out_c = update(
        out_proj, grad_outw, out_proj_mom, out_proj_avg, step_rate
    )
    gu_g, gu_m, gu_w, gu_a, gu_c = update(gate_up, grad_gate, gate_up_mom, gate_up_avg, step_rate)
    dn_g, dn_m, dn_w, dn_a, dn_c = update(
        down_proj, reduced[3], down_proj_mom, down_proj_avg, step_rate
    )
    gn_g, gn_m, gn_w, gn_a, gn_c = update(gains_pair, grad_gain, gains_mom, gains_avg, step_rate)
    return (
        jnp.stack(produced_all),
        jnp.stack(grad_inputs_all),
        in_g,
        in_m,
        in_w,
        in_a,
        in_c,
        out_g,
        out_m,
        out_w,
        out_a,
        out_c,
        gu_g,
        gu_m,
        gu_w,
        gu_a,
        gu_c,
        dn_g,
        dn_m,
        dn_w,
        dn_a,
        dn_c,
        gn_g,
        gn_m,
        gn_w,
        gn_a,
        gn_c,
    )


def solution(mesh):
    in_specs = (
        P(("dp", "fsdp"), None, None),
        P(("dp", "fsdp"), None, None),
        P(("dp", "fsdp")),
        P(None, ("dp", "fsdp")),
        P(None, ("dp", "fsdp")),
        P(None, None, ("dp", "fsdp")),
        P(("dp", "fsdp"), None),
        P(None, ("dp", "fsdp")),
        P(None, ("dp", "fsdp")),
        P(None, ("dp", "fsdp")),
        P(None, None, ("dp", "fsdp")),
        P(("dp", "fsdp"), None),
        P(None, ("dp", "fsdp")),
        P(None, ("dp", "fsdp")),
        P(None, ("dp", "fsdp")),
        P(None, None, ("dp", "fsdp")),
        P(("dp", "fsdp"), None),
        P(None, ("dp", "fsdp")),
    )
    out_specs = (
        P(("dp", "fsdp"), None, None),
        P(("dp", "fsdp"), None, None),
        P(None, ("dp", "fsdp")),
        P(None, ("dp", "fsdp")),
        P(None, ("dp", "fsdp")),
        P(None, ("dp", "fsdp")),
        P(None, ("dp", "fsdp")),
        P(None, ("dp", "fsdp")),
        P(None, ("dp", "fsdp")),
        P(None, ("dp", "fsdp")),
        P(None, ("dp", "fsdp")),
        P(None, ("dp", "fsdp")),
        P(None, None, ("dp", "fsdp")),
        P(None, None, ("dp", "fsdp")),
        P(None, None, ("dp", "fsdp")),
        P(None, None, ("dp", "fsdp")),
        P(None, None, ("dp", "fsdp")),
        P(("dp", "fsdp"), None),
        P(("dp", "fsdp"), None),
        P(("dp", "fsdp"), None),
        P(("dp", "fsdp"), None),
        P(("dp", "fsdp"), None),
        P(None, ("dp", "fsdp")),
        P(None, ("dp", "fsdp")),
        P(None, ("dp", "fsdp")),
        P(None, ("dp", "fsdp")),
        P(None, ("dp", "fsdp")),
    )
    return jax.shard_map(
        on_device, mesh=mesh, in_specs=in_specs, out_specs=out_specs, check_vma=False
    )
```

profile of v0, /device:TPU:0, one launch (start us, length us, event | category | flops | bytes accessed | tf_op | source)
XLA Modules:
  0.0 1700.2 jit_solution(2000524422870482889)
XLA Ops:
  16.0 43.1 %all-gather = bf16[32,48,2]{1,2,0:T(2,128)(2,1)S(1)} all-gather(bf16[1,48,2]{1,2,0:T(2,128)(2,1)S(1)} %convert_bitcast_fusion), channel_id=1, replica_groups=mesh['dp'=4,'fsdp'=8] {'dp','fsdp'}, dimensions={0}, use_global_device_ids=true | all-gather | bytes 6336 | tf_op jit(solution)/shard_map/all_gather | solution.py:72
  63.5 32.7 %all-gather.6.cloned.1.call-done = bf16[1536,3072]{0,1:T(8,128)(2,1)} async-done(((bf16[1536,96]{0,1:T(8,128)(2,1)}), bf16[1536,3072]{0,1:T(8,128)(2,1)}) %all-gather.6.cloned.1.call-update) | async-done | bytes 9437200 | tf_op jit(solution)/shard_map/all_gather | solution.py:68
  96.2 6.9 fusion.84
  103.2 3.0 fusion.88
  113.7 48.4 %all-gather.8.cloned.1.call-done = bf16[1536,1536]{0,1:T(8,128)(2,1)} async-done(((bf16[1536,48]{0,1:T(8,128)(2,1)}), bf16[1536,1536]{0,1:T(8,128)(2,1)}) %all-gather.8.cloned.1.call-update) | async-done | bytes 4718608 | tf_op jit(solution)/shard_map/all_gather | solution.py:69
  162.1 4.0 multiply_reduce_fusion.7
  166.1 4.1 multiply_reduce_fusion.6
  170.4 149.4 %all-gather.10.cloned.1.call-done = bf16[2,1536,4096]{2,1,0:T(8,128)(2,1)} async-done(((bf16[2,1536,128]{2,1,0:T(8,128)(2,1)}), bf16[2,1536,4096]{2,1,0:T(8,128)(2,1)}) %all-gather.10.cloned.1.call-update) | async-done | bytes 25165840 | tf_op jit(solution)/shard_map/all_gather | solution.py:70
  319.8 8.2 fusion.5
  328.0 8.3 fusion.9
  336.3 82.0 %all-gather.12.cloned.1.call-done = bf16[4096,1536]{1,0:T(8,128)(2,1)} async-done(((bf16[128,1536]{1,0:T(8,128)(2,1)}), bf16[4096,1536]{1,0:T(8,128)(2,1)}) %all-gather.12.cloned.1.call-update) | async-done | bytes 12582928 | tf_op jit(solution)/shard_map/all_gather | solution.py:71
  418.3 9.8 multiply_convert_fusion.2
  428.1 7.2 fusion.3
  435.4 9.9 multiply_reduce_fusion.3
  445.8 8.1 fusion.4
  453.9 8.1 fusion.8
  462.0 6.7 multiply_convert_fusion
  468.7 7.1 fusion.2
  475.9 7.4 multiply_reduce_fusion.2
  489.3 3.2 convolution_convert_fusion
  498.2 2.6 fusion.34
  500.8 2.6 fusion.35
  503.4 6.0 fusion.76
  524.9 5.5 fusion.119
  531.0 3.3 fusion.52
  535.6 8.8 convolution_add_fusion.2
  544.5 8.1 fusion.86
  552.7 12.2 convolution_add_fusion.1
  565.9 10.3 fusion.104
  576.2 16.8 convolution_add_fusion
  594.1 10.5 convolution_bitcast_fusion.2
  604.6 10.3 convolution_bitcast_fusion.3
  614.9 10.2 convolution_bitcast_fusion
  625.1 10.2 convolution_bitcast_fusion.1
  635.3 53.0 %maximum_add_fusion = f32[4096,2,1536]{2,0,1:T(8,128)} fusion(f32[4096,1,1536]{2,0,1:T(8,128)} %convolution_bitcast_fusion.2, f32[4096,1,1536]{2,0,1:T(8,128)} %convolution_bitcast_fusion.3, f32[4096,1,1536]{2,0,1:T(8,128)} %convolution_bitcast_fusion, f32[4096,1,1536]{2,0,1:T(8,128)} %convolution_bitcast_fusion.1), kind=kLoop, calls=%fused_computation.2 | loop fusion | flops 37748736 | bytes 150994944 | tf_op jit(solution)/shard_map/add | solution.py:322
  691.3 3.1 copy.184
  694.4 3.1 copy.186
  697.5 6.9 fusion.17
  704.5 7.1 fusion.16
  715.7 54.5 %reduce-scatter.10.cloned.1.call-done = f32[48,1536]{1,0:T(8,128)} async-done(((f32[1536,1536]{1,0:T(8,128)}), f32[48,1536]{1,0:T(8,128)}) %reduce-scatter.10.cloned.1.call-update) | async-done | bytes 294928 | tf_op jit(solution)/shard_map/reduce_scatter | solution.py:79
  774.0 210.3 %reduce-scatter.8.cloned.1.call-done = f32[96,1536]{1,0:T(8,128)} async-done(((f32[3072,1536]{1,0:T(8,128)}), f32[96,1536]{1,0:T(8,128)}) %reduce-scatter.8.cloned.1.call-update) | async-done | bytes 589840 | tf_op jit(solution)/shard_map/reduce_scatter | solution.py:78
  989.3 247.4 %reduce-scatter.14.cloned.1.call-done = f32[128,1536]{1,0:T(8,128)} async-done(((f32[4096,1536]{1,0:T(8,128)}), f32[128,1536]{1,0:T(8,128)}) %reduce-scatter.14.cloned.1.call-update) | async-done | bytes 786448 | tf_op jit(solution)/shard_map/reduce_scatter | solution.py:81
  1236.7 2.6 fusion.108
  1241.7 432.6 %reduce-scatter.12.cloned.1.call-done = f32[128,2,1536]{2,0,1:T(8,128)} async-done(((f32[4096,2,1536]{2,0,1:T(8,128)}), f32[128,2,1536]{2,0,1:T(8,128)}) %reduce-scatter.12.cloned.1.call-update) | async-done | bytes 1572880 | tf_op jit(solution)/shard_map/reduce_scatter | solution.py:80
  1674.3 3.0 copy.187
  1677.4 4.4 fusion.109
  1681.7 3.0 copy.188
  1687.8 3.0 copy.190
  (296 shorter events, 75.6 us)
Async XLA Ops:
  7.2 95.9 %copy-start.1 = (bf16[2,64,1536]{2,1,0:T(8,128)(2,1)S(1)}, bf16[2,64,1536]{2,1,0:T(8,128)(2,1)}, u32[]{:S(2)}) copy-start(bf16[2,64,1536]{2,1,0:T(8,128)(2,1)} %param.18) | copy-start | bytes 1179652
  7.2 89.0 %all-gather.6.cloned.1.call-start = ((), (), s32[]{:S(2)}) async-start(), calls=%async_computation.5 | async-start | bytes 9732096 | tf_op jit(solution)/shard_map/all_gather | solution.py:68
  9.1 153.0 %all-gather.8.cloned.1.call-start = ((), (), s32[]{:S(2)}) async-start(), calls=%async_computation.6 | async-start | bytes 4866048 | tf_op jit(solution)/shard_map/all_gather | solution.py:69
  10.8 309.0 %all-gather.10.cloned.1.call-start = ((), (), s32[]{:S(2)}) async-start(), calls=%async_computation.7 | async-start | bytes 25952256 | tf_op jit(solution)/shard_map/all_gather | solution.py:70
  13.3 405.0 %all-gather.12.cloned.1.call-start = ((), (), s32[]{:S(2)}) async-start(), calls=%async_computation.8 | async-start | bytes 12976128 | tf_op jit(solution)/shard_map/all_gather | solution.py:71
  15.3 698.4 %reduce-scatter.16.cloned.1.call-start = ((), (), s32[]{:S(2)}) async-start(), calls=%async_computation.13 | async-start | bytes 811008
  63.2 481.4 %copy-start.54 = (f32[64]{0:T(128)}, f32[64]{0:T(128)S(1)}, u32[]{:S(2)}) copy-start(f32[64]{0:T(128)S(1)} %get-tuple-element.227) | copy-start | bytes 772
  63.3 46.2 %copy-start.58 = (pred[64,64]{0,1:T(8,128)(4,1)}, pred[64,64]{0,1:T(8,128)(4,1)S(1)}, u32[]{:S(2)}) copy-start(pred[64,64]{0,1:T(8,128)(4,1)S(1)} %fusion.81) | copy-start | bytes 12292
  63.4 49.1 %copy-start.57 = (pred[64,64]{0,1:T(8,128)(4,1)}, pred[64,64]{0,1:T(8,128)(4,1)S(1)}, u32[]{:S(2)}) copy-start(pred[64,64]{0,1:T(8,128)(4,1)S(1)} %fusion.82) | copy-start | bytes 12292
  106.4 59.7 %copy-start.52 = (bf16[64,8,96]{2,1,0:T(8,128)(2,1)}, bf16[64,8,96]{2,1,0:T(8,128)(2,1)S(1)}, u32[]{:S(2)}) copy-start(bf16[64,8,96]{2,1,0:T(8,128)(2,1)S(1)} %convert_element_type.166) | copy-start | bytes 294916
  107.3 62.9 %copy-start.37 = (bf16[64,16,48]{2,0,1:T(8,128)(2,1)}, bf16[64,16,48]{2,0,1:T(8,128)(2,1)S(1)}, u32[]{:S(2)}) copy-start(bf16[64,16,48]{2,0,1:T(8,128)(2,1)S(1)} %copy.164) | copy-start | bytes 294916
  107.4 62.9 %copy-start.38 = (bf16[64,16,48]{2,0,1:T(8,128)(2,1)}, bf16[64,16,48]{2,0,1:T(8,128)(2,1)S(1)}, u32[]{:S(2)}) copy-start(bf16[64,16,48]{2,0,1:T(8,128)(2,1)S(1)} %copy.163) | copy-start | bytes 294916
  108.2 219.8 %copy-start.45 = (bf16[64,8,48]{2,0,1:T(8,128)(2,1)}, bf16[64,8,48]{2,0,1:T(8,128)(2,1)S(1)}, u32[]{:S(2)}) copy-start(bf16[64,8,48]{2,0,1:T(8,128)(2,1)S(1)} %get-tuple-element.174) | copy-start | bytes 147460
  108.2 219.8 %copy-start.46 = (bf16[64,8,48]{2,0,1:T(8,128)(2,1)}, bf16[64,8,48]{2,0,1:T(8,128)(2,1)S(1)}, u32[]{:S(2)}) copy-start(bf16[64,8,48]{2,0,1:T(8,128)(2,1)S(1)} %get-tuple-element.175) | copy-start | bytes 147460
  109.5 218.5 %copy-start.59 = (f32[8,2,64]{2,1,0:T(2,128)}, f32[8,2,64]{2,1,0:T(2,128)S(1)}, u32[]{:S(2)}) copy-start(f32[8,2,64]{2,1,0:T(2,128)S(1)} %get-tuple-element.211) | copy-start | bytes 12292
  110.8 59.5 %copy-start.33 = (bf16[64,1536]{1,0:T(8,128)(2,1)}, bf16[64,1536]{1,0:T(8,128)(2,1)S(1)}, u32[]{:S(2)}) copy-start(bf16[64,1536]{1,0:T(8,128)(2,1)S(1)} %convert_element_type.170) | copy-start | bytes 589828
  110.9 217.1 %copy-start.53 = (bf16[64,8,96]{2,1,0:T(8,128)(2,1)}, bf16[64,8,96]{2,1,0:T(8,128)(2,1)S(1)}, u32[]{:S(2)}) copy-start(bf16[64,8,96]{2,1,0:T(8,128)(2,1)S(1)} %convert_element_type.152) | copy-start | bytes 294916
  111.0 217.0 %copy-start.39 = (bf16[64,16,48]{2,0,1:T(8,128)(2,1)}, bf16[64,16,48]{2,0,1:T(8,128)(2,1)S(1)}, u32[]{:S(2)}) copy-start(bf16[64,16,48]{2,0,1:T(8,128)(2,1)S(1)} %copy.157) | copy-start | bytes 294916
  111.1 59.2 %copy-start.41 = (bf16[64,16,48]{2,0,1:T(8,128)(2,1)}, bf16[64,16,48]{2,0,1:T(8,128)(2,1)S(1)}, u32[]{:S(2)}) copy-start(bf16[64,16,48]{2,0,1:T(8,128)(2,1)S(1)} %copy.156) | copy-start | bytes 294916
  112.4 215.6 %copy-start.61 = (f32[8,2,64]{2,1,0:T(2,128)}, f32[8,2,64]{2,1,0:T(2,128)S(1)}, u32[]{:S(2)}) copy-start(f32[8,2,64]{2,1,0:T(2,128)S(1)} %get-tuple-element.213) | copy-start | bytes 12292
  113.6 52.4 %copy-start.34 = (bf16[64,1536]{1,0:T(8,128)(2,1)}, bf16[64,1536]{1,0:T(8,128)(2,1)S(1)}, u32[]{:S(2)}) copy-start(bf16[64,1536]{1,0:T(8,128)(2,1)S(1)} %convert_element_type.156) | copy-start | bytes 589828
  166.1 269.3 %copy-start.8 = (f32[64,1536]{1,0:T(8,128)}, f32[64,1536]{1,0:T(8,128)S(1)}, u32[]{:S(2)}) copy-start(f32[64,1536]{1,0:T(8,128)S(1)} %get-tuple-element.216) | copy-start | bytes 1179652
  166.1 269.2 %copy-start.65 = (f32[64]{0:T(128)}, f32[64]{0:T(128)S(1)}, u32[]{:S(2)}) copy-start(f32[64]{0:T(128)S(1)} %add_rsqrt_fusion.2) | copy-start | bytes 772
  170.2 265.1 %copy-start.13 = (f32[64,1536]{1,0:T(8,128)}, f32[64,1536]{1,0:T(8,128)S(1)}, u32[]{:S(2)}) copy-start(f32[64,1536]{1,0:T(8,128)S(1)} %get-tuple-element.218) | copy-start | bytes 1179652
  170.3 265.1 %copy-start.72 = (f32[64]{0:T(128)}, f32[64]{0:T(128)S(1)}, u32[]{:S(2)}) copy-start(f32[64]{0:T(128)S(1)} %add_rsqrt_fusion) | copy-start | bytes 772
  170.4 165.9 %copy-start.31 = (bf16[64,1536]{1,0:T(8,128)(2,1)}, bf16[64,1536]{1,0:T(8,128)(2,1)S(1)}, u32[]{:S(2)}) copy-start(bf16[64,1536]{1,0:T(8,128)(2,1)S(1)} %multiply_convert_fusion.9) | copy-start | bytes 589828
  170.4 247.9 %copy-start.18 = (bf16[2,64,1536]{2,1,0:T(8,128)(2,1)S(1)}, bf16[2,64,1536]{2,1,0:T(8,128)(2,1)}, u32[]{:S(2)}) copy-start(bf16[2,64,1536]{2,1,0:T(8,128)(2,1)} %param.19) | copy-start | bytes 1179652
  428.1 17.1 %copy-start.24 = (bf16[64,4096]{1,0:T(8,128)(2,1)}, bf16[64,4096]{1,0:T(8,128)(2,1)S(1)}, u32[]{:S(2)}) copy-start(bf16[64,4096]{1,0:T(8,128)(2,1)S(1)} %get-tuple-element.165) | copy-start | bytes 1572868
  428.1 17.1 %copy-start.26 = (bf16[64,4096]{1,0:T(8,128)(2,1)}, bf16[64,4096]{1,0:T(8,128)(2,1)S(1)}, u32[]{:S(2)}) copy-start(bf16[64,4096]{1,0:T(8,128)(2,1)S(1)} %get-tuple-element.164) | copy-start | bytes 1572868
  445.8 16.2 slice-start
  445.8 16.2 slice-start.1
  468.7 14.6 copy-start.19
  468.7 14.6 copy-start.49
  483.7 19.8 %copy-start.3 = (f32[64,1536]{1,0:T(8,128)}, f32[64,1536]{1,0:T(8,128)S(1)}, u32[]{:S(2)}) copy-start(f32[64,1536]{1,0:T(8,128)S(1)} %get-tuple-element.188) | copy-start | bytes 1179652
  483.7 52.0 %copy-start.11 = (f32[64,1536]{1,0:T(8,128)}, f32[64,1536]{1,0:T(8,128)S(1)}, u32[]{:S(2)}) copy-start(f32[64,1536]{1,0:T(8,128)S(1)} %get-tuple-element.189) | copy-start | bytes 1179652
  503.4 19.6 %copy-start.56 = (f32[1536]{0:T(1024)S(1)}, f32[1536]{0:T(1024)}, u32[]{:S(2)}) copy-start(f32[1536]{0:T(1024)} %get-tuple-element.141) | copy-start | bytes 18436
  511.8 18.6 %slice-start.3 = ((s8[9437184]{0:T(1024)(128)(4,1)}), s8[1048576]{0:T(1024)(128)(4,1)S(1)}, s32[]{:S(2)}) async-start(s8[9437184]{0:T(1024)(128)(4,1)} %bitcast.270), calls=%async_computation.17 | async-start | bytes 2097152
  535.6 234.6 %reduce-scatter.10.cloned.1.call-start = ((), (), s32[]{:S(2)}) async-start(), calls=%async_computation.10 | async-start | bytes 9732096 | tf_op jit(solution)/shard_map/reduce_scatter | solution.py:79
  544.5 439.8 %reduce-scatter.8.cloned.1.call-start = ((), (), s32[]{:S(2)}) async-start(), calls=%async_computation.9 | async-start | bytes 19464192 | tf_op jit(solution)/shard_map/reduce_scatter | solution.py:78
  564.9 671.8 %reduce-scatter.14.cloned.1.call-start = ((), (), s32[]{:S(2)}) async-start(), calls=%async_computation.12 | async-start | bytes 25952256 | tf_op jit(solution)/shard_map/reduce_scatter | solution.py:81
  593.1 1081.2 %reduce-scatter.12.cloned.1.call-start = ((), (), s32[]{:S(2)}) async-start(), calls=%async_computation.11 | async-start | bytes 51904512 | tf_op jit(solution)/shard_map/reduce_scatter | solution.py:80
  704.5 279.8 %copy-start.23 = (f32[1536,96]{0,1:T(8,128)S(1)}, f32[1536,96]{0,1:T(8,128)}, u32[]{:S(2)}) copy-start(f32[1536,96]{0,1:T(8,128)} %param.21) | copy-start | bytes 1769476
  711.6 525.1 %copy-start.20 = (f32[128,1536]{1,0:T(8,128)S(1)}, f32[128,1536]{1,0:T(8,128)}, u32[]{:S(2)}) copy-start(f32[128,1536]{1,0:T(8,128)} %param.24) | copy-start | bytes 2359300
  714.5 967.2 %copy-start.63 = (f32[48,2]{0,1:T(2,128)}, f32[48,2]{0,1:T(2,128)S(1)}, u32[]{:S(2)}) copy-start(f32[48,2]{0,1:T(2,128)S(1)} %copy.215) | copy-start | bytes 1156
  715.1 966.6 %copy-start.64 = (f32[2,48]{1,0:T(2,128)}, f32[2,48]{1,0:T(2,128)S(1)}, u32[]{:S(2)}) copy-start(f32[2,48]{1,0:T(2,128)S(1)} %get-tuple-element.150) | copy-start | bytes 1156
  772.2 912.6 %copy-start.36 = (f32[1536,48]{0,1:T(8,128)}, f32[1536,48]{0,1:T(8,128)S(1)}, u32[]{:S(2)}) copy-start(f32[1536,48]{0,1:T(8,128)S(1)} %get-tuple-element.158) | copy-start | bytes 884740
  989.3 697.0 %copy-start.7 = (f32[2,1536,128]{1,2,0:T(8,128)S(1)}, f32[2,1536,128]{1,2,0:T(8,128)}, u32[]{:S(2)}) copy-start(f32[2,1536,128]{1,2,0:T(8,128)} %copy.186) | copy-start | bytes 4718596
  1239.3 435.0 %copy-start.21 = (f32[128,1536]{1,0:T(8,128)}, f32[128,1536]{1,0:T(8,128)S(1)}, u32[]{:S(2)}) copy-start(f32[128,1536]{1,0:T(8,128)S(1)} %get-tuple-element.153) | copy-start | bytes 2359300
  (44 other events, 351.1 us)
Sparse Core Ops, SparseCore 0:
  11.6 84.5 all-gather.5
  99.8 62.2 all-gather.7
  164.2 155.5 all-gather.9
  323.2 95.0 all-gather.11
  535.7 93.7 reduce-scatter.15
  635.8 134.3 reduce-scatter.9
  778.3 205.9 reduce-scatter.7
  992.4 244.2 reduce-scatter.13
  1243.2 431.1 reduce-scatter.11
where the time goes:
time: 1710 us; the launch traced here: 1700 us
  waiting for transfers between devices  1260 us (74%)
  matrix products  246 us (14%)
  other arithmetic  96.3 us (6%)
  blocking collectives  43.1 us (3%)
  local copies, waits for them, and re-layouts  41.7 us (2%)
    reduce_scatter x1, waiting for transfers between devices, reduce_grads(): lax.psum_scatter(grad_gate, ('dp', 'fsdp'), scatter_dimension=0, tiled=True)  433 us
    reduce_scatter x1, waiting for transfers between devices, reduce_grads(): lax.psum_scatter(grad_down, ('dp', 'fsdp'), scatter_dimension=0, tiled=True)  247 us
    reduce_scatter x1, waiting for transfers between devices, reduce_grads(): lax.psum_scatter(grad_qkv, ('dp', 'fsdp'), scatter_dimension=0, tiled=True)  210 us
    all_gather x1, waiting for transfers between devices, gather_weights(): lax.all_gather(gate_low, ('dp', 'fsdp'), axis=2, tiled=True)  149 us
    all_gather x1, waiting for transfers between devices, gather_weights(): lax.all_gather(down_low, ('dp', 'fsdp'), axis=0, tiled=True)  82 us
    reduce_scatter x1, waiting for transfers between devices, reduce_grads(): lax.psum_scatter(grad_out, ('dp', 'fsdp'), scatter_dimension=0, tiled=True)  54.5 us
    add x2, other arithmetic, on_device(): earlier + later  53 us
    all_gather x1, waiting for transfers between devices, gather_weights(): lax.all_gather(out_low, ('dp', 'fsdp'), axis=1, tiled=True)  48.4 us
  transfers between devices with their start and end apart: 9, of which 8 were waited for; matrix products, arithmetic and copies ran while one was open for 14% of the time, Pallas kernels for 0%

commit v1 on v0

v1 whole, which is shorter than its diff:
```python
import math

import jax
import jax.numpy as jnp
from jax import lax
from jax.sharding import PartitionSpec as P

D = 1536
HEADS = 16
KV_HEADS = 8
HEAD_DIM = 96
ALL_HEADS = HEADS + 2 * KV_HEADS
GROUPS = HEADS // KV_HEADS

EPS = 1e-05
THETA = 10000.0
MASKED = -1e30
MOMENTUM_RATE = 0.9
AVERAGE_RATE = 0.75
RATE_BASE = 0.1
AXES = ("dp", "fsdp")
LEFT_ROWS = (((0,), (0,)), ((), ()))
RIGHT_ROWS = (((1,), (1,)), ((), ()))


def rotary_tables(seq_len):
    positions = jnp.arange(seq_len, dtype=jnp.float32)
    halves = jnp.arange(HEAD_DIM // 2, dtype=jnp.float32)
    frequencies = jnp.power(THETA, -2.0 * halves / HEAD_DIM)
    angles = positions[:, None] * frequencies[None, :]
    return (jnp.cos(angles), jnp.sin(angles))


def turn(values, cos_part, sine_part):
    half_width = values.shape[-1] // 2
    first_half = values[..., :half_width]
    second_half = values[..., half_width:]
    return jnp.concatenate(
        [
            first_half * cos_part - second_half * sine_part,
            second_half * cos_part + first_half * sine_part,
        ],
        axis=-1,
    )


def rms_scale(values):
    return lax.rsqrt(jnp.mean(values * values, axis=-1, keepdims=True) + EPS)


def low(values):
    return values.astype(jnp.bfloat16)


def wide(values):
    return values.astype(jnp.float32)


def mm(a, b):
    return jnp.dot(a, b, preferred_element_type=jnp.float32)


def mm_left(a, b):
    return lax.dot_general(a, b, LEFT_ROWS, preferred_element_type=jnp.float32)


def mm_right(a, b):
    return lax.dot_general(a, b, RIGHT_ROWS, preferred_element_type=jnp.float32)


def update(weight, gradient, moment, average, step_rate):
    moment_new = MOMENTUM_RATE * moment + gradient
    weight_new = weight - step_rate * (gradient + MOMENTUM_RATE * moment_new)
    average_new = AVERAGE_RATE * average + (1.0 - AVERAGE_RATE) * weight_new
    return (gradient, moment_new, weight_new, average_new, weight_new.astype(jnp.bfloat16))


def flip_bits(values, axis, index):
    count = values.shape[axis]
    bit = 1
    while bit < count:
        shape = values.shape
        split = shape[:axis] + (count // (2 * bit), 2, bit) + shape[axis + 1 :]
        parts = values.reshape(split)
        flipped = jnp.flip(parts, axis + 1)
        values = jnp.where((index & bit) != 0, flipped, parts).reshape(shape)
        bit *= 2
    return values


class Links:
    def __init__(self, n_dp, n_fsdp):
        self.n_dp, self.n_z, self.count = n_dp, n_fsdp // 2, n_dp * n_fsdp
        self.dp = [n_fsdp * k for k in range(n_dp)]
        self.z = [2 * k for k in range(self.n_z)]
        assert n_dp & (n_dp - 1) == 0 and n_fsdp & (n_fsdp - 1) == 0

    def send(self, values, mask):
        return lax.ppermute(values, AXES, [(i, i ^ mask) for i in range(self.count)])

    def gather(self, values, masks):
        return jnp.stack([values] + [self.send(values, m) for m in masks[1:]])

    def gather_pair(self, values, masks):
        own = self.gather(values, masks)
        return jnp.stack([own, self.send(own, 1)])

    def spread(self, blocks, masks):
        return jnp.stack([blocks[0]] + [self.send(blocks[k], m) for k, m in enumerate(masks) if k])

    def spread_pair(self, blocks, masks):
        moved = jnp.stack([blocks[0], self.send(blocks[1], 1)])
        moved = jnp.swapaxes(moved, 0, 1)
        return jnp.swapaxes(self.spread(moved, masks), 0, 1)

    def add_up(self, blocks, masks):
        total = blocks[0]
        for k, m in enumerate(masks):
            if k:
                total = total + wide(self.send(low(blocks[k]), m))
        return total

    def add_up_pair(self, blocks, masks):
        mine = blocks[0] + wide(self.send(low(blocks[1]), 1))
        return self.add_up(mine, masks)


def on_device(
    tokens,
    cotangent,
    lengths,
    in_proj,
    out_proj,
    gate_up,
    down_proj,
    gains_pair,
    in_proj_mom,
    out_proj_mom,
    gate_up_mom,
    down_proj_mom,
    gains_mom,
    in_proj_avg,
    out_proj_avg,
    gate_up_avg,
    down_proj_avg,
    gains_avg,
):
    n_dp, n_fsdp = lax.axis_size("dp"), lax.axis_size("fsdp")
    links = Links(n_dp, n_fsdp)
    n_z, devices = links.n_z, links.count
    at_dp, at_fsdp = lax.axis_index("dp"), lax.axis_index("fsdp")
    at_z, at_core = at_fsdp // 2, at_fsdp % 2
    slots, seq_len = tokens.shape[:2]
    rows = slots * seq_len
    members = 2 * n_dp
    group_rows = 2 * n_z
    step_rate = RATE_BASE / math.sqrt(slots * devices * seq_len)
    inv_root = HEAD_DIM ** (-0.5)
    in_width = in_proj.shape[1]
    out_width = out_proj.shape[1]
    ff_width = down_proj.shape[0]

    in_low = low(jnp.transpose(in_proj))
    out_low = low(jnp.transpose(out_proj))
    gate_low = low(gate_up)
    down_low = low(down_proj)
    gain_low = low(gains_pair)

    gain_parts = links.gather_pair(links.gather(gain_low, links.z), links.dp)
    gain_parts = jnp.transpose(gain_parts, (1, 2, 0, 3, 4))
    gain_parts = gain_parts.reshape(devices, -1)
    at = at_dp * n_fsdp + at_fsdp
    one_hot = (jnp.arange(devices)[:, None] ^ at) == jnp.arange(devices)[None, :]
    gain_all = mm(low(one_hot), gain_parts).reshape(devices, 2, -1)
    gain_one = gain_all[:, 0].reshape(-1)
    gain_two = gain_all[:, 1].reshape(-1)

    token_rows = tokens.reshape(rows, D)
    token_group = links.gather_pair(token_rows, links.dp).reshape(members * rows, D)
    in_group = links.gather(in_low, links.z).reshape(n_z * in_width, D)
    out_full_t = lax.all_gather(out_low, AXES, axis=0, tiled=True)

    inputs_group = wide(token_group)
    unit_group = inputs_group * rms_scale(inputs_group)
    normed_group = low(unit_group * gain_one)
    projected = mm_right(normed_group, in_group)
    cos_table, sine_table = rotary_tables(seq_len)
    whole_heads = in_width == HEAD_DIM
    if whole_heads:
        heads = projected.reshape(members * slots, seq_len, n_z, HEAD_DIM)
        head_base = at_dp * n_fsdp
        turned = head_base < HEADS + KV_HEADS
        cos_here = jnp.where(turned, cos_table, 1.0)[:, None, :]
        sine_here = jnp.where(turned, sine_table, 0.0)[:, None, :]
        projected = low(turn(heads, cos_here, sine_here))
    blocks = projected.reshape(2, n_dp, rows, n_z * in_width)
    blocks = links.spread_pair(blocks, links.dp)
    blocks = blocks.reshape(2, n_dp, rows, n_z, in_width)
    blocks = jnp.transpose(blocks, (1, 3, 0, 2, 4))
    for axis, index in ((0, at_dp), (1, at_z), (2, at_core)):
        blocks = flip_bits(blocks, axis, index)
    blocks = blocks.reshape(devices, rows, in_width)
    if not whole_heads:
        blocks = jnp.transpose(blocks, (1, 0, 2)).reshape(rows, ALL_HEADS, HEAD_DIM)
        blocks = jnp.transpose(blocks, (1, 0, 2)).reshape(ALL_HEADS, slots, seq_len, HEAD_DIM)
        rotated = turn(blocks[: HEADS + KV_HEADS], cos_table, sine_table)
        blocks = low(jnp.concatenate([rotated, blocks[HEADS + KV_HEADS :]]))
    blocks = blocks.reshape(ALL_HEADS, slots, seq_len, HEAD_DIM)
    queries = blocks[:HEADS].reshape(KV_HEADS, GROUPS, slots, seq_len, HEAD_DIM)
    key_rows = blocks[HEADS : HEADS + KV_HEADS]
    value_rows = blocks[HEADS + KV_HEADS :]

    positions = jnp.arange(seq_len)
    is_valid = positions[None, :] < lengths[:, None]
    row_valid = is_valid.reshape(rows, 1)
    scores = (
        jnp.einsum("kgbsd,kbtd->kgbst", queries, key_rows, preferred_element_type=jnp.float32)
        * inv_root
    )
    allowed = (positions[None, :] <= positions[:, None])[None] & is_valid[:, None, :]
    masked = jnp.where(allowed, scores, MASKED)
    row_max = jnp.max(masked, axis=-1, keepdims=True)
    exps = jnp.exp(masked - row_max)
    probabilities = exps / jnp.sum(exps, axis=-1, keepdims=True)
    prob_low = low(probabilities)
    attended = jnp.einsum(
        "kgbst,kbtd->bskgd", prob_low, value_rows, preferred_element_type=jnp.float32
    )
    attended = low(attended).reshape(rows, D)
    inputs = wide(token_rows)
    hidden = inputs + mm_right(attended, out_full_t)
    scale_two = rms_scale(hidden)
    unit_two = hidden * scale_two
    normed_two = low(unit_two * gain_two)

    upstream = jnp.where(row_valid, cotangent.reshape(rows, D), jnp.zeros((), jnp.bfloat16))
    upstream_group = links.gather_pair(upstream, links.z).reshape(group_rows * rows, D)
    gate_group = links.gather(gate_low, links.dp)
    gate_w = jnp.transpose(gate_group, (1, 2, 0, 3)).reshape(2, D, n_dp * ff_width)
    down_w = links.gather(down_low, links.dp).reshape(n_dp * ff_width, D)
    normed_rows = links.gather_pair(normed_two, links.z).reshape(group_rows * rows, D)
    gate_part = mm(normed_rows, gate_w[0])
    up_part = mm(normed_rows, gate_w[1])
    sigmoid_gate = jax.nn.sigmoid(gate_part)
    silu_gate = gate_part * sigmoid_gate
    active = low(silu_gate * up_part)
    grad_active = mm_right(upstream_group, down_w)
    grad_gate = low(
        grad_active * up_part * sigmoid_gate * (1.0 + gate_part * (1.0 - sigmoid_gate))
    )
    grad_up = low(grad_active * silu_gate)
    grad_normed_two = mm_right(grad_gate, gate_w[0]) + mm_right(grad_up, gate_w[1])
    grad_normed_two = links.add_up_pair(
        grad_normed_two.reshape(2, n_z, rows, D), links.z
    )
    partial_out = mm(active, down_w)
    partial_out = links.add_up_pair(partial_out.reshape(2, n_z, rows, D), links.z)
    produced = low(jnp.where(row_valid, hidden + partial_out, 0.0))

    grad_gate_up = jnp.stack([mm_left(normed_rows, grad_gate), mm_left(normed_rows, grad_up)])
    grad_gate_up = jnp.moveaxis(grad_gate_up.reshape(2, D, n_dp, ff_width), 2, 0)
    grad_gate_up = links.add_up(grad_gate_up, links.dp)
    grad_down = mm_left(active, upstream_group).reshape(n_dp, ff_width, D)
    grad_down = links.add_up(grad_down, links.dp)

    gain_two_grad = jnp.sum(grad_normed_two * unit_two, axis=0)
    scaled_two = grad_normed_two * gain_two
    grad_hidden = wide(upstream) + scale_two * (
        scaled_two - unit_two * jnp.mean(scaled_two * unit_two, axis=-1, keepdims=True)
    )
    grad_branch = low(grad_hidden)
    grad_attended = low(mm(grad_branch, out_full_t))
    grad_attended = grad_attended.reshape(slots, seq_len, KV_HEADS, GROUPS, HEAD_DIM)
    grad_values = jnp.einsum(
        "kgbst,bskgd->kbtd", prob_low, grad_attended, preferred_element_type=jnp.float32
    )
    grad_probs = jnp.einsum(
        "bskgd,kbtd->kgbst", grad_attended, value_rows, preferred_element_type=jnp.float32
    )
    grad_scores = low(
        probabilities
        * (grad_probs - jnp.sum(probabilities * grad_probs, axis=-1, keepdims=True))
    )
    grad_queries = (
        jnp.einsum("kgbst,kbtd->kgbsd", grad_scores, key_rows, preferred_element_type=jnp.float32)
        * inv_root
    )
    grad_keys = (
        jnp.einsum("kgbst,kgbsd->kbtd", grad_scores, queries, preferred_element_type=jnp.float32)
        * inv_root
    )
    grad_heads = jnp.concatenate(
        [
            turn(grad_queries.reshape(HEADS, slots, seq_len, HEAD_DIM), cos_table, -sine_table),
            turn(grad_keys, cos_table, -sine_table),
            grad_values,
        ]
    )
    grad_heads = low(grad_heads).reshape(ALL_HEADS, rows, HEAD_DIM)
    if not whole_heads:
        grad_heads = jnp.transpose(grad_heads, (1, 0, 2)).reshape(rows, devices, in_width)
        grad_heads = jnp.transpose(grad_heads, (1, 0, 2))
    blocks = grad_heads.reshape(n_dp, n_z, 2, rows, in_width)
    for axis, index in ((0, at_dp), (1, at_z), (2, at_core)):
        blocks = flip_bits(blocks, axis, index)
    blocks = jnp.transpose(blocks, (2, 0, 3, 1, 4)).reshape(2, n_dp, rows, n_z * in_width)
    grad_proj = links.spread_pair(blocks, links.dp).reshape(members * rows, n_z * in_width)

    grad_in = mm_left(grad_proj, normed_group).reshape(n_z, in_width, D)
    grad_in = jnp.transpose(links.add_up(grad_in, links.z))
    grad_normed_one = mm(grad_proj, in_group).reshape(2, n_dp, rows, D)
    grad_normed_one = links.add_up_pair(grad_normed_one, links.dp)

    attended_group = links.gather_pair(attended, links.dp).reshape(members * rows, D)
    columns = jnp.transpose(grad_branch).reshape(n_dp, n_z, 2, out_width, rows)
    for axis, index in ((0, at_dp), (1, at_z), (2, at_core)):
        columns = flip_bits(columns, axis, index)
    columns = jnp.transpose(columns, (2, 0, 1, 3, 4)).reshape(2, n_dp, n_z * out_width, rows)
    columns = links.spread_pair(columns, links.dp).reshape(members, n_z * out_width, rows)
    columns = jnp.transpose(columns, (1, 0, 2)).reshape(n_z * out_width, members * rows)
    grad_out = mm(columns, attended_group).reshape(n_z, out_width, D)
    grad_out = jnp.transpose(links.add_up(grad_out, links.z))

    scale_one = rms_scale(inputs)
    unit_one = inputs * scale_one
    gain_one_grad = jnp.sum(grad_normed_one * unit_one, axis=0)
    scaled_one = grad_normed_one * gain_one
    grad_inputs = grad_hidden + scale_one * (
        scaled_one - unit_one * jnp.mean(scaled_one * unit_one, axis=-1, keepdims=True)
    )
    grad_gains = jnp.stack([gain_one_grad, gain_two_grad]).reshape(2, n_dp, n_z, 2, -1)
    grad_gains = jnp.transpose(grad_gains, (1, 2, 3, 0, 4)).reshape(devices, -1)
    grad_gains = jnp.dot(wide(one_hot), grad_gains, precision=lax.Precision.HIGHEST)
    grad_gains = grad_gains.reshape(n_dp, n_z, 2, 2, -1)
    total = grad_gains[:, :, 0] + links.send(grad_gains[:, :, 1], 1)
    total = total[0] + sum(links.send(total[k], m) for k, m in enumerate(links.dp) if k)
    grad_gain = total[0] + sum(links.send(total[k], m) for k, m in enumerate(links.z) if k)

    return (
        produced.reshape(tokens.shape),
        grad_inputs.reshape(tokens.shape),
        *update(in_proj, grad_in, in_proj_mom, in_proj_avg, step_rate),
        *update(out_proj, grad_out, out_proj_mom, out_proj_avg, step_rate),
        *update(gate_up, grad_gate_up, gate_up_mom, gate_up_avg, step_rate),
        *update(down_proj, grad_down, down_proj_mom, down_proj_avg, step_rate),
        *update(gains_pair, grad_gain, gains_mom, gains_avg, step_rate),
    )


def solution(mesh):
    rows = P(AXES, None, None)
    last_of_two = P(None, AXES)
    first_of_two = P(AXES, None)
    last_of_three = P(None, None, AXES)
    weights = (last_of_two, last_of_two, last_of_three, first_of_two, last_of_two)
    in_specs = (rows, rows, P(AXES)) + weights * 3
    out_specs = (rows, rows) + tuple(spec for spec in weights for _ in range(5))
    return jax.shard_map(
        on_device, mesh=mesh, in_specs=in_specs, out_specs=out_specs, check_vma=False
    )
```

time: 1710 us -> 522 us (0.31)
  waiting for transfers between devices: 1260 us -> 244 us
  matrix products: 246 us -> 44.4 us
  starting transfers between devices: 0.37 us -> 89.6 us
  blocking collectives: 43.1 us -> 0 us
  other arithmetic: 96.3 us -> 75.5 us
    reduce_scatter x4 -> x0, waiting for transfers between devices: 945 us -> none  [the longest x1 433 us: reduce_grads(): lax.psum_scatter(grad_gate, ('dp', 'fsdp'), scatter_dimension=0, tiled=True)]
    all_gather x4 -> x1, waiting for transfers between devices: 313 us -> 0.01 us  [on_device(): out_full_t = lax.all_gather(out_low, AXES, axis=0, tiled=True)]
    ppermute x0 -> x75, waiting for transfers between devices: none -> 244 us  [send(): lax.ppermute(values, AXES, [(i, i ^ mask) for i in range(self.count)])]
    dot_general x40 -> x22, matrix products: 243 us -> 42.7 us  [the longest x7 14.5 us: mm(): return jnp.dot(a, b, preferred_element_type=jnp.float32)]
    ppermute x0 -> x75, starting transfers between devices: none -> 89.5 us  [send(): lax.ppermute(values, AXES, [(i, i ^ mask) for i in range(self.count)])]
    add x3, other arithmetic: 53.3 us -> 1.18 us  [the longest x1 1.17 us: on_device(): grad_hidden + scale_one * (scaled_one - unit_one * jnp.mean(scaled_one *...]
    all_gather x1 -> x0, blocking collectives: 43.1 us -> none  [gather_weights(): lax.all_gather(gain_low, ('dp', 'fsdp'), axis=1, tiled=True)]
    another operation x7 -> x29, other arithmetic: 5.56 us -> 29.8 us  [the longest x8 14.6 us: gather_pair(): return jnp.stack([own, self.send(own, 1)])]
  transfers between devices with their start and end apart: 9 -> 76, of which waited for: 8 -> 34; matrix products, arithmetic and copies ran while one was open for 14% -> 22% of each run, Pallas kernels for 0% -> 0%
where the time goes in v1:
time: 522 us; the launch traced here: 514 us
  waiting for transfers between devices  244 us (47%)
  starting transfers between devices  89.6 us (17%)
  other arithmetic  75.5 us (14%)
  local copies, waits for them, and re-layouts  44.8 us (9%)
  matrix products  44.4 us (9%)
  between operations  15.8 us (3%)
    ppermute x75, waiting for transfers between devices, send(): lax.ppermute(values, AXES, [(i, i ^ mask) for i in range(self.count)])  244 us
    ppermute x75, starting transfers between devices, send(): lax.ppermute(values, AXES, [(i, i ^ mask) for i in range(self.count)])  89.5 us
    unnamed x165, local copies, waits for them, and re-layouts  15.7 us
    another operation x8, other arithmetic, gather_pair(): return jnp.stack([own, self.send(own, 1)])  14.6 us
    dot_general x7, matrix products, mm(): return jnp.dot(a, b, preferred_element_type=jnp.float32)  14.5 us
    dot_general x5, matrix products, mm_right(): return lax.dot_general(a, b, RIGHT_ROWS, preferred_element_type=jnp.float32)  14.2 us
  transfers between devices with their start and end apart: 76, of which 34 were waited for; matrix products, arithmetic and copies ran while one was open for 22% of the time, Pallas kernels for 0%

profile of v1, /device:TPU:0, one launch (start us, length us, event | category | flops | bytes accessed | tf_op | source)
XLA Modules:
  0.0 514.2 jit_solution(17341662756970374847)
XLA Ops:
  9.0 4.0 collective-permute-start.2
  14.3 4.0 collective-permute-start.6
  25.2 6.5 %collective-permute-done.1 = bf16[128,1536]{1,0:T(8,128)(2,1)S(1)} collective-permute-done((bf16[128,1536]{1,0:T(8,128)(2,1)}, bf16[128,1536]{1,0:T(8,128)(2,1)S(1)}, u32[]{:S(2)}, u32[]{:S(2)}) %collective-permute-start.1) | collective-permute-done | bytes 393248 | tf_op jit(solution)/shard_map/ppermute | solution.py:99
  31.7 3.8 collective-permute-start.13
  36.3 2.4 fusion.113
  47.5 2.3 collective-permute-start.34
  54.5 41.6 %collective-permute-done.12 = bf16[96,1536]{1,0:T(8,128)(2,1)S(1)} collective-permute-done((bf16[96,1536]{1,0:T(8,128)(2,1)}, bf16[96,1536]{1,0:T(8,128)(2,1)S(1)}, u32[]{:S(2)}, u32[]{:S(2)}) %collective-permute-start.12) | collective-permute-done | bytes 294944 | tf_op jit(solution)/shard_map/ppermute | solution.py:99
  96.1 3.0 fusion.2
  105.9 2.9 collective-permute-start.16
  110.0 4.4 collective-permute-done.17
  114.6 3.6 collective-permute-done.16
  131.4 4.2 multiply_reduce_fusion.5
  136.5 2.9 collective-permute-start.20
  139.5 2.6 copy.81
  148.4 2.4 collective-permute-done.20
  150.7 22.1 %collective-permute-done.19 = bf16[128,1536]{1,0:T(8,128)(2,1)} collective-permute-done((bf16[128,1536]{1,0:T(8,128)(2,1)}, bf16[128,1536]{1,0:T(8,128)(2,1)}, u32[]{:S(2)}, u32[]{:S(2)}) %collective-permute-start.19) | collective-permute-done | bytes 393248 | tf_op jit(solution)/shard_map/ppermute | solution.py:99
  173.0 10.3 %collective-permute-done.18 = bf16[128,1536]{1,0:T(8,128)(2,1)S(1)} collective-permute-done((bf16[128,1536]{1,0:T(8,128)(2,1)}, bf16[128,1536]{1,0:T(8,128)(2,1)S(1)}, u32[]{:S(2)}, u32[]{:S(2)}) %collective-permute-start.18) | collective-permute-done | bytes 393248 | tf_op jit(solution)/shard_map/ppermute | solution.py:99
  183.3 3.1 fusion.112
  196.0 4.5 collective-permute-done.57
  200.5 8.0 %collective-permute-done.56 = bf16[128,1536]{1,0:T(8,128)(2,1)} collective-permute-done((bf16[128,1536]{1,0:T(8,128)(2,1)}, bf16[128,1536]{1,0:T(8,128)(2,1)}, u32[]{:S(2)}, u32[]{:S(2)}) %collective-permute-start.56) | collective-permute-done | bytes 393248 | tf_op jit(solution)/shard_map/ppermute | solution.py:99
  225.7 5.3 %collective-permute-done.67 = bf16[128,1536]{1,0:T(8,128)(2,1)S(1)} collective-permute-done((bf16[128,1536]{1,0:T(8,128)(2,1)S(1)}, bf16[128,1536]{1,0:T(8,128)(2,1)S(1)}, u32[]{:S(2)}, u32[]{:S(2)}) %collective-permute-start.67) | collective-permute-done | bytes 393248 | tf_op jit(solution)/shard_map/ppermute | solution.py:99
  231.0 7.9 %collective-permute-done.66 = bf16[128,1536]{1,0:T(8,128)(2,1)S(1)} collective-permute-done((bf16[128,1536]{1,0:T(8,128)(2,1)S(1)}, bf16[128,1536]{1,0:T(8,128)(2,1)S(1)}, u32[]{:S(2)}, u32[]{:S(2)}) %collective-permute-start.66) | collective-permute-done | bytes 393248 | tf_op jit(solution)/shard_map/ppermute | solution.py:99
  244.9 8.4 %collective-permute-done.27 = bf16[128,1536]{1,0:T(8,128)(2,1)S(1)} collective-permute-done((bf16[128,1536]{1,0:T(8,128)(2,1)S(1)}, bf16[128,1536]{1,0:T(8,128)(2,1)S(1)}, u32[]{:S(2)}, u32[]{:S(2)}) %collective-permute-start.27) | collective-permute-done | bytes 393248 | tf_op jit(solution)/shard_map/ppermute | solution.py:99
  253.4 7.5 %collective-permute-done.26 = bf16[128,1536]{1,0:T(8,128)(2,1)S(1)} collective-permute-done((bf16[128,1536]{1,0:T(8,128)(2,1)S(1)}, bf16[128,1536]{1,0:T(8,128)(2,1)S(1)}, u32[]{:S(2)}, u32[]{:S(2)}) %collective-permute-start.26) | collective-permute-done | bytes 393248 | tf_op jit(solution)/shard_map/ppermute | solution.py:99
  261.1 2.4 fusion.15
  263.5 2.4 fusion.35
  281.0 2.3 copy-done.2
  283.5 13.2 %collective-permute-done.64 = bf16[2,1536,128]{2,1,0:T(8,128)(2,1)S(1)} collective-permute-done((bf16[2,1536,128]{2,1,0:T(8,128)(2,1)}, bf16[2,1536,128]{2,1,0:T(8,128)(2,1)S(1)}, u32[]{:S(2)}, u32[]{:S(2)}) %collective-permute-start.64) | collective-permute-done | bytes 786464 | tf_op jit(solution)/shard_map/ppermute | solution.py:99
  296.7 16.4 %collective-permute-done.63 = bf16[2,1536,128]{2,1,0:T(8,128)(2,1)S(1)} collective-permute-done((bf16[2,1536,128]{2,1,0:T(8,128)(2,1)}, bf16[2,1536,128]{2,1,0:T(8,128)(2,1)S(1)}, u32[]{:S(2)}, u32[]{:S(2)}) %collective-permute-start.63) | collective-permute-done | bytes 786464 | tf_op jit(solution)/shard_map/ppermute | solution.py:99
  314.0 3.8 fusion.117
  325.0 2.6 collective-permute-start.37
  330.0 7.2 %collective-permute-done.39 = bf16[128,1536]{1,0:T(8,128)(2,1)S(1)} collective-permute-done((bf16[128,1536]{1,0:T(8,128)(2,1)S(1)}, bf16[128,1536]{1,0:T(8,128)(2,1)S(1)}, u32[]{:S(2)}, u32[]{:S(2)}) %collective-permute-start.39) | collective-permute-done | bytes 393248 | tf_op jit(solution)/shard_map/ppermute | solution.py:99
  337.2 15.2 %collective-permute-start.29 = (bf16[128,1536]{1,0:T(8,128)(2,1)S(1)}, bf16[128,1536]{1,0:T(8,128)(2,1)S(1)}, u32[]{:S(2)}, u32[]{:S(2)}) collective-permute-start(bf16[128,1536]{1,0:T(8,128)(2,1)S(1)} %get-tuple-element.85), channel_id=1, source_target_pairs={{0,2},{1,3},{2,0},{3,1},{4,6},{5,7},{6,4},{7,5},{8,10},{9,11},{10,... | collective-permute-start | bytes 1179656 | tf_op jit(solution)/shard_map/ppermute | solution.py:99
  352.3 24.8 %collective-permute-done.38 = bf16[128,1536]{1,0:T(8,128)(2,1)S(1)} collective-permute-done((bf16[128,1536]{1,0:T(8,128)(2,1)S(1)}, bf16[128,1536]{1,0:T(8,128)(2,1)S(1)}, u32[]{:S(2)}, u32[]{:S(2)}) %collective-permute-start.38) | collective-permute-done | bytes 393248 | tf_op jit(solution)/shard_map/ppermute | solution.py:99
  378.0 15.0 %collective-permute-done.30 = bf16[128,1536]{1,0:T(8,128)(2,1)S(1)} collective-permute-done((bf16[128,1536]{1,0:T(8,128)(2,1)S(1)}, bf16[128,1536]{1,0:T(8,128)(2,1)S(1)}, u32[]{:S(2)}, u32[]{:S(2)}) %collective-permute-start.30) | collective-permute-done | bytes 393248 | tf_op jit(solution)/shard_map/ppermute | solution.py:99
  396.3 2.3 reshape.530
  425.4 3.9 fusion.142
  435.9 3.2 collective-permute-done.43
  439.1 3.6 collective-permute-done.42
  445.9 3.1 fusion.145
  450.5 2.9 fusion.119
  456.1 3.1 fusion.141
  460.5 3.2 collective-permute-start.48
  466.9 4.3 collective-permute-done.50
  472.0 13.2 %collective-permute-done.49 = bf16[96,1536]{1,0:T(8,128)(2,1)S(1)} collective-permute-done((bf16[96,1536]{1,0:T(8,128)(2,1)S(1)}, bf16[96,1536]{1,0:T(8,128)(2,1)S(1)}, u32[]{:S(2)}, u32[]{:S(2)}) %collective-permute-start.49) | collective-permute-done | bytes 294944 | tf_op jit(solution)/shard_map/ppermute | solution.py:99
  496.3 2.7 collective-permute-start.74
  499.0 2.3 collective-permute-start.72
  502.9 2.9 collective-permute-done.73
  (439 shorter events, 174.9 us)
Async XLA Ops:
  7.2 124.2 %all-gather.2.cloned.1.call-start = ((), (), s32[]{:S(2)}) async-start(), calls=%async_computation | async-start | bytes 4866048 | tf_op jit(solution)/shard_map/all_gather | solution.py:181
  9.0 15.6 %collective-permute-start.2 = (bf16[128,1536]{1,0:T(8,128)(2,1)}, bf16[128,1536]{1,0:T(8,128)(2,1)S(1)}, u32[]{:S(2)}, u32[]{:S(2)}) collective-permute-start(bf16[128,1536]{1,0:T(8,128)(2,1)} %bitcast.457), channel_id=1, source_target_pairs={{0,24},{1,25},{2,26},{3,27},{4,28},{5,29},{6,30},{7,31},{8,16},{9,... | collective-permute-start | bytes 1179656 | tf_op jit(solution)/shard_map/ppermute | solution.py:99
  12.9 18.8 %collective-permute-start.1 = (bf16[128,1536]{1,0:T(8,128)(2,1)}, bf16[128,1536]{1,0:T(8,128)(2,1)S(1)}, u32[]{:S(2)}, u32[]{:S(2)}) collective-permute-start(bf16[128,1536]{1,0:T(8,128)(2,1)} %bitcast.458), channel_id=1, source_target_pairs={{0,16},{1,17},{2,18},{3,19},{4,20},{5,21},{6,22},{7,23},{8,24},{9,... | collective-permute-start | bytes 1179656 | tf_op jit(solution)/shard_map/ppermute | solution.py:99
  13.4 22.1 %collective-permute-start = (bf16[128,1536]{1,0:T(8,128)(2,1)}, bf16[128,1536]{1,0:T(8,128)(2,1)S(1)}, u32[]{:S(2)}, u32[]{:S(2)}) collective-permute-start(bf16[128,1536]{1,0:T(8,128)(2,1)} %bitcast.459), channel_id=1, source_target_pairs={{0,8},{1,9},{2,10},{3,11},{4,12},{5,13},{6,14},{7,15},{8,0},{9,1},... | collective-permute-start | bytes 1179656 | tf_op jit(solution)/shard_map/ppermute | solution.py:99
  14.3 25.3 %collective-permute-start.6 = (bf16[2,48]{1,0:T(2,128)(2,1)S(1)}, bf16[2,48]{1,0:T(2,128)(2,1)S(1)}, u32[]{:S(2)}, u32[]{:S(2)}) collective-permute-start(bf16[2,48]{1,0:T(2,128)(2,1)S(1)} %convert_element_type.269), channel_id=1, source_target_pairs={{0,6},{1,7},{2,4},{3,5},{4,2},{5,3},{6,0},{7,1},{8,14},{9,15},{10,... | collective-permute-start | bytes 584 | tf_op jit(solution)/shard_map/ppermute | solution.py:99
  18.3 21.3 %collective-permute-start.5 = (bf16[2,48]{1,0:T(2,128)(2,1)S(1)}, bf16[2,48]{1,0:T(2,128)(2,1)S(1)}, u32[]{:S(2)}, u32[]{:S(2)}) collective-permute-start(bf16[2,48]{1,0:T(2,128)(2,1)S(1)} %convert_element_type.269), channel_id=1, source_target_pairs={{0,4},{1,5},{2,6},{3,7},{4,0},{5,1},{6,2},{7,3},{8,12},{9,13},{10,... | collective-permute-start | bytes 584 | tf_op jit(solution)/shard_map/ppermute | solution.py:99
  24.6 15.0 %collective-permute-start.4 = (bf16[2,48]{1,0:T(2,128)(2,1)S(1)}, bf16[2,48]{1,0:T(2,128)(2,1)S(1)}, u32[]{:S(2)}, u32[]{:S(2)}) collective-permute-start(bf16[2,48]{1,0:T(2,128)(2,1)S(1)} %convert_element_type.269), channel_id=1, source_target_pairs={{0,2},{1,3},{2,0},{3,1},{4,6},{5,7},{6,4},{7,5},{8,10},{9,11},{10,... | collective-permute-start | bytes 584 | tf_op jit(solution)/shard_map/ppermute | solution.py:99
  31.7 22.7 %collective-permute-start.13 = (bf16[96,1536]{1,0:T(8,128)(2,1)}, bf16[96,1536]{1,0:T(8,128)(2,1)}, u32[]{:S(2)}, u32[]{:S(2)}) collective-permute-start(bf16[96,1536]{1,0:T(8,128)(2,1)} %get-tuple-element.117), channel_id=1, source_target_pairs={{0,6},{1,7},{2,4},{3,5},{4,2},{5,3},{6,0},{7,1},{8,14},{9,15},{10,... | collective-permute-start | bytes 884744 | tf_op jit(solution)/shard_map/ppermute | solution.py:99
  44.2 51.9 %collective-permute-start.12 = (bf16[96,1536]{1,0:T(8,128)(2,1)}, bf16[96,1536]{1,0:T(8,128)(2,1)S(1)}, u32[]{:S(2)}, u32[]{:S(2)}) collective-permute-start(bf16[96,1536]{1,0:T(8,128)(2,1)} %get-tuple-element.117), channel_id=1, source_target_pairs={{0,4},{1,5},{2,6},{3,7},{4,0},{5,1},{6,2},{7,3},{8,12},{9,13},{10,... | collective-permute-start | bytes 884744 | tf_op jit(solution)/shard_map/ppermute | solution.py:99
  45.0 51.0 %collective-permute-start.11 = (bf16[96,1536]{1,0:T(8,128)(2,1)}, bf16[96,1536]{1,0:T(8,128)(2,1)S(1)}, u32[]{:S(2)}, u32[]{:S(2)}) collective-permute-start(bf16[96,1536]{1,0:T(8,128)(2,1)} %get-tuple-element.117), channel_id=1, source_target_pairs={{0,2},{1,3},{2,0},{3,1},{4,6},{5,7},{6,4},{7,5},{8,10},{9,11},{10,... | collective-permute-start | bytes 884744 | tf_op jit(solution)/shard_map/ppermute | solution.py:99
  47.5 95.8 %collective-permute-start.34 = (bf16[128,1536]{1,0:T(8,128)(2,1)}, bf16[128,1536]{1,0:T(8,128)(2,1)}, u32[]{:S(2)}, u32[]{:S(2)}) collective-permute-start(bf16[128,1536]{1,0:T(8,128)(2,1)} %bitcast_select_fusion.1), channel_id=1, source_target_pairs={{0,6},{1,7},{2,4},{3,5},{4,2},{5,3},{6,0},{7,1},{8,14},{9,15},{10,... | collective-permute-start | bytes 1179656 | tf_op jit(solution)/shard_map/ppermute | solution.py:99
  50.4 94.6 %collective-permute-start.33 = (bf16[128,1536]{1,0:T(8,128)(2,1)}, bf16[128,1536]{1,0:T(8,128)(2,1)}, u32[]{:S(2)}, u32[]{:S(2)}) collective-permute-start(bf16[128,1536]{1,0:T(8,128)(2,1)} %bitcast_select_fusion.1), channel_id=1, source_target_pairs={{0,4},{1,5},{2,6},{3,7},{4,0},{5,1},{6,2},{7,3},{8,12},{9,13},{10,... | collective-permute-start | bytes 1179656 | tf_op jit(solution)/shard_map/ppermute | solution.py:99
  114.4 31.8 %collective-permute-start.32 = (bf16[128,1536]{1,0:T(8,128)(2,1)}, bf16[128,1536]{1,0:T(8,128)(2,1)}, u32[]{:S(2)}, u32[]{:S(2)}) collective-permute-start(bf16[128,1536]{1,0:T(8,128)(2,1)} %bitcast_select_fusion.1), channel_id=1, source_target_pairs={{0,2},{1,3},{2,0},{3,1},{4,6},{5,7},{6,4},{7,5},{8,10},{9,11},{10,... | collective-permute-start | bytes 1179656 | tf_op jit(solution)/shard_map/ppermute | solution.py:99
  136.5 14.2 %collective-permute-start.20 = (bf16[128,1536]{1,0:T(8,128)(2,1)}, bf16[128,1536]{1,0:T(8,128)(2,1)}, u32[]{:S(2)}, u32[]{:S(2)}) collective-permute-start(bf16[128,1536]{1,0:T(8,128)(2,1)} %multiply_convert_fusion.11), channel_id=1, source_target_pairs={{0,6},{1,7},{2,4},{3,5},{4,2},{5,3},{6,0},{7,1},{8,14},{9,15},{10,... | collective-permute-start | bytes 1179656 | tf_op jit(solution)/shard_map/ppermute | solution.py:99
  139.5 33.4 %collective-permute-start.19 = (bf16[128,1536]{1,0:T(8,128)(2,1)}, bf16[128,1536]{1,0:T(8,128)(2,1)}, u32[]{:S(2)}, u32[]{:S(2)}) collective-permute-start(bf16[128,1536]{1,0:T(8,128)(2,1)} %multiply_convert_fusion.11), channel_id=1, source_target_pairs={{0,4},{1,5},{2,6},{3,7},{4,0},{5,1},{6,2},{7,3},{8,12},{9,13},{10,... | collective-permute-start | bytes 1179656 | tf_op jit(solution)/shard_map/ppermute | solution.py:99
  143.3 43.1 %collective-permute-start.24 = (bf16[2,1536,128]{1,2,0:T(8,128)(2,1)}, bf16[2,1536,128]{1,2,0:T(8,128)(2,1)S(1)}, u32[]{:S(2)}, u32[]{:S(2)}) collective-permute-start(bf16[2,1536,128]{1,2,0:T(8,128)(2,1)} %copy.81), channel_id=1, source_target_pairs={{0,24},{1,25},{2,26},{3,27},{4,28},{5,29},{6,30},{7,31},{8,16},{9,... | collective-permute-start | bytes 2359304 | tf_op jit(solution)/shard_map/ppermute | solution.py:99
  145.0 41.4 %collective-permute-start.23 = (bf16[2,1536,128]{1,2,0:T(8,128)(2,1)}, bf16[2,1536,128]{1,2,0:T(8,128)(2,1)S(1)}, u32[]{:S(2)}, u32[]{:S(2)}) collective-permute-start(bf16[2,1536,128]{1,2,0:T(8,128)(2,1)} %copy.81), channel_id=1, source_target_pairs={{0,16},{1,17},{2,18},{3,19},{4,20},{5,21},{6,22},{7,23},{8,24},{9,... | collective-permute-start | bytes 2359304 | tf_op jit(solution)/shard_map/ppermute | solution.py:99
  146.2 40.2 %collective-permute-start.22 = (bf16[2,1536,128]{1,2,0:T(8,128)(2,1)}, bf16[2,1536,128]{1,2,0:T(8,128)(2,1)S(1)}, u32[]{:S(2)}, u32[]{:S(2)}) collective-permute-start(bf16[2,1536,128]{1,2,0:T(8,128)(2,1)} %copy.81), channel_id=1, source_target_pairs={{0,8},{1,9},{2,10},{3,11},{4,12},{5,13},{6,14},{7,15},{8,0},{9,1},... | collective-permute-start | bytes 2359304 | tf_op jit(solution)/shard_map/ppermute | solution.py:99
  150.7 42.0 %collective-permute-start.35 = (bf16[4,128,1536]{2,1,0:T(8,128)(2,1)S(1)}, bf16[4,128,1536]{2,1,0:T(8,128)(2,1)S(1)}, u32[]{:S(2)}, u32[]{:S(2)}) collective-permute-start(bf16[4,128,1536]{2,1,0:T(8,128)(2,1)S(1)} %get-tuple-element.84), channel_id=1, source_target_pairs={{0,1},{1,0},{2,3},{3,2},{4,5},{5,4},{6,7},{7,6},{8,9},{9,8},{10,11... | collective-permute-start | bytes 4718600 | tf_op jit(solution)/shard_map/ppermute | solution.py:99
  186.4 24.0 %collective-permute-start.21 = (bf16[4,128,1536]{2,1,0:T(8,128)(2,1)}, bf16[4,128,1536]{2,1,0:T(8,128)(2,1)}, u32[]{:S(2)}, u32[]{:S(2)}) collective-permute-start(bf16[4,128,1536]{2,1,0:T(8,128)(2,1)} %get-tuple-element.89), channel_id=1, source_target_pairs={{0,1},{1,0},{2,3},{3,2},{4,5},{5,4},{6,7},{7,6},{8,9},{9,8},{10,11... | collective-permute-start | bytes 4718600 | tf_op jit(solution)/shard_map/ppermute | solution.py:99
  187.3 13.2 %collective-permute-start.57 = (bf16[128,1536]{1,0:T(8,128)(2,1)}, bf16[128,1536]{1,0:T(8,128)(2,1)}, u32[]{:S(2)}, u32[]{:S(2)}) collective-permute-start(bf16[128,1536]{1,0:T(8,128)(2,1)} %reshape.523), channel_id=1, source_target_pairs={{0,24},{1,25},{2,26},{3,27},{4,28},{5,29},{6,30},{7,31},{8,16},{9,... | collective-permute-start | bytes 1179656 | tf_op jit(solution)/shard_map/ppermute | solution.py:99
  188.7 19.8 %collective-permute-start.56 = (bf16[128,1536]{1,0:T(8,128)(2,1)}, bf16[128,1536]{1,0:T(8,128)(2,1)}, u32[]{:S(2)}, u32[]{:S(2)}) collective-permute-start(bf16[128,1536]{1,0:T(8,128)(2,1)} %reshape.523), channel_id=1, source_target_pairs={{0,16},{1,17},{2,18},{3,19},{4,20},{5,21},{6,22},{7,23},{8,24},{9,... | collective-permute-start | bytes 1179656 | tf_op jit(solution)/shard_map/ppermute | solution.py:99
  189.6 18.9 %collective-permute-start.55 = (bf16[128,1536]{1,0:T(8,128)(2,1)}, bf16[128,1536]{1,0:T(8,128)(2,1)}, u32[]{:S(2)}, u32[]{:S(2)}) collective-permute-start(bf16[128,1536]{1,0:T(8,128)(2,1)} %reshape.523), channel_id=1, source_target_pairs={{0,8},{1,9},{2,10},{3,11},{4,12},{5,13},{6,14},{7,15},{8,0},{9,1},... | collective-permute-start | bytes 1179656 | tf_op jit(solution)/shard_map/ppermute | solution.py:99
  210.2 13.5 %collective-permute-start.58 = (bf16[4,128,1536]{2,1,0:T(8,128)(2,1)S(1)}, bf16[4,128,1536]{2,1,0:T(8,128)(2,1)S(1)}, u32[]{:S(2)}, u32[]{:S(2)}) collective-permute-start(bf16[4,128,1536]{2,1,0:T(8,128)(2,1)S(1)} %get-tuple-element.76), channel_id=1, source_target_pairs={{0,1},{1,0},{2,3},{3,2},{4,5},{5,4},{6,7},{7,6},{8,9},{9,8},{10,11... | collective-permute-start | bytes 4718600 | tf_op jit(solution)/shard_map/ppermute | solution.py:99
  218.0 12.9 %collective-permute-start.67 = (bf16[128,1536]{1,0:T(8,128)(2,1)S(1)}, bf16[128,1536]{1,0:T(8,128)(2,1)S(1)}, u32[]{:S(2)}, u32[]{:S(2)}) collective-permute-start(bf16[128,1536]{1,0:T(8,128)(2,1)S(1)} %get-tuple-element.73), channel_id=1, source_target_pairs={{0,24},{1,25},{2,26},{3,27},{4,28},{5,29},{6,30},{7,31},{8,16},{9,... | collective-permute-start | bytes 1179656 | tf_op jit(solution)/shard_map/ppermute | solution.py:99
  219.5 19.4 %collective-permute-start.66 = (bf16[128,1536]{1,0:T(8,128)(2,1)S(1)}, bf16[128,1536]{1,0:T(8,128)(2,1)S(1)}, u32[]{:S(2)}, u32[]{:S(2)}) collective-permute-start(bf16[128,1536]{1,0:T(8,128)(2,1)S(1)} %get-tuple-element.74), channel_id=1, source_target_pairs={{0,16},{1,17},{2,18},{3,19},{4,20},{5,21},{6,22},{7,23},{8,24},{9,... | collective-permute-start | bytes 1179656 | tf_op jit(solution)/shard_map/ppermute | solution.py:99
  220.4 18.5 %collective-permute-start.65 = (bf16[128,1536]{1,0:T(8,128)(2,1)S(1)}, bf16[128,1536]{1,0:T(8,128)(2,1)S(1)}, u32[]{:S(2)}, u32[]{:S(2)}) collective-permute-start(bf16[128,1536]{1,0:T(8,128)(2,1)S(1)} %get-tuple-element.72), channel_id=1, source_target_pairs={{0,8},{1,9},{2,10},{3,11},{4,12},{5,13},{6,14},{7,15},{8,0},{9,1},... | collective-permute-start | bytes 1179656 | tf_op jit(solution)/shard_map/ppermute | solution.py:99
  241.8 19.0 %collective-permute-start.26 = (bf16[128,1536]{1,0:T(8,128)(2,1)S(1)}, bf16[128,1536]{1,0:T(8,128)(2,1)S(1)}, u32[]{:S(2)}, u32[]{:S(2)}) collective-permute-start(bf16[128,1536]{1,0:T(8,128)(2,1)S(1)} %get-tuple-element.101), channel_id=1, source_target_pairs={{0,16},{1,17},{2,18},{3,19},{4,20},{5,21},{6,22},{7,23},{8,24},{9,... | collective-permute-start | bytes 1179656 | tf_op jit(solution)/shard_map/ppermute | solution.py:99
  242.8 18.1 %collective-permute-start.25 = (bf16[128,1536]{1,0:T(8,128)(2,1)S(1)}, bf16[128,1536]{1,0:T(8,128)(2,1)S(1)}, u32[]{:S(2)}, u32[]{:S(2)}) collective-permute-start(bf16[128,1536]{1,0:T(8,128)(2,1)S(1)} %get-tuple-element.101), channel_id=1, source_target_pairs={{0,8},{1,9},{2,10},{3,11},{4,12},{5,13},{6,14},{7,15},{8,0},{9,1},... | collective-permute-start | bytes 1179656 | tf_op jit(solution)/shard_map/ppermute | solution.py:99
  269.6 49.9 %collective-permute-start.36 = (bf16[4,128,1536]{2,1,0:T(8,128)(2,1)}, bf16[4,128,1536]{2,1,0:T(8,128)(2,1)}, u32[]{:S(2)}, u32[]{:S(2)}) collective-permute-start(bf16[4,128,1536]{2,1,0:T(8,128)(2,1)} %bitcast.92), channel_id=1, source_target_pairs={{0,1},{1,0},{2,3},{3,2},{4,5},{5,4},{6,7},{7,6},{8,9},{9,8},{10,11... | collective-permute-start | bytes 4718600 | tf_op jit(solution)/shard_map/ppermute | solution.py:99
  275.2 21.5 %collective-permute-start.64 = (bf16[2,1536,128]{2,1,0:T(8,128)(2,1)}, bf16[2,1536,128]{2,1,0:T(8,128)(2,1)S(1)}, u32[]{:S(2)}, u32[]{:S(2)}) collective-permute-start(bf16[2,1536,128]{2,1,0:T(8,128)(2,1)} %get-tuple-element.64), channel_id=1, source_target_pairs={{0,24},{1,25},{2,26},{3,27},{4,28},{5,29},{6,30},{7,31},{8,16},{9,... | collective-permute-start | bytes 2359304 | tf_op jit(solution)/shard_map/ppermute | solution.py:99
  276.6 36.5 %collective-permute-start.63 = (bf16[2,1536,128]{2,1,0:T(8,128)(2,1)}, bf16[2,1536,128]{2,1,0:T(8,128)(2,1)S(1)}, u32[]{:S(2)}, u32[]{:S(2)}) collective-permute-start(bf16[2,1536,128]{2,1,0:T(8,128)(2,1)} %get-tuple-element.65), channel_id=1, source_target_pairs={{0,16},{1,17},{2,18},{3,19},{4,20},{5,21},{6,22},{7,23},{8,24},{9,... | collective-permute-start | bytes 2359304 | tf_op jit(solution)/shard_map/ppermute | solution.py:99
  277.5 36.5 %collective-permute-start.62 = (bf16[2,1536,128]{2,1,0:T(8,128)(2,1)S(1)}, bf16[2,1536,128]{2,1,0:T(8,128)(2,1)}, u32[]{:S(2)}, u32[]{:S(2)}) collective-permute-start(bf16[2,1536,128]{2,1,0:T(8,128)(2,1)S(1)} %get-tuple-element.63), channel_id=1, source_target_pairs={{0,8},{1,9},{2,10},{3,11},{4,12},{5,13},{6,14},{7,15},{8,0},{9,1},... | collective-permute-start | bytes 2359304 | tf_op jit(solution)/shard_map/ppermute | solution.py:99
  283.4 44.2 %collective-permute-start.28 = (bf16[4,128,1536]{2,1,0:T(8,128)(2,1)S(1)}, bf16[4,128,1536]{2,1,0:T(8,128)(2,1)S(1)}, u32[]{:S(2)}, u32[]{:S(2)}) collective-permute-start(bf16[4,128,1536]{2,1,0:T(8,128)(2,1)S(1)} %bitcast.486), channel_id=1, source_target_pairs={{0,1},{1,0},{2,3},{3,2},{4,5},{5,4},{6,7},{7,6},{8,9},{9,8},{10,11... | collective-permute-start | bytes 4718600 | tf_op jit(solution)/shard_map/ppermute | solution.py:99
  323.2 14.0 %collective-permute-start.39 = (bf16[128,1536]{1,0:T(8,128)(2,1)S(1)}, bf16[128,1536]{1,0:T(8,128)(2,1)S(1)}, u32[]{:S(2)}, u32[]{:S(2)}) collective-permute-start(bf16[128,1536]{1,0:T(8,128)(2,1)S(1)} %get-tuple-element.81), channel_id=1, source_target_pairs={{0,6},{1,7},{2,4},{3,5},{4,2},{5,3},{6,0},{7,1},{8,14},{9,15},{10,... | collective-permute-start | bytes 1179656 | tf_op jit(solution)/shard_map/ppermute | solution.py:99
  324.0 53.1 %collective-permute-start.38 = (bf16[128,1536]{1,0:T(8,128)(2,1)S(1)}, bf16[128,1536]{1,0:T(8,128)(2,1)S(1)}, u32[]{:S(2)}, u32[]{:S(2)}) collective-permute-start(bf16[128,1536]{1,0:T(8,128)(2,1)S(1)} %get-tuple-element.82), channel_id=1, source_target_pairs={{0,4},{1,5},{2,6},{3,7},{4,0},{5,1},{6,2},{7,3},{8,12},{9,13},{10,... | collective-permute-start | bytes 1179656 | tf_op jit(solution)/shard_map/ppermute | solution.py:99
  325.0 52.1 %collective-permute-start.37 = (bf16[128,1536]{1,0:T(8,128)(2,1)S(1)}, bf16[128,1536]{1,0:T(8,128)(2,1)S(1)}, u32[]{:S(2)}, u32[]{:S(2)}) collective-permute-start(bf16[128,1536]{1,0:T(8,128)(2,1)S(1)} %get-tuple-element.80), channel_id=1, source_target_pairs={{0,2},{1,3},{2,0},{3,1},{4,6},{5,7},{6,4},{7,5},{8,10},{9,11},{10,... | collective-permute-start | bytes 1179656 | tf_op jit(solution)/shard_map/ppermute | solution.py:99
  328.5 49.6 %collective-permute-start.31 = (bf16[128,1536]{1,0:T(8,128)(2,1)S(1)}, bf16[128,1536]{1,0:T(8,128)(2,1)S(1)}, u32[]{:S(2)}, u32[]{:S(2)}) collective-permute-start(bf16[128,1536]{1,0:T(8,128)(2,1)S(1)} %get-tuple-element.86), channel_id=1, source_target_pairs={{0,6},{1,7},{2,4},{3,5},{4,2},{5,3},{6,0},{7,1},{8,14},{9,15},{10,... | collective-permute-start | bytes 1179656 | tf_op jit(solution)/shard_map/ppermute | solution.py:99
  329.3 63.7 %collective-permute-start.30 = (bf16[128,1536]{1,0:T(8,128)(2,1)S(1)}, bf16[128,1536]{1,0:T(8,128)(2,1)S(1)}, u32[]{:S(2)}, u32[]{:S(2)}) collective-permute-start(bf16[128,1536]{1,0:T(8,128)(2,1)S(1)} %get-tuple-element.87), channel_id=1, source_target_pairs={{0,4},{1,5},{2,6},{3,7},{4,0},{5,1},{6,2},{7,3},{8,12},{9,13},{10,... | collective-permute-start | bytes 1179656 | tf_op jit(solution)/shard_map/ppermute | solution.py:99
  337.2 55.9 %collective-permute-start.29 = (bf16[128,1536]{1,0:T(8,128)(2,1)S(1)}, bf16[128,1536]{1,0:T(8,128)(2,1)S(1)}, u32[]{:S(2)}, u32[]{:S(2)}) collective-permute-start(bf16[128,1536]{1,0:T(8,128)(2,1)S(1)} %get-tuple-element.85), channel_id=1, source_target_pairs={{0,2},{1,3},{2,0},{3,1},{4,6},{5,7},{6,4},{7,5},{8,10},{9,11},{10,... | collective-permute-start | bytes 1179656 | tf_op jit(solution)/shard_map/ppermute | solution.py:99
  434.7 14.7 %collective-permute-start.61 = (bf16[48,1536]{1,0:T(8,128)(2,1)}, bf16[48,1536]{1,0:T(8,128)(2,1)}, u32[]{:S(2)}, u32[]{:S(2)}) collective-permute-start(bf16[48,1536]{1,0:T(8,128)(2,1)} %get-tuple-element.112), channel_id=1, source_target_pairs={{0,6},{1,7},{2,4},{3,5},{4,2},{5,3},{6,0},{7,1},{8,14},{9,15},{10,... | collective-permute-start | bytes 442376 | tf_op jit(solution)/shard_map/ppermute | solution.py:99
  435.9 13.5 %collective-permute-start.60 = (bf16[48,1536]{1,0:T(8,128)(2,1)}, bf16[48,1536]{1,0:T(8,128)(2,1)}, u32[]{:S(2)}, u32[]{:S(2)}) collective-permute-start(bf16[48,1536]{1,0:T(8,128)(2,1)} %get-tuple-element.113), channel_id=1, source_target_pairs={{0,4},{1,5},{2,6},{3,7},{4,0},{5,1},{6,2},{7,3},{8,12},{9,13},{10,... | collective-permute-start | bytes 442376 | tf_op jit(solution)/shard_map/ppermute | solution.py:99
  449.2 14.5 %collective-permute-start.44 = (bf16[4,128,1536]{2,1,0:T(8,128)(2,1)S(1)}, bf16[4,128,1536]{2,1,0:T(8,128)(2,1)S(1)}, u32[]{:S(2)}, u32[]{:S(2)}) collective-permute-start(bf16[4,128,1536]{2,1,0:T(8,128)(2,1)S(1)} %bitcast.485), channel_id=1, source_target_pairs={{0,1},{1,0},{2,3},{3,2},{4,5},{5,4},{6,7},{7,6},{8,9},{9,8},{10,11... | collective-permute-start | bytes 4718600 | tf_op jit(solution)/shard_map/ppermute | solution.py:99
  460.5 24.6 %collective-permute-start.49 = (bf16[96,1536]{1,0:T(8,128)(2,1)S(1)}, bf16[96,1536]{1,0:T(8,128)(2,1)S(1)}, u32[]{:S(2)}, u32[]{:S(2)}) collective-permute-start(bf16[96,1536]{1,0:T(8,128)(2,1)S(1)} %get-tuple-element.94), channel_id=1, source_target_pairs={{0,4},{1,5},{2,6},{3,7},{4,0},{5,1},{6,2},{7,3},{8,12},{9,13},{10,... | collective-permute-start | bytes 884744 | tf_op jit(solution)/shard_map/ppermute | solution.py:99
  460.5 24.6 %collective-permute-start.48 = (bf16[96,1536]{1,0:T(8,128)(2,1)S(1)}, bf16[96,1536]{1,0:T(8,128)(2,1)S(1)}, u32[]{:S(2)}, u32[]{:S(2)}) collective-permute-start(bf16[96,1536]{1,0:T(8,128)(2,1)S(1)} %get-tuple-element.92), channel_id=1, source_target_pairs={{0,2},{1,3},{2,0},{3,1},{4,6},{5,7},{6,4},{7,5},{8,10},{9,11},{10,... | collective-permute-start | bytes 884744 | tf_op jit(solution)/shard_map/ppermute | solution.py:99
  464.5 22.0 %collective-permute-start.47 = (bf16[128,1536]{1,0:T(8,128)(2,1)S(1)}, bf16[128,1536]{1,0:T(8,128)(2,1)S(1)}, u32[]{:S(2)}, u32[]{:S(2)}) collective-permute-start(bf16[128,1536]{1,0:T(8,128)(2,1)S(1)} %get-tuple-element.78), channel_id=1, source_target_pairs={{0,24},{1,25},{2,26},{3,27},{4,28},{5,29},{6,30},{7,31},{8,16},{9,... | collective-permute-start | bytes 1179656 | tf_op jit(solution)/shard_map/ppermute | solution.py:99
  465.9 20.6 %collective-permute-start.46 = (bf16[128,1536]{1,0:T(8,128)(2,1)S(1)}, bf16[128,1536]{1,0:T(8,128)(2,1)S(1)}, u32[]{:S(2)}, u32[]{:S(2)}) collective-permute-start(bf16[128,1536]{1,0:T(8,128)(2,1)S(1)} %get-tuple-element.79), channel_id=1, source_target_pairs={{0,16},{1,17},{2,18},{3,19},{4,20},{5,21},{6,22},{7,23},{8,24},{9,... | collective-permute-start | bytes 1179656 | tf_op jit(solution)/shard_map/ppermute | solution.py:99
  471.1 15.4 %collective-permute-start.45 = (bf16[128,1536]{1,0:T(8,128)(2,1)S(1)}, bf16[128,1536]{1,0:T(8,128)(2,1)S(1)}, u32[]{:S(2)}, u32[]{:S(2)}) collective-permute-start(bf16[128,1536]{1,0:T(8,128)(2,1)S(1)} %get-tuple-element.77), channel_id=1, source_target_pairs={{0,8},{1,9},{2,10},{3,11},{4,12},{5,13},{6,14},{7,15},{8,0},{9,1},... | collective-permute-start | bytes 1179656 | tf_op jit(solution)/shard_map/ppermute | solution.py:99
  (112 other events, 1091.8 us)
Sparse Core Ops, SparseCore 0:
  11.6 89.2 all-gather.1

commit v2 on v1

v2 whole, which is shorter than its diff:
```python
import functools
import math

import jax
import jax.numpy as jnp
from jax import lax
from jax.experimental import pallas as pl
from jax.experimental.pallas import tpu as pltpu
from jax.sharding import Mesh
from jax.sharding import PartitionSpec as P

D = 1536
HEADS = 16
KV_HEADS = 8
HEAD_DIM = 96
HALF = HEAD_DIM // 2
ALL_HEADS = HEADS + 2 * KV_HEADS
GROUPS = HEADS // KV_HEADS

EPS = 1e-05
THETA = 10000.0
MASKED = -1e30
MOMENTUM_RATE = 0.9
AVERAGE_RATE = 0.75
RATE_BASE = 0.1
AXES = ("dp", "z", "core")
PLANE = ("dp", "core")
NN = (((1,), (0,)), ((), ()))
TN = (((0,), (0,)), ((), ()))
NT = (((1,), (1,)), ((), ()))
VMEM_SLACK = 12 * 1024 * 1024
TILE = 256

bf16 = jnp.bfloat16
f32 = jnp.float32


def dot(a, b, dims):
    return lax.dot_general(a, b, dims, preferred_element_type=f32)


def low(values):
    return values.astype(bf16)


def wide(values):
    return values.astype(f32)


def rms_scale(values):
    return lax.rsqrt(jnp.mean(values * values, axis=-1, keepdims=True) + EPS)


def rotary_rows(seq_len, slots, heads):
    positions = jnp.arange(seq_len, dtype=f32)
    halves = jnp.arange(HALF, dtype=f32)
    frequencies = jnp.power(THETA, -2.0 * halves / HEAD_DIM)
    angles = positions[:, None] * frequencies[None, :]
    cos_table, sine_table = jnp.cos(angles), jnp.sin(angles)
    cos_rows = jnp.concatenate([cos_table, cos_table], axis=1)
    sine_rows = jnp.concatenate([-sine_table, sine_table], axis=1)
    return jnp.tile(cos_rows, (slots, heads)), jnp.tile(sine_rows, (slots, heads))


def swap_halves(values):
    width = values.shape[1]
    if width % 128 == 0:
        left = pltpu.roll(values, width - HALF, 1)
        right = pltpu.roll(values, HALF, 1)
    else:
        left = jnp.concatenate([values[:, HALF:], values[:, :HALF]], axis=1)
        right = jnp.concatenate([values[:, -HALF:], values[:, :-HALF]], axis=1)
    column = lax.broadcasted_iota(jnp.int32, values.shape, 1)
    return jnp.where(lax.rem(column, HEAD_DIM) < HALF, left, right)


def kernel_call(body, outs, ins, smem=(), hbm=(), scratch=(), sems=()):
    moved = [i for i in range(len(ins)) if i not in smem and i not in hbm]

    def fetched(*refs):
        given, rest = list(refs[: len(ins)]), refs[len(ins) :]
        held, sems = rest[-1 - len(moved) : -1], rest[-1]
        copies = [
            pltpu.make_async_copy(given[i], held[j], sems.at[j]) for j, i in enumerate(moved)
        ]
        for copy in copies:
            copy.start()
        for copy in copies:
            copy.wait()
        for j, i in enumerate(moved):
            given[i] = held[j]
        body(*given, *rest[: -1 - len(moved)])

    arrays = [*outs, *((ins[i].shape, ins[i].dtype) for i in moved)]
    arrays += scratch
    held_bytes = sum(math.prod(s) * jnp.dtype(t).itemsize for s, t in arrays)
    outputs = pl.pallas_call(
        fetched,
        out_shape=[jax.ShapeDtypeStruct(s, t) for s, t in outs],
        in_specs=[
            pl.BlockSpec(memory_space=pltpu.SMEM if i in smem else pltpu.HBM)
            for i in range(len(ins))
        ],
        out_specs=[pl.BlockSpec(memory_space=pltpu.VMEM)] * len(outs),
        scratch_shapes=[
            *(pltpu.VMEM(s, t) for s, t in scratch),
            *(pltpu.SemaphoreType.DMA(s) for s in sems),
            *(pltpu.VMEM(ins[i].shape, ins[i].dtype) for i in moved),
            pltpu.SemaphoreType.DMA((len(moved),)),
        ],
        compiler_params=pltpu.CompilerParams(vmem_limit_bytes=held_bytes + VMEM_SLACK),
        cost_estimate=pl.CostEstimate(flops=0, bytes_accessed=0, transcendentals=0),
    )(*ins)
    return list(outputs)


def project_body(x_ref, w_ref, gains_ref, cos_ref, sine_ref, out_ref, normed_ref, rows_ref):
    if gains_ref.shape[1] == D:
        rows_ref[...] = gains_ref[...]
    else:
        gains = wide(gains_ref[...])
        width = gains.shape[1] // 2
        for i in range(2):
            rows_ref[i : i + 1, :] = jnp.concatenate(
                [
                    gains[d : d + 1, i * width : (i + 1) * width]
                    for d in range(gains.shape[0])
                ],
                axis=1,
            )
    for k in range(x_ref.shape[0]):
        x = wide(x_ref[k])
        normed_ref[k] = low(x * rms_scale(x) * rows_ref[0:1, :])
        p = dot(normed_ref[k], w_ref[...], NT)
        out_ref[k] = low(p * cos_ref[...] + swap_halves(p) * sine_ref[...])


def head_columns(blocks_ref, head):
    per = blocks_ref.shape[2] // HEAD_DIM
    at = (head % per) * HEAD_DIM
    return blocks_ref[head // per, :, at : at + HEAD_DIM]


def attend_body(slots, len_ref, qkv_ref, prob_ref, att_ref):
    rows = qkv_ref.shape[1]
    seq_len = rows // slots
    shape = (GROUPS * rows, rows)
    row = lax.rem(lax.broadcasted_iota(jnp.int32, shape, 0), rows)
    col = lax.broadcasted_iota(jnp.int32, shape, 1)
    limit = jnp.zeros(shape, jnp.int32)
    for b in range(slots):
        limit = jnp.where(row >= b * seq_len, b * seq_len + len_ref[b], limit)
    first = row - lax.rem(row, seq_len)
    allowed = (col >= first) & (col <= row) & (col < limit)
    outs = []
    for g in range(KV_HEADS):
        q = jnp.concatenate([head_columns(qkv_ref, GROUPS * g + i) for i in range(GROUPS)], axis=0)
        k = head_columns(qkv_ref, HEADS + g)
        v = head_columns(qkv_ref, HEADS + KV_HEADS + g)
        s = jnp.where(allowed, dot(q, k, NT) * HEAD_DIM ** (-0.5), MASKED)
        e = jnp.exp(s - jnp.max(s, axis=-1, keepdims=True))
        p = e / jnp.sum(e, axis=-1, keepdims=True)
        prob_ref[g] = p
        o = dot(low(p), v, NN)
        outs += [o[i * rows : (i + 1) * rows] for i in range(GROUPS)]
    att_ref[...] = low(jnp.concatenate(outs, axis=1))


def out_body(n_z, at_ref, att_ref, x_ref, gain_ref, *refs):
    hidden_ref, normed_ref, wo_ref, sem = refs[-4:]
    parts = refs[:-4]
    copies = []
    if len(parts) == 1:
        copies.append(pltpu.make_async_copy(parts[0], wo_ref, sem))
    else:
        for c, part in enumerate(parts):
            for k in range(part.shape[0]):
                to = (at_ref[0] ^ (k // n_z)) * n_z + (at_ref[1] ^ (k % n_z))
                to = to * 2 + (at_ref[2] ^ c)
                copies.append(pltpu.make_async_copy(part.at[k], wo_ref.at[to], sem))
    for copy in copies:
        copy.start()
    for copy in copies:
        copy.wait()
    hidden = wide(x_ref[...]) + dot(att_ref[...], wo_ref[...].reshape(D, D), NT)
    hidden_ref[...] = hidden
    normed_ref[...] = low(hidden * rms_scale(hidden) * gain_ref[1:2, :])


def units_back_body(n, tile, *refs):
    dy_refs, (w_ref, rows_ref, out_ref, held_ref, sems) = refs[:n], refs[n:]
    tiles = range(0, held_ref.shape[0], tile)
    copies = [
        pltpu.make_async_copy(
            w_ref.at[2, pl.ds(j, tile)], held_ref.at[pl.ds(j, tile)], sems.at[i]
        )
        for i, j in enumerate(tiles)
    ]
    for copy in copies:
        copy.start()
    rows = dy_refs[0].shape[0]
    for k in range(n):
        rows_ref[k * rows : (k + 1) * rows, :] = dy_refs[k][...]
    for copy, j in zip(copies, tiles):
        copy.wait()
        out_ref[:, j : j + tile] = dot(rows_ref[...], held_ref[j : j + tile, :], NT)


def units_body(n, tile, *refs):
    n2_refs, (w_ref, da_ref) = refs[:n], refs[n : n + 2]
    rows_ref, act_ref, gate_ref, up_ref = refs[n + 2 : n + 6]
    own_ref, out_refs = refs[n + 6], refs[n + 7 : 2 * n + 6]
    held_ref, sems, row_sems = refs[2 * n + 6 :]
    tiles = range(0, held_ref.shape[1], tile)
    copies = [
        [
            pltpu.make_async_copy(
                w_ref.at[p, pl.ds(j, tile)], held_ref.at[p, pl.ds(j, tile)], sems.at[p, i]
            )
            for p in range(2)
        ]
        for i, j in enumerate(tiles)
    ]
    for pair in copies:
        for copy in pair:
            copy.start()
    rows = n2_refs[0].shape[0]
    moves = [
        pltpu.make_async_copy(n2_refs[k], rows_ref.at[pl.ds(k * rows, rows)], row_sems.at[k])
        for k in range(n)
    ]
    for move in moves:
        move.start()
    for move in moves:
        move.wait()
    for pair, j in zip(copies, tiles):
        for copy in pair:
            copy.wait()
        at = slice(j, j + tile)
        gate = dot(rows_ref[...], held_ref[0, at, :], NT)
        up = dot(rows_ref[...], held_ref[1, at, :], NT)
        da = da_ref[:, at]
        sig = jax.nn.sigmoid(gate)
        silu = gate * sig
        act_ref[:, at] = low(silu * up)
        gate_ref[:, at] = low(da * up * sig * (1.0 + gate * (1.0 - sig)))
        up_ref[:, at] = low(da * silu)
    for j in range(0, D, tile):
        at = slice(j, j + tile)
        back = dot(gate_ref[...], held_ref[0, :, at], NN) + dot(
            up_ref[...], held_ref[1, :, at], NN
        )
        own_ref[:, at] = back[:rows]
        for k in range(1, n):
            out_refs[k - 1][:, at] = low(back[k * rows : (k + 1) * rows])


def norm_back_body(n_z, n, at_ref, own_ref, *refs):
    got = refs[: n_z - 1]
    hidden_ref, gain_ref, up_ref = refs[n_z - 1 : n_z + 2]
    grad_ref, low_ref, gain_grad_ref = refs[n_z + 2 : n_z + 5]
    col_refs, held_ref, sems = refs[n_z + 5 : -2], refs[-2], refs[-1]
    width = D // n
    copies = [pltpu.make_async_copy(r, held_ref.at[k], sems.at[k]) for k, r in enumerate(got)]
    for copy in copies:
        copy.start()
    hidden = hidden_ref[...]
    scale = rms_scale(hidden)
    unit = hidden * scale
    dn = own_ref[...]
    for k, copy in enumerate(copies):
        copy.wait()
        dn = dn + wide(held_ref[k])
    gain_grad_ref[...] = jnp.sum(dn * unit, axis=0, keepdims=True)
    scaled = dn * gain_ref[1:2, :]
    grad = wide(up_ref[...]) + scale * (
        scaled - unit * jnp.mean(scaled * unit, axis=-1, keepdims=True)
    )
    grad_ref[...] = grad
    low_ref[...] = low(grad)
    if col_refs:
        for k in range(n):
            at = pl.multiple_of((at_ref[0] ^ k) * width, 128)
            col_refs[k][...] = low_ref[:, pl.ds(at, width)]


def attend_back_body(n, grad_ref, wo_ref, qkv_ref, prob_ref, cos_ref, sine_ref, heads_ref):
    rows = grad_ref.shape[0]
    do = low(dot(grad_ref[...], wo_ref[...], NN))
    grads = [None] * ALL_HEADS
    root = HEAD_DIM ** (-0.5)
    for g in range(KV_HEADS):
        q = jnp.concatenate([head_columns(qkv_ref, GROUPS * g + i) for i in range(GROUPS)], axis=0)
        k = head_columns(qkv_ref, HEADS + g)
        v = head_columns(qkv_ref, HEADS + KV_HEADS + g)
        d = jnp.concatenate(
            [
                do[:, h * HEAD_DIM : (h + 1) * HEAD_DIM]
                for h in range(GROUPS * g, GROUPS * g + GROUPS)
            ],
            axis=0,
        )
        p = prob_ref[g]
        dp = dot(d, v, NT)
        ds = low(p * (dp - jnp.sum(p * dp, axis=-1, keepdims=True)))
        dq = dot(ds, k, NN) * root
        for i in range(GROUPS):
            grads[GROUPS * g + i] = dq[i * rows : (i + 1) * rows]
        grads[HEADS + g] = dot(ds, q, TN) * root
        grads[HEADS + KV_HEADS + g] = dot(low(p), d, TN)
    per = ALL_HEADS // n
    for j in range(n):
        block = jnp.concatenate(grads[j * per : (j + 1) * per], axis=1)
        turned = max(0, min(per, HEADS + KV_HEADS - j * per))
        if turned:
            back = block * cos_ref[...] - swap_halves(block) * sine_ref[...]
            if turned < per:
                column = lax.broadcasted_iota(jnp.int32, block.shape, 1)
                back = jnp.where(column < turned * HEAD_DIM, back, block)
            block = back
        heads_ref[j] = low(block)


def units_grad_body(n, gate_ref, up_ref, act_ref, rows_ref, dy_ref, w_ref, *refs):
    out_ref, own_ref, part_refs = refs[0], refs[1], refs[2 : n + 1]
    held_ref, sem = refs[n + 1 :]
    copy = pltpu.make_async_copy(w_ref.at[2], held_ref, sem)
    copy.start()
    for j in range(0, gate_ref.shape[1], TILE):
        at = slice(j, j + TILE)
        out_ref[0, at, :] = low(dot(gate_ref[:, at], rows_ref[...], TN))
        out_ref[1, at, :] = low(dot(up_ref[:, at], rows_ref[...], TN))
        out_ref[2, at, :] = low(dot(act_ref[:, at], dy_ref[...], TN))
    copy.wait()
    rows = own_ref.shape[0]
    for j in range(0, D, TILE):
        at = slice(j, j + TILE)
        out = dot(act_ref[...], held_ref[:, at], NN)
        own_ref[:, at] = out[:rows]
        for k in range(1, n):
            part_refs[k - 1][:, at] = low(out[k * rows : (k + 1) * rows])


def columns_grad_body(n, at_ref, in_ref, normed_ref, att_ref, *refs):
    col_refs, (mine_ref, other_ref, held_ref, sum_ref) = refs[:n], refs[n:]
    for k in range(n):
        held_ref[at_ref[0] ^ k] = col_refs[k][...]
    n_z = mine_ref.shape[0]
    blocks = 2 * n_z
    grads = in_ref[...].reshape(-1, in_ref.shape[2])
    cols = held_ref[...].reshape(-1, held_ref.shape[2])
    normed = normed_ref[...].reshape(-1, D)
    att = att_ref[...].reshape(-1, D)
    first, second = grads.shape[1] // blocks, cols.shape[1] // blocks
    for j in range(0, D, 512):
        at = slice(j, j + 512)
        one = dot(grads, normed[:, at], TN)
        two = dot(cols, att[:, at], TN)
        for i in range(blocks):
            sum_ref[i, :first, at] = one[i * first : (i + 1) * first]
            sum_ref[i, first:, at] = two[i * second : (i + 1) * second]
    for z in range(n_z):
        i = (at_ref[1] ^ z) * 2
        mine_ref[z] = sum_ref[i + at_ref[2]]
        other_ref[z] = low(sum_ref[i + (at_ref[2] ^ 1)])


def add_body(mine_ref, other_ref, own_ref, *out_refs):
    own_ref[...] = mine_ref[0] + wide(other_ref[0])
    for k, ref in enumerate(out_refs):
        ref[...] = low(mine_ref[k + 1] + wide(other_ref[k + 1]))


def inputs_grad_body(grad_ref, w_ref, x_ref, out_ref, gain_ref):
    total = jnp.zeros((1, D), f32)
    for k in range(x_ref.shape[0]):
        back = dot(grad_ref[k], w_ref[...], NN)
        x = wide(x_ref[k])
        total = total + jnp.sum(back * (x * rms_scale(x)), axis=0, keepdims=True)
        out_ref[k] = low(back)
    gain_ref[...] = total


def settle_body(rate, n, *refs):
    grad_refs, refs = refs[:n], refs[n:]
    at = 0
    for ins, outs in ((refs[0:3], refs[6:11]), (refs[3:6], refs[11:16])):
        weight, moment, average = (r[...] for r in ins)
        gradient = sum(wide(r[at : at + weight.shape[0], :]) for r in grad_refs)
        at += weight.shape[0]
        for ref, value in zip(outs, update(weight, gradient, moment, average, rate)):
            ref[...] = value


def pack_body(gate_ref, down_ref, out_ref):
    out_ref[0] = low(gate_ref[0].T)
    out_ref[1] = low(gate_ref[1].T)
    out_ref[2] = low(down_ref[...])


def update_body(rate, flip, n, *refs):
    grad_ref, refs = refs[0], refs[1:]
    for i in range(n):
        weight, moment, average = (r[i] for r in refs[:3])
        gradient = wide(grad_ref[i].T if flip else grad_ref[i])
        for ref, value in zip(refs[3:], update(weight, gradient, moment, average, rate)):
            ref[i] = value


def update(weight, gradient, moment, average, step_rate):
    moment_new = MOMENTUM_RATE * moment + gradient
    weight_new = weight - step_rate * (gradient + MOMENTUM_RATE * moment_new)
    average_new = AVERAGE_RATE * average + (1.0 - AVERAGE_RATE) * weight_new
    return (gradient, moment_new, weight_new, average_new, weight_new.astype(bf16))


class Links:
    def __init__(self, n_dp, n_z):
        assert n_dp & (n_dp - 1) == 0 and n_z & (n_z - 1) == 0
        self.count = n_dp * n_z * 2
        self.dp = [n_z * 2 * k for k in range(n_dp)]
        self.z = [2 * k for k in range(n_z)]

    def send(self, values, mask):
        return lax.ppermute(values, AXES, [(i, i ^ mask) for i in range(self.count)])

    def gather(self, values, masks):
        return [values] + [self.send(values, m) for m in masks[1:]]

    def spread(self, blocks, masks):
        return [blocks[0]] + [self.send(b, m) for b, m in zip(blocks[1:], masks[1:])]


def block_of(values, index):
    return lax.dynamic_index_in_dim(values, index, keepdims=False)


def exchange(values, axes):
    return lax.all_to_all(values, axes, split_axis=0, concat_axis=0, tiled=True)


def tie(*values):
    return lax.optimization_barrier(values)


def on_device(
    tokens,
    cotangent,
    lengths,
    in_proj,
    out_proj,
    gate_up,
    down_proj,
    gains_pair,
    in_proj_mom,
    out_proj_mom,
    gate_up_mom,
    down_proj_mom,
    gains_mom,
    in_proj_avg,
    out_proj_avg,
    gate_up_avg,
    down_proj_avg,
    gains_avg,
):
    n_dp, n_z = lax.axis_size("dp"), lax.axis_size("z")
    n_zc = n_z * 2
    links = Links(n_dp, n_z)
    devices = links.count
    at_dp, at_z, at_core = (lax.axis_index(a) for a in AXES)
    at = jnp.stack([at_dp, at_z, at_core]).astype(jnp.int32)
    slots, seq_len = tokens.shape[:2]
    rows = slots * seq_len
    step_rate = RATE_BASE / math.sqrt(slots * devices * seq_len)
    in_width = in_proj.shape[1]
    out_width = out_proj.shape[1]
    ff_width = down_proj.shape[0]
    group = n_zc * in_width
    heads_here = group // HEAD_DIM
    aligned = in_width % 16 == 0 and out_width % 16 == 0

    in_low = low(jnp.transpose(in_proj))
    out_low = low(jnp.transpose(out_proj))
    gain_low = low(gains_pair)
    token_rows = tokens.reshape(rows, D)

    out_z = links.gather(out_low, links.z)
    in_group = lax.all_gather(in_low, ("z", "core"), axis=0, tiled=True)
    token_group = exchange(jnp.tile(token_rows[None], (n_dp, 1, 1)), "dp")
    cos_rows, sine_rows = rotary_rows(seq_len, slots, heads_here)
    head = at_dp * heads_here + jnp.arange(group) // HEAD_DIM
    turned = (head < HEADS + KV_HEADS)[None, :]
    cos_here = jnp.where(turned, cos_rows, 1.0)
    sine_here = jnp.where(turned, sine_rows, 0.0)
    gain_all = jnp.tile(gain_low.reshape(1, -1), (devices, 1))
    gain_all, cos_here, sine_here, cos_rows, sine_rows = tie(
        gain_all, cos_here, sine_here, cos_rows, sine_rows
    )
    gain_all, token_group, out_z = tie(gain_all, token_group, out_z)
    gain_all = exchange(gain_all, AXES)
    out_own = links.gather(jnp.stack(out_z), links.dp)
    gain_all, out_own, in_group = tie(gain_all, out_own, in_group)
    row_valid = (jnp.arange(seq_len)[None, :] < lengths[:, None]).reshape(rows, 1)
    upstream = jnp.where(row_valid, cotangent.reshape(rows, D), jnp.zeros((), bf16))
    upstream, in_group = tie(upstream, in_group)
    upstream_parts = links.gather(upstream, links.z)
    if not aligned:
        gain_all = wide(gain_all).reshape(devices, 2, -1)
        gain_all = jnp.swapaxes(gain_all, 0, 1).reshape(2, D)

    (ff_low,) = kernel_call(pack_body, [((3, ff_width, D), bf16)], [gate_up, down_proj])
    ff_low, in_group = tie(ff_low, in_group)
    ff = lax.all_gather(ff_low, PLANE, axis=1, tiled=True)

    blocks, normed_group, gain_rows = kernel_call(
        project_body,
        [
            ((n_dp, rows, group), bf16),
            ((n_dp, rows, D), bf16),
            ((2, D), f32),
        ],
        [token_group, in_group, gain_all, cos_here, sine_here],
    )
    qkv = exchange(blocks, "dp")

    out_own = jnp.stack(out_own).reshape(n_dp * n_z, out_width, D)
    out_other = links.send(out_own, 1)
    out_parts = [out_own, out_other]
    if not aligned:
        both = jnp.stack(out_parts)
        out_here = at_dp * n_z + at_z
        out_parts = [
            jnp.stack(
                [
                    block_of(block_of(both, at_core ^ c), out_here ^ k)
                    for k in range(n_dp * n_z)
                    for c in range(2)
                ]
            )
        ]

    prob, attended = kernel_call(
        functools.partial(attend_body, slots),
        [((KV_HEADS, GROUPS * rows, rows), f32), ((rows, D), bf16)],
        [lengths.astype(jnp.int32), qkv],
        smem=(0,),
    )
    attended, upstream_parts = tie(attended, upstream_parts)
    hidden, normed_two, out_full = kernel_call(
        functools.partial(out_body, n_z),
        [((rows, D), f32), ((rows, D), bf16), ((devices, out_width, D), bf16)],
        [at, attended, token_rows, gain_rows, *out_parts],
        smem=(0,),
        hbm=range(4, 4 + len(out_parts)),
        sems=[()],
    )
    out_full = out_full.reshape(D, D)

    normed_parts = links.gather(normed_two, links.z)
    attended_group = lax.all_gather(attended, "dp", axis=0)
    group_rows, units = n_z * rows, n_dp * 2 * ff_width
    upstream_group, grad_active = kernel_call(
        functools.partial(units_back_body, n_z, TILE),
        [((group_rows, D), bf16), ((group_rows, units), f32)],
        [*upstream_parts, ff],
        hbm=(n_z,),
        scratch=[((units, D), bf16)],
        sems=[(units // TILE,)],
    )
    normed_parts, grad_active = tie(normed_parts, grad_active)
    normed_rows, active, grad_gate, grad_up, *grad_normed = kernel_call(
        functools.partial(units_body, n_z, TILE),
        [((group_rows, D), bf16)]
        + [((group_rows, units), bf16)] * 3
        + [((rows, D), f32)]
        + [((rows, D), bf16)] * (n_z - 1),
        [*normed_parts, ff, grad_active],
        hbm=range(n_z + 1),
        scratch=[((2, units, D), bf16)],
        sems=[(2, units // TILE), (n_z,)],
    )
    grad_normed = links.spread(grad_normed, links.z)
    grad_ff, *partial_out = kernel_call(
        functools.partial(units_grad_body, n_z),
        [((3, units, D), bf16), ((rows, D), f32)] + [((rows, D), bf16)] * (n_z - 1),
        [grad_gate, grad_up, active, normed_rows, upstream_group, ff],
        hbm=(5,),
        scratch=[((units, D), bf16)],
        sems=[()],
    )
    grad_ff, partial_out, grad_normed = tie(grad_ff, partial_out, grad_normed)
    grad_ff = lax.psum_scatter(grad_ff, PLANE, scatter_dimension=1, tiled=True)
    partial_out = links.spread(partial_out, links.z)

    col_width = D // n_dp
    col_aligned = col_width % 128 == 0
    grad_hidden, grad_branch, gain_two_grad, *columns = kernel_call(
        functools.partial(norm_back_body, n_z, n_dp),
        [((rows, D), f32), ((rows, D), bf16), ((1, D), f32)]
        + ([((rows, col_width), bf16)] * n_dp if col_aligned else []),
        [at, *grad_normed, hidden, gain_rows, upstream],
        smem=(0,),
        hbm=range(2, n_z + 1),
        scratch=[((n_z - 1, rows, D), bf16)],
        sems=[(n_z - 1,)],
    )
    if not col_aligned:
        split = jnp.swapaxes(grad_branch.reshape(rows, n_dp, col_width), 0, 1)
        columns = [block_of(split, at_dp ^ k) for k in range(n_dp)]
    columns = links.spread(columns, links.dp)

    (blocks,) = kernel_call(
        functools.partial(attend_back_body, n_dp),
        [((n_dp, rows, group), bf16)],
        [grad_branch, out_full, qkv, prob, cos_rows, sine_rows],
    )
    blocks, partial_out[-1] = tie(blocks, partial_out[-1])
    grad_proj = exchange(blocks, "dp")
    grad_proj, partial_out, columns = tie(grad_proj, partial_out, columns)

    col_rows = in_width + out_width
    if aligned:
        mine, other = kernel_call(
            functools.partial(columns_grad_body, n_dp),
            [((n_z, col_rows, D), f32), ((n_z, col_rows, D), bf16)],
            [at, grad_proj, normed_group, attended_group, *columns],
            scratch=[((n_dp, rows, col_width), bf16), ((n_zc, col_rows, D), f32)],
            smem=(0,),
        )
    else:
        columns = jnp.stack(columns)
        columns = jnp.concatenate([block_of(columns, at_dp ^ k) for k in range(n_dp)])
        total = jnp.concatenate(
            [
                dot(lhs.reshape(n_dp * rows, -1), rhs.reshape(-1, D), TN).reshape(n_zc, -1, D)
                for lhs, rhs in ((grad_proj, normed_group), (columns, attended_group))
            ],
            axis=1,
        ).reshape(n_z, 2, col_rows, D)
        mine, other = (
            jnp.stack(
                [block_of(block_of(total, at_z ^ z), at_core ^ c) for z in range(n_z)]
            )
            for c in range(2)
        )
        other = low(other)
    grad_proj, mine = tie(grad_proj, mine)
    other = links.send(other, 1)
    grad_cols = kernel_call(
        add_body,
        [((col_rows, D), f32)] + [((col_rows, D), bf16)] * (n_z - 1),
        [mine, other],
    )
    grad_normed_one, gain_one_grad = kernel_call(
        inputs_grad_body,
        [((n_dp, rows, D), bf16), ((1, D), f32)],
        [grad_proj, in_group, token_group],
    )
    grad_gains = jnp.concatenate([gain_one_grad, gain_two_grad])
    grad_gains = jnp.swapaxes(grad_gains.reshape(2, devices, -1), 0, 1).reshape(devices, -1)
    grad_gains = exchange(grad_gains, AXES)
    grad_normed_one, grad_gains, grad_cols[0] = tie(grad_normed_one, grad_gains, grad_cols[0])
    grad_cols = links.spread(grad_cols, links.z)
    grad_gain = jnp.sum(grad_gains, axis=0).reshape(gains_pair.shape)
    parts = exchange(grad_normed_one, "dp")
    total_out = hidden + partial_out[0] + sum(wide(r) for r in partial_out[1:])
    produced = low(jnp.where(row_valid, total_out, 0.0))

    grad_normed_one = jnp.sum(wide(parts), axis=0)
    inputs = wide(token_rows)
    scale_one = rms_scale(inputs)
    unit_one = inputs * scale_one
    scaled_one = grad_normed_one * gain_rows[0:1]
    grad_inputs = grad_hidden + scale_one * (
        scaled_one - unit_one * jnp.mean(scaled_one * unit_one, axis=-1, keepdims=True)
    )


    def update_ff(grad, weight, moment, average, flip):
        outs = [(weight.shape, f32)] * 4 + [(weight.shape, bf16)]
        return kernel_call(
            functools.partial(update_body, step_rate, flip, weight.shape[0]),
            outs,
            [grad, weight, moment, average],
        )

    def settle(grads, *state):
        state = [jnp.transpose(v) for v in state]
        outs = kernel_call(
            functools.partial(settle_body, step_rate, len(grads)),
            [(v.shape, t) for v in state[::3] for t in (f32, f32, f32, f32, bf16)],
            [*grads, *state],
        )
        return [jnp.transpose(v) for v in outs]

    new_gate_up = update_ff(grad_ff[:2], gate_up, gate_up_mom, gate_up_avg, True)
    new_down = update(down_proj, wide(grad_ff[2]), down_proj_mom, down_proj_avg, step_rate)
    new_gains = update(gains_pair, grad_gain, gains_mom, gains_avg, step_rate)
    grad_cols, new_gate_up, new_down = tie(grad_cols, new_gate_up, new_down)
    new_cols = settle(
        grad_cols, in_proj, in_proj_mom, in_proj_avg, out_proj, out_proj_mom, out_proj_avg
    )
    return (
        produced.reshape(tokens.shape),
        grad_inputs.reshape(tokens.shape),
        *new_cols,
        *new_gate_up,
        *new_down,
        *new_gains,
    )


def solution(mesh):
    n_dp, n_fsdp = mesh.devices.shape
    fine = Mesh(mesh.devices.reshape(n_dp, n_fsdp // 2, 2), AXES)
    rows = P(AXES, None, None)
    last_of_two = P(None, AXES)
    first_of_two = P(AXES, None)
    last_of_three = P(None, None, AXES)
    weights = (last_of_two, last_of_two, last_of_three, first_of_two, last_of_two)
    in_specs = (rows, rows, P(AXES)) + weights * 3
    out_specs = (rows, rows) + tuple(spec for spec in weights for _ in range(5))
    return jax.shard_map(
        on_device, mesh=fine, in_specs=in_specs, out_specs=out_specs, check_vma=False
    )
```

time: 522 us -> 357 us (0.68)
  waiting for transfers between devices: 244 us -> 101 us
  Pallas kernels: 0 us -> 66.1 us
  other arithmetic: 75.5 us -> 24.8 us
  matrix products: 44.4 us -> 0 us
  starting transfers between devices: 89.6 us -> 100 us
    ppermute x75 -> x26, waiting for transfers between devices: 244 us -> 76.2 us  [send(): lax.ppermute(values, AXES, [(i, i ^ mask) for i in range(self.count)])]
    pallas_call x0 -> x14, Pallas kernels: none -> 66.1 us  [kernel_call(): pl.pallas_call(fetched, out_shape=[jax.ShapeDtypeStruct(s, t) for s, t in...]
    dot_general x22 -> x0, matrix products: 42.7 us -> none  [the longest x7 14.5 us: mm(): return jnp.dot(a, b, preferred_element_type=jnp.float32)]
    all_to_all x0 -> x6, starting transfers between devices: none -> 36.4 us  [exchange(): return lax.all_to_all(values, axes, split_axis=0, concat_axis=0, tiled=True)]
    ppermute x75 -> x26, starting transfers between devices: 89.5 us -> 63.3 us  [send(): lax.ppermute(values, AXES, [(i, i ^ mask) for i in range(self.count)])]
    all_to_all x0 -> x6, waiting for transfers between devices: none -> 24.8 us  [exchange(): return lax.all_to_all(values, axes, split_axis=0, concat_axis=0, tiled=True)]
    another operation x29 -> x3, other arithmetic: 29.8 us -> 5.65 us  [the longest x1 3.56 us: on_device(): out_own = jnp.stack(out_own).reshape(n_dp * n_z, out_width, D)]
    unnamed x165 -> x147, local copies, waits for them, and re-layouts: 15.7 us -> 39.6 us
  transfers between devices with their start and end apart: 76 -> 36, of which waited for: 34 -> 13; matrix products, arithmetic and copies ran while one was open for 22% -> 8% of each run, Pallas kernels for 0% -> 18%
where the time goes in v2:
time: 357 us; the launch traced here: 351 us
  waiting for transfers between devices  101 us (28%)
  starting transfers between devices  100 us (28%)
  Pallas kernels  66.1 us (19%)
  local copies, waits for them, and re-layouts  45 us (13%)
  other arithmetic  24.8 us (7%)
  between operations  14.5 us (4%)
    ppermute x26, waiting for transfers between devices, send(): lax.ppermute(values, AXES, [(i, i ^ mask) for i in range(self.count)])  76.2 us
    pallas_call x14, Pallas kernels, kernel_call(): pl.pallas_call(fetched, out_shape=[jax.ShapeDtypeStruct(s, t) for s, t in...  66.1 us
    ppermute x26, starting transfers between devices, send(): lax.ppermute(values, AXES, [(i, i ^ mask) for i in range(self.count)])  63.3 us
    unnamed x147, local copies, waits for them, and re-layouts  39.6 us
    all_to_all x6, starting transfers between devices, exchange(): return lax.all_to_all(values, axes, split_axis=0, concat_axis=0, tiled=True)  36.4 us
    all_to_all x6, waiting for transfers between devices, exchange(): return lax.all_to_all(values, axes, split_axis=0, concat_axis=0, tiled=True)  24.8 us
  transfers between devices with their start and end apart: 36, of which 13 were waited for; matrix products, arithmetic and copies ran while one was open for 8% of the time, Pallas kernels for 18%

profile of v2, /device:TPU:0, one launch (start us, length us, event | category | flops | bytes accessed | tf_op | source)
XLA Modules:
  0.0 351.4 jit_solution(14165265268616662669)
XLA Ops:
  9.1 2.3 tile.41
  11.3 5.3 %all-to-all-start = ((bf16[4,128,1536]{2,1,0:T(8,128)(2,1)}), bf16[4,128,1536]{2,1,0:T(8,128)(2,1)S(1)}, u32[]{:S(2)}, u32[]{:S(2)}) async-start(bf16[4,128,1536]{2,1,0:T(8,128)(2,1)} %tile.41), calls=%async_computation | async-start | bytes 3145728 | tf_op jit(solution)/shard_map/all_to_all | solution.py:439
  18.9 2.6 collective-permute-start.1
  23.3 2.0 broadcast_select_fusion
  26.6 14.2 %collective-permute-done.1 = bf16[48,1536]{1,0:T(8,128)(2,1)} collective-permute-done((bf16[48,1536]{1,0:T(8,128)(2,1)}, bf16[48,1536]{1,0:T(8,128)(2,1)}, u32[]{:S(2)}, u32[]{:S(2)}) %collective-permute-start.1) | collective-permute-done | bytes 147488 | tf_op jit(solution)/shard_map/ppermute | solution.py:425
  42.8 2.9 collective-permute-start.3
  47.9 12.2 %all-to-all-start.1 = ((bf16[32,1,96]{2,1,0:T(2,128)(2,1)}), bf16[32,1,96]{2,1,0:T(2,128)(2,1)S(1)}, u32[]{:S(2)}, u32[]{:S(2)}) async-start(bf16[32,1,96]{2,1,0:T(2,128)(2,1)} %copy.48), calls=%async_computation.1 | async-start | bytes 32768 | tf_op jit(solution)/shard_map/all_to_all | solution.py:439
  64.6 2.5 all-to-all-done.1
  67.2 3.6 %pad_maximum_fusion = bf16[4,4,48,1536]{3,2,1,0:T(8,128)(2,1)} fusion(bf16[1,4,48,1536]{3,2,1,0:T(8,128)(2,1)} %bitcast.15, bf16[1,4,48,1536]{3,2,1,0:T(8,128)(2,1)} %bitcast.14, bf16[1,4,48,1536]{3,2,1,0:T(8,128)(2,1)} %bitcast.13, bf16[1,4,48,1536]{3,2,1,0:T(8,128)(2,1)} %bitcast.12), kind=kLoop, calls=%fused_computation.1 | loop fusion | flops 3538944 | bytes 4718592 | tf_op jit(solution)/shard_map/stack | solution.py:526
  70.8 4.3 %shard_map.386 = (bf16[4,128,768]{2,1,0:T(8,128)(2,1)S(1)}, bf16[4,128,1536]{2,1,0:T(8,128)(2,1)S(1)}, f32[2,1536]{1,0:T(2,128)S(1)}) custom-call(bf16[4,128,1536]{2,1,0:T(8,128)(2,1)S(1)} %all-to-all-done.refs_0_.refs_2_, bf16[768,1536]{1,0:T(8,128)(2,1)S(1)} %copy-done.4, bf16[32,96]{1,0:T(8,128)(2,1)S(1)} %bitcast.73, f32[128,768]{1,0:T(8,128)S(1)} %copy-done.27, ...), custom_call_target="tpu_custom_call" | custom-call | tf_op jit(solution)/shard_map/pallas_call | solution.py:97
  77.2 3.6 %all-to-all-start.2 = ((bf16[4,128,768]{2,1,0:T(8,128)(2,1)}), bf16[4,128,768]{2,1,0:T(8,128)(2,1)S(1)}, u32[]{:S(2)}, u32[]{:S(2)}) async-start(bf16[4,128,768]{2,1,0:T(8,128)(2,1)} %copy-done.34), calls=%async_computation.2 | async-start | bytes 1572864 | tf_op jit(solution)/shard_map/all_to_all | solution.py:439
  80.9 9.2 %collective-permute-start.6 = (bf16[128,1536]{1,0:T(8,128)(2,1)S(1)}, bf16[128,1536]{1,0:T(8,128)(2,1)S(1)}, u32[]{:S(2)}, u32[]{:S(2)}) collective-permute-start(bf16[128,1536]{1,0:T(8,128)(2,1)S(1)} %copy-done.14), channel_id=1, source_target_pairs={{0,2},{1,3},{2,0},{3,1},{4,6},{5,7},{6,4},{7,5},{8,10},{9,11},{10,... | collective-permute-start | bytes 1179656 | tf_op jit(solution)/shard_map/ppermute | solution.py:425
  93.4 6.4 %all-to-all-done.2.refs_1_.refs_2_ = bf16[4,128,768]{2,1,0:T(8,128)(2,1)S(1)} async-done(((bf16[4,128,768]{2,1,0:T(8,128)(2,1)}), bf16[4,128,768]{2,1,0:T(8,128)(2,1)S(1)}, u32[]{:S(2)}, u32[]{:S(2)}) %all-to-all-start.2) | async-done | bytes 786464 | tf_op jit(solution)/shard_map/all_to_all | solution.py:439
  99.9 3.5 shard_map.387
  104.4 3.8 %collective-permute-done.6.refs_1_ = bf16[128,1536]{1,0:T(8,128)(2,1)S(1)} collective-permute-done((bf16[128,1536]{1,0:T(8,128)(2,1)S(1)}, bf16[128,1536]{1,0:T(8,128)(2,1)S(1)}, u32[]{:S(2)}, u32[]{:S(2)}) %collective-permute-start.6) | collective-permute-done | bytes 393248 | tf_op jit(solution)/shard_map/ppermute | solution.py:425
  108.2 11.8 %collective-permute-done.8.refs_3_ = bf16[128,1536]{1,0:T(8,128)(2,1)} collective-permute-done((bf16[128,1536]{1,0:T(8,128)(2,1)S(1)}, bf16[128,1536]{1,0:T(8,128)(2,1)}, u32[]{:S(2)}, u32[]{:S(2)}) %collective-permute-start.8) | collective-permute-done | bytes 393248 | tf_op jit(solution)/shard_map/ppermute | solution.py:425
  120.3 6.6 %shard_map.388 = (f32[128,1536]{1,0:T(8,128)S(1)}, bf16[128,1536]{1,0:T(8,128)(2,1)}, bf16[32,48,1536]{2,1,0:T(8,128)(2,1)S(1)}) custom-call(s32[3]{0:T(128)S(1)} %pad_add_fusion.refs_0_, bf16[128,1536]{1,0:T(8,128)(2,1)} %get-tuple-element.166.refs_1_, bf16[128,1536]{1,0:T(8,128)(2,1)S(1)} %bitcast.64, f32[2,1536]{1,0:T(2,128)S(1)} %get-tuple-element.167.refs_3_.refs_6_, ...), custom_call_target="tpu_custom_call" | custom-call | tf_op jit(solution)/shard_map/pallas_call | solution.py:97
  126.9 2.2 copy-done.9
  129.9 8.1 %collective-permute-start.10 = (bf16[128,1536]{1,0:T(8,128)(2,1)}, bf16[128,1536]{1,0:T(8,128)(2,1)}, u32[]{:S(2)}, u32[]{:S(2)}) collective-permute-start(bf16[128,1536]{1,0:T(8,128)(2,1)} %get-tuple-element.180.refs_0_), channel_id=1, source_target_pairs={{0,2},{1,3},{2,0},{3,1},{4,6},{5,7},{6,4},{7,5},{8,10},{9,11},{10,... | collective-permute-start | bytes 1179656 | tf_op jit(solution)/shard_map/ppermute | solution.py:425
  141.5 3.7 %copy-done = bf16[3,1024,1536]{2,1,0:T(8,128)(2,1)S(1)} copy-done((bf16[3,1024,1536]{2,1,0:T(8,128)(2,1)S(1)}, bf16[3,1024,1536]{2,1,0:T(8,128)(2,1)}, u32[]{:S(2)}) %copy-start) | copy-done | bytes 9437208
  145.2 6.0 %shard_map.389 = (bf16[512,1536]{1,0:T(8,128)(2,1)S(1)}, f32[512,1024]{1,0:T(8,128)S(1)}) custom-call(bf16[128,1536]{1,0:T(8,128)(2,1)S(1)} %copy-done.14, bf16[128,1536]{1,0:T(8,128)(2,1)S(1)} %collective-permute-done.6.refs_1_, bf16[128,1536]{1,0:T(8,128)(2,1)} %collective-permute-done.7.refs_2_, bf16[128,1536]{1,0:T(8,128)(2,1)} %collective-permute-done.8.refs_3_, ...), custom_call_target="tpu_custom_call" | custom-call | tf_op jit(solution)/shard_map/pallas_call | solution.py:97
  151.2 3.7 %collective-permute-done.10.refs_1_ = bf16[128,1536]{1,0:T(8,128)(2,1)} collective-permute-done((bf16[128,1536]{1,0:T(8,128)(2,1)}, bf16[128,1536]{1,0:T(8,128)(2,1)}, u32[]{:S(2)}, u32[]{:S(2)}) %collective-permute-start.10) | collective-permute-done | bytes 393248 | tf_op jit(solution)/shard_map/ppermute | solution.py:425
  154.9 13.2 %collective-permute-done.11.refs_2_ = bf16[128,1536]{1,0:T(8,128)(2,1)} collective-permute-done((bf16[128,1536]{1,0:T(8,128)(2,1)}, bf16[128,1536]{1,0:T(8,128)(2,1)}, u32[]{:S(2)}, u32[]{:S(2)}) %collective-permute-start.11) | collective-permute-done | bytes 393248 | tf_op jit(solution)/shard_map/ppermute | solution.py:425
  168.1 9.8 %shard_map.390 = (bf16[512,1536]{1,0:T(8,128)(2,1)S(1)}, bf16[512,1024]{1,0:T(8,128)(2,1)S(1)}, bf16[512,1024]{1,0:T(8,128)(2,1)S(1)}, bf16[512,1024]{1,0:T(8,12...) custom-call(bf16[128,1536]{1,0:T(8,128)(2,1)} %get-tuple-element.180, ...), custom_call_target="tpu_custom_call" | custom-call | tf_op jit(solution)/shard_map/pallas_call | solution.py:97
  178.8 7.2 %collective-permute-start.13 = (bf16[128,1536]{1,0:T(8,128)(2,1)S(1)}, bf16[128,1536]{1,0:T(8,128)(2,1)S(1)}, u32[]{:S(2)}, u32[]{:S(2)}) collective-permute-start(bf16[128,1536]{1,0:T(8,128)(2,1)S(1)} %get-tuple-element.196), channel_id=1, source_target_pairs={{0,2},{1,3},{2,0},{3,1},{4,6},{5,7},{6,4},{7,5},{8,10},{9,11},{10,... | collective-permute-start | bytes 1179656 | tf_op jit(solution)/shard_map/ppermute | solution.py:425
  189.3 7.6 %shard_map.391 = (bf16[3,1024,1536]{2,1,0:T(8,128)(2,1)S(1)}, f32[128,1536]{1,0:T(8,128)S(1)}, bf16[128,1536]{1,0:T(8,128)(2,1)S(1)}, bf16[128,1536]{1,0:T(8,128)(2,1)S(1)}, bf16[128,1536]{1,0:T(8,128)(2,1)S(1)}) custom-call(bf16[512,1024]{1,0:T(8,128)(2,1)S(1)} %get-tuple-element.185.refs_0_, bf16[512,1024]{1,0:T(8,128)(2,1)S(1)} %get-tuple-element.186.refs_1_, ...), custom_call_target="tpu_custom_call" | custom-call | tf_op jit(solution)/shard_map/pallas_call | solution.py:97
  196.9 3.7 %copy-done.3 = bf16[3,1024,1536]{2,1,0:T(8,128)(2,1)} copy-done((bf16[3,1024,1536]{2,1,0:T(8,128)(2,1)}, bf16[3,1024,1536]{2,1,0:T(8,128)(2,1)S(1)}, u32[]{:S(2)}) %copy-start.3) | copy-done | bytes 9437208
  203.0 12.7 %collective-permute-done.14.refs_3_ = bf16[128,1536]{1,0:T(8,128)(2,1)S(1)} collective-permute-done((bf16[128,1536]{1,0:T(8,128)(2,1)S(1)}, bf16[128,1536]{1,0:T(8,128)(2,1)S(1)}, u32[]{:S(2)}, u32[]{:S(2)}) %collective-permute-start.14) | collective-permute-done | bytes 393248 | tf_op jit(solution)/shard_map/ppermute | solution.py:425
  217.3 7.6 %collective-permute-start.16 = (bf16[128,1536]{1,0:T(8,128)(2,1)}, bf16[128,1536]{1,0:T(8,128)(2,1)}, u32[]{:S(2)}, u32[]{:S(2)}) collective-permute-start(bf16[128,1536]{1,0:T(8,128)(2,1)} %copy-done.57), channel_id=1, source_target_pairs={{0,6},{1,7},{2,4},{3,5},{4,2},{5,3},{6,0},{7,1},{8,14},{9,15},{10,... | collective-permute-start | bytes 1179656 | tf_op jit(solution)/shard_map/ppermute | solution.py:425
  229.2 3.2 shard_map.392
  235.1 3.4 copy-done.10
  238.4 5.9 %shard_map.393 = bf16[4,128,768]{2,1,0:T(8,128)(2,1)} custom-call(bf16[128,1536]{1,0:T(8,128)(2,1)S(1)} %get-tuple-element.203.refs_0_, bf16[1536,1536]{1,0:T(8,128)(2,1)S(1)} %bitcast.65, bf16[4,128,768]{2,1,0:T(8,128)(2,1)S(1)} %all-to-all-done.2.refs_1_.refs_2_, f32[8,256,128]{2,1,0:T(8,128)S(1)} %copy-done.33, f32[128,768]{1,0:T(8,128)S(1)} %copy-done.12, ...), custom_call_target="tpu_custom_call" | custom-call | tf_op jit(solution)/shard_map/pallas_call | solution.py:97
  244.4 3.9 %all-to-all-start.3 = ((bf16[4,128,768]{2,1,0:T(8,128)(2,1)}), bf16[4,128,768]{2,1,0:T(8,128)(2,1)S(1)}, u32[]{:S(2)}, u32[]{:S(2)}) async-start(bf16[4,128,768]{2,1,0:T(8,128)(2,1)} %shard_map.393), calls=%async_computation.3 | async-start | bytes 1572864 | tf_op jit(solution)/shard_map/all_to_all | solution.py:439
  248.3 4.3 %collective-permute-start.17 = (bf16[128,1536]{1,0:T(8,128)(2,1)}, bf16[128,1536]{1,0:T(8,128)(2,1)S(1)}, u32[]{:S(2)}, u32[]{:S(2)}) collective-permute-start(bf16[128,1536]{1,0:T(8,128)(2,1)} %copy-done.56), channel_id=1, source_target_pairs={{0,2},{1,3},{2,0},{3,1},{4,6},{5,7},{6,4},{7,5},{8,10},{9,11},{10,... | collective-permute-start | bytes 1179656 | tf_op jit(solution)/shard_map/ppermute | solution.py:425
  256.2 11.4 %collective-permute-done.19.refs_5_ = bf16[128,384]{1,0:T(8,128)(2,1)S(1)} collective-permute-done((bf16[128,384]{1,0:T(8,128)(2,1)}, bf16[128,384]{1,0:T(8,128)(2,1)S(1)}, u32[]{:S(2)}, u32[]{:S(2)}) %collective-permute-start.19) | collective-permute-done | bytes 98336 | tf_op jit(solution)/shard_map/ppermute | solution.py:425
  267.6 4.1 %collective-permute-done.21.refs_7_ = bf16[128,384]{1,0:T(8,128)(2,1)S(1)} collective-permute-done((bf16[128,384]{1,0:T(8,128)(2,1)}, bf16[128,384]{1,0:T(8,128)(2,1)S(1)}, u32[]{:S(2)}, u32[]{:S(2)}) %collective-permute-start.21) | collective-permute-done | bytes 98336 | tf_op jit(solution)/shard_map/ppermute | solution.py:425
  275.5 5.0 %shard_map.394 = (f32[4,144,1536]{2,1,0:T(8,128)S(1)}, bf16[4,144,1536]{2,1,0:T(8,128)(2,1)}) custom-call(s32[3]{0:T(128)S(1)} %pad_add_fusion.refs_0_, bf16[4,128,768]{2,1,0:T(8,128)(2,1)S(1)} %all-to-all-done.3.refs_1_.refs_0_, bf16[4,128,1536]{2,1,0:T(8,128)(2,1)S(1)} %copy-done.24, bf16[4,128,1536]{2,1,0:T(8,128)(2,1)S(1)} %bitcast.67, ...), custom_call_target="tpu_custom_call" | custom-call | tf_op jit(solution)/shard_map/pallas_call | solution.py:97
  280.6 3.0 shard_map.395
  284.5 6.9 %all-to-all-start.4 = ((f32[32,1,96]{2,1,0:T(1,128)}), f32[32,1,96]{2,1,0:T(1,128)S(1)}, u32[]{:S(2)}, u32[]{:S(2)}) async-start(f32[32,1,96]{2,1,0:T(1,128)} %bitcast.21), calls=%async_computation.4 | async-start | bytes 32768 | tf_op jit(solution)/shard_map/all_to_all | solution.py:439
  291.5 2.2 copy-done.16
  293.7 3.0 shard_map.396
  298.4 4.5 %all-to-all-start.5 = ((bf16[4,128,1536]{2,1,0:T(8,128)(2,1)}), bf16[4,128,1536]{2,1,0:T(8,128)(2,1)}, u32[]{:S(2)}, u32[]{:S(2)}) async-start(bf16[4,128,1536]{2,1,0:T(8,128)(2,1)} %get-tuple-element.237), calls=%async_computation.5 | async-start | bytes 3145728 | tf_op jit(solution)/shard_map/all_to_all | solution.py:439
  303.1 2.2 select_convert_fusion
  310.9 14.2 %all-to-all-done.5 = bf16[4,128,1536]{2,1,0:T(8,128)(2,1)} async-done(((bf16[4,128,1536]{2,1,0:T(8,128)(2,1)}), bf16[4,128,1536]{2,1,0:T(8,128)(2,1)}, u32[]{:S(2)}, u32[]{:S(2)}) %all-to-all-start.5) | async-done | bytes 1572896 | tf_op jit(solution)/shard_map/all_to_all | solution.py:439
  328.1 2.4 multiply_add_fusion.2
  330.5 2.6 fusion.13
  335.6 3.9 %shard_map.397 = (f32[2,1536,128]{2,1,0:T(8,128)}, f32[2,1536,128]{2,1,0:T(8,128)}, f32[2,1536,128]{2,1,0:T(8,128)}, f32[2,1536,128]{2,1,0:T(8,128)}, bf16[2,1536,128]{2,1,0:T(8,128)(2,1)}) custom-call(bf16[2,128,1536]{2,1,0:T(8,128)(2,1)S(1)} %slice.12.refs_0_, f32[2,1536,128]{2,1,0:T(8,128)S(1)} %copy-done.7, f32[2,1536,128]{2,1,0:T(8,128)S(1)} %copy-done.28, ...), custom_call_target="tpu_custom_call" | custom-call | tf_op jit(solution)/shard_map/pallas_call | solution.py:97
  341.1 3.8 %shard_map.398 = (f32[96,1536]{1,0:T(8,128)}, f32[96,1536]{1,0:T(8,128)}, f32[96,1536]{1,0:T(8,128)}, f32[96,1536]{1,0:T(8,128)}, bf16[96,1536]{1,0:T(8,128)(2,1...) custom-call(f32[144,1536]{1,0:T(8,128)S(1)} %get-tuple-element.248.r, ...), custom_call_target="tpu_custom_call" | custom-call | tf_op jit(solution)/shard_map/pallas_call | solution.py:97
  (233 shorter events, 64.9 us)
Async XLA Ops:
  7.2 60.0 %all-gather.5.cloned.1.call-start = ((), (), s32[]{:S(2)}) async-start(), calls=%async_computation.7 | async-start | bytes 2654208 | tf_op jit(solution)/shard_map/all_gather | solution.py:488
  11.3 29.4 %all-to-all-start = ((bf16[4,128,1536]{2,1,0:T(8,128)(2,1)}), bf16[4,128,1536]{2,1,0:T(8,128)(2,1)S(1)}, u32[]{:S(2)}, u32[]{:S(2)}) async-start(bf16[4,128,1536]{2,1,0:T(8,128)(2,1)} %tile.41), calls=%async_computation | async-start | bytes 3145728 | tf_op jit(solution)/shard_map/all_to_all | solution.py:439
  17.3 9.2 %collective-permute-start = (bf16[48,1536]{1,0:T(8,128)(2,1)}, bf16[48,1536]{1,0:T(8,128)(2,1)}, u32[]{:S(2)}, u32[]{:S(2)}) collective-permute-start(bf16[48,1536]{1,0:T(8,128)(2,1)} %bitcast_convert_fusion.1), channel_id=1, source_target_pairs={{0,2},{1,3},{2,0},{3,1},{4,6},{5,7},{6,4},{7,5},{8,10},{9,11},{10,... | collective-permute-start | bytes 442376 | tf_op jit(solution)/shard_map/ppermute | solution.py:425
  18.9 21.9 %collective-permute-start.1 = (bf16[48,1536]{1,0:T(8,128)(2,1)}, bf16[48,1536]{1,0:T(8,128)(2,1)}, u32[]{:S(2)}, u32[]{:S(2)}) collective-permute-start(bf16[48,1536]{1,0:T(8,128)(2,1)} %bitcast_convert_fusion.1), channel_id=1, source_target_pairs={{0,4},{1,5},{2,6},{3,7},{4,0},{5,1},{6,2},{7,3},{8,12},{9,13},{10,... | collective-permute-start | bytes 442376 | tf_op jit(solution)/shard_map/ppermute | solution.py:425
  21.5 19.3 %collective-permute-start.2 = (bf16[48,1536]{1,0:T(8,128)(2,1)}, bf16[48,1536]{1,0:T(8,128)(2,1)}, u32[]{:S(2)}, u32[]{:S(2)}) collective-permute-start(bf16[48,1536]{1,0:T(8,128)(2,1)} %bitcast_convert_fusion.1), channel_id=1, source_target_pairs={{0,6},{1,7},{2,4},{3,5},{4,2},{5,3},{6,0},{7,1},{8,14},{9,15},{10,... | collective-permute-start | bytes 442376 | tf_op jit(solution)/shard_map/ppermute | solution.py:425
  22.2 20.6 %copy-start.11 = (f32[128,768]{1,0:T(8,128)}, f32[128,768]{1,0:T(8,128)S(1)}, u32[]{:S(2)}) copy-start(f32[128,768]{1,0:T(8,128)S(1)} %tile.37.refs_4_) | copy-start | bytes 1179652
  23.2 23.9 %copy-start.53 = (s32[2]{0:T(128)S(1)}, s32[2]{0:T(128)}, u32[]{:S(2)}) copy-start(s32[2]{0:T(128)} %refs_0_.3) | copy-start | bytes 28
  23.3 38.6 %copy-start.6 = (f32[2,1536,128]{2,1,0:T(8,128)S(1)}, f32[2,1536,128]{2,1,0:T(8,128)}, u32[]{:S(2)}) copy-start(f32[2,1536,128]{2,1,0:T(8,128)} %refs_1_.3) | copy-start | bytes 4718596
  42.8 24.4 %collective-permute-start.3 = (bf16[4,48,1536]{2,1,0:T(8,128)(2,1)}, bf16[4,48,1536]{2,1,0:T(8,128)(2,1)}, u32[]{:S(2)}, u32[]{:S(2)}) collective-permute-start(bf16[4,48,1536]{2,1,0:T(8,128)(2,1)} %pad_maximum_fusion.1), channel_id=1, source_target_pairs={{0,8},{1,9},{2,10},{3,11},{4,12},{5,13},{6,14},{7,15},{8,0},{9,1},... | collective-permute-start | bytes 1769480 | tf_op jit(solution)/shard_map/ppermute | solution.py:425
  45.6 21.5 %collective-permute-start.4 = (bf16[4,48,1536]{2,1,0:T(8,128)(2,1)}, bf16[4,48,1536]{2,1,0:T(8,128)(2,1)}, u32[]{:S(2)}, u32[]{:S(2)}) collective-permute-start(bf16[4,48,1536]{2,1,0:T(8,128)(2,1)} %pad_maximum_fusion.1), channel_id=1, source_target_pairs={{0,16},{1,17},{2,18},{3,19},{4,20},{5,21},{6,22},{7,23},{8,24},{9,... | collective-permute-start | bytes 1769480 | tf_op jit(solution)/shard_map/ppermute | solution.py:425
  47.1 20.1 %collective-permute-start.5 = (bf16[4,48,1536]{2,1,0:T(8,128)(2,1)}, bf16[4,48,1536]{2,1,0:T(8,128)(2,1)}, u32[]{:S(2)}, u32[]{:S(2)}) collective-permute-start(bf16[4,48,1536]{2,1,0:T(8,128)(2,1)} %pad_maximum_fusion.1), channel_id=1, source_target_pairs={{0,24},{1,25},{2,26},{3,27},{4,28},{5,29},{6,30},{7,31},{8,16},{9,... | collective-permute-start | bytes 1769480 | tf_op jit(solution)/shard_map/ppermute | solution.py:425
  47.3 16.3 %copy-start.66 = (pred[128]{0:T(512)(128)(4,1)}, pred[128]{0:T(512)(128)(4,1)S(1)}, u32[]{:S(2)}) copy-start(pred[128]{0:T(512)(128)(4,1)S(1)} %lt.33) | copy-start | bytes 388
  47.9 19.2 %all-to-all-start.1 = ((bf16[32,1,96]{2,1,0:T(2,128)(2,1)}), bf16[32,1,96]{2,1,0:T(2,128)(2,1)S(1)}, u32[]{:S(2)}, u32[]{:S(2)}) async-start(bf16[32,1,96]{2,1,0:T(2,128)(2,1)} %copy.48), calls=%async_computation.1 | async-start | bytes 32768 | tf_op jit(solution)/shard_map/all_to_all | solution.py:439
  60.1 81.4 %all-gather.7.cloned.1.call-start = ((), (), s32[]{:S(2)}) async-start(), calls=%async_computation.8 | async-start | bytes 10616832 | tf_op jit(solution)/shard_map/all_gather | solution.py:513
  70.8 49.5 %collective-permute-start.9 = (bf16[16,48,1536]{2,1,0:T(8,128)(2,1)}, bf16[16,48,1536]{2,1,0:T(8,128)(2,1)}, u32[]{:S(2)}, u32[]{:S(2)}) collective-permute-start(bf16[16,48,1536]{2,1,0:T(8,128)(2,1)} %bitcast.16.refs_4_), channel_id=1, source_target_pairs={{0,1},{1,0},{2,3},{3,2},{4,5},{5,4},{6,7},{7,6},{8,9},{9,8},{10,11... | collective-permute-start | bytes 7077896 | tf_op jit(solution)/shard_map/ppermute | solution.py:425
  77.2 43.1 %copy-start.2 = (bf16[2,64,1536]{2,1,0:T(8,128)(2,1)S(1)}, bf16[2,64,1536]{2,1,0:T(8,128)(2,1)}, u32[]{:S(2)}) copy-start(bf16[2,64,1536]{2,1,0:T(8,128)(2,1)} %param.18) | copy-start | bytes 1179652
  77.2 22.7 %all-to-all-start.2 = ((bf16[4,128,768]{2,1,0:T(8,128)(2,1)}), bf16[4,128,768]{2,1,0:T(8,128)(2,1)S(1)}, u32[]{:S(2)}, u32[]{:S(2)}) async-start(bf16[4,128,768]{2,1,0:T(8,128)(2,1)} %copy-done.34), calls=%async_computation.2 | async-start | bytes 1572864 | tf_op jit(solution)/shard_map/all_to_all | solution.py:439
  80.8 191.6 %all-gather.9.cloned.1.call-start = ((), (), s32[]{:S(2)}) async-start(), calls=%async_computation.10 | async-start | bytes 1966080 | tf_op jit(solution)/shard_map/all_gather | solution.py:560
  80.9 27.3 %collective-permute-start.6 = (bf16[128,1536]{1,0:T(8,128)(2,1)S(1)}, bf16[128,1536]{1,0:T(8,128)(2,1)S(1)}, u32[]{:S(2)}, u32[]{:S(2)}) collective-permute-start(bf16[128,1536]{1,0:T(8,128)(2,1)S(1)} %copy-done.14), channel_id=1, source_target_pairs={{0,2},{1,3},{2,0},{3,1},{4,6},{5,7},{6,4},{7,5},{8,10},{9,11},{10,... | collective-permute-start | bytes 1179656 | tf_op jit(solution)/shard_map/ppermute | solution.py:425
  90.0 18.1 %collective-permute-start.7 = (bf16[128,1536]{1,0:T(8,128)(2,1)S(1)}, bf16[128,1536]{1,0:T(8,128)(2,1)}, u32[]{:S(2)}, u32[]{:S(2)}) collective-permute-start(bf16[128,1536]{1,0:T(8,128)(2,1)S(1)} %copy-done.14), channel_id=1, source_target_pairs={{0,4},{1,5},{2,6},{3,7},{4,0},{5,1},{6,2},{7,3},{8,12},{9,13},{10,... | collective-permute-start | bytes 1179656 | tf_op jit(solution)/shard_map/ppermute | solution.py:425
  92.1 27.9 %collective-permute-start.8 = (bf16[128,1536]{1,0:T(8,128)(2,1)S(1)}, bf16[128,1536]{1,0:T(8,128)(2,1)}, u32[]{:S(2)}, u32[]{:S(2)}) collective-permute-start(bf16[128,1536]{1,0:T(8,128)(2,1)S(1)} %copy-done.14), channel_id=1, source_target_pairs={{0,6},{1,7},{2,4},{3,5},{4,2},{5,3},{6,0},{7,1},{8,14},{9,15},{10,... | collective-permute-start | bytes 1179656 | tf_op jit(solution)/shard_map/ppermute | solution.py:425
  120.0 210.5 %reduce-scatter.2.cloned.1.call-start = ((), (), s32[]{:S(2)}) async-start(), calls=%async_computation.9 | async-start | bytes 10616832 | tf_op jit(solution)/shard_map/reduce_scatter | solution.py:592
  129.9 25.0 %collective-permute-start.10 = (bf16[128,1536]{1,0:T(8,128)(2,1)}, bf16[128,1536]{1,0:T(8,128)(2,1)}, u32[]{:S(2)}, u32[]{:S(2)}) collective-permute-start(bf16[128,1536]{1,0:T(8,128)(2,1)} %get-tuple-element.180.refs_0_), channel_id=1, source_target_pairs={{0,2},{1,3},{2,0},{3,1},{4,6},{5,7},{6,4},{7,5},{8,10},{9,11},{10,... | collective-permute-start | bytes 1179656 | tf_op jit(solution)/shard_map/ppermute | solution.py:425
  138.0 30.1 %collective-permute-start.11 = (bf16[128,1536]{1,0:T(8,128)(2,1)}, bf16[128,1536]{1,0:T(8,128)(2,1)}, u32[]{:S(2)}, u32[]{:S(2)}) collective-permute-start(bf16[128,1536]{1,0:T(8,128)(2,1)} %get-tuple-element.180.refs_0_), channel_id=1, source_target_pairs={{0,4},{1,5},{2,6},{3,7},{4,0},{5,1},{6,2},{7,3},{8,12},{9,13},{10,... | collective-permute-start | bytes 1179656 | tf_op jit(solution)/shard_map/ppermute | solution.py:425
  140.0 28.1 %collective-permute-start.12 = (bf16[128,1536]{1,0:T(8,128)(2,1)}, bf16[128,1536]{1,0:T(8,128)(2,1)}, u32[]{:S(2)}, u32[]{:S(2)}) collective-permute-start(bf16[128,1536]{1,0:T(8,128)(2,1)} %get-tuple-element.180.refs_0_), channel_id=1, source_target_pairs={{0,6},{1,7},{2,4},{3,5},{4,2},{5,3},{6,0},{7,1},{8,14},{9,15},{10,... | collective-permute-start | bytes 1179656 | tf_op jit(solution)/shard_map/ppermute | solution.py:425
  145.2 22.9 %copy-start.1 = (bf16[3,1024,1536]{2,1,0:T(8,128)(2,1)S(1)}, bf16[3,1024,1536]{2,1,0:T(8,128)(2,1)}, u32[]{:S(2)}) copy-start(bf16[3,1024,1536]{2,1,0:T(8,128)(2,1)} %all-gather.7.cloned.1.call-done.refs_4_.refs_5_) | copy-start | bytes 28311556
  178.8 24.2 %collective-permute-start.13 = (bf16[128,1536]{1,0:T(8,128)(2,1)S(1)}, bf16[128,1536]{1,0:T(8,128)(2,1)S(1)}, u32[]{:S(2)}, u32[]{:S(2)}) collective-permute-start(bf16[128,1536]{1,0:T(8,128)(2,1)S(1)} %get-tuple-element.196), channel_id=1, source_target_pairs={{0,2},{1,3},{2,0},{3,1},{4,6},{5,7},{6,4},{7,5},{8,10},{9,11},{10,... | collective-permute-start | bytes 1179656 | tf_op jit(solution)/shard_map/ppermute | solution.py:425
  185.9 29.8 %collective-permute-start.14 = (bf16[128,1536]{1,0:T(8,128)(2,1)S(1)}, bf16[128,1536]{1,0:T(8,128)(2,1)S(1)}, u32[]{:S(2)}, u32[]{:S(2)}) collective-permute-start(bf16[128,1536]{1,0:T(8,128)(2,1)S(1)} %get-tuple-element.197), channel_id=1, source_target_pairs={{0,4},{1,5},{2,6},{3,7},{4,0},{5,1},{6,2},{7,3},{8,12},{9,13},{10,... | collective-permute-start | bytes 1179656 | tf_op jit(solution)/shard_map/ppermute | solution.py:425
  187.8 28.7 %collective-permute-start.15 = (bf16[128,1536]{1,0:T(8,128)(2,1)S(1)}, bf16[128,1536]{1,0:T(8,128)(2,1)S(1)}, u32[]{:S(2)}, u32[]{:S(2)}) collective-permute-start(bf16[128,1536]{1,0:T(8,128)(2,1)S(1)} %get-tuple-element.198), channel_id=1, source_target_pairs={{0,6},{1,7},{2,4},{3,5},{4,2},{5,3},{6,0},{7,1},{8,14},{9,15},{10,... | collective-permute-start | bytes 1179656 | tf_op jit(solution)/shard_map/ppermute | solution.py:425
  203.0 13.5 %copy-start.56 = (bf16[128,1536]{1,0:T(8,128)(2,1)}, bf16[128,1536]{1,0:T(8,128)(2,1)S(1)}, u32[]{:S(2)}) copy-start(bf16[128,1536]{1,0:T(8,128)(2,1)S(1)} %get-tuple-element.211) | copy-start | bytes 1179652
  217.3 27.2 %collective-permute-start.16 = (bf16[128,1536]{1,0:T(8,128)(2,1)}, bf16[128,1536]{1,0:T(8,128)(2,1)}, u32[]{:S(2)}, u32[]{:S(2)}) collective-permute-start(bf16[128,1536]{1,0:T(8,128)(2,1)} %copy-done.57), channel_id=1, source_target_pairs={{0,6},{1,7},{2,4},{3,5},{4,2},{5,3},{6,0},{7,1},{8,14},{9,15},{10,... | collective-permute-start | bytes 1179656 | tf_op jit(solution)/shard_map/ppermute | solution.py:425
  244.4 8.3 %copy-start.55 = (bf16[128,1536]{1,0:T(8,128)(2,1)S(1)}, bf16[128,1536]{1,0:T(8,128)(2,1)}, u32[]{:S(2)}) copy-start(bf16[128,1536]{1,0:T(8,128)(2,1)} %copy-done.54) | copy-start | bytes 1179652
  244.4 28.0 %copy-start.50 = (bf16[128,384]{1,0:T(8,128)(2,1)S(1)}, bf16[128,384]{1,0:T(8,128)(2,1)}, u32[]{:S(2)}) copy-start(bf16[128,384]{1,0:T(8,128)(2,1)} %copy-done.49) | copy-start | bytes 294916
  244.4 28.0 %all-to-all-start.3 = ((bf16[4,128,768]{2,1,0:T(8,128)(2,1)}), bf16[4,128,768]{2,1,0:T(8,128)(2,1)S(1)}, u32[]{:S(2)}, u32[]{:S(2)}) async-start(bf16[4,128,768]{2,1,0:T(8,128)(2,1)} %shard_map.393), calls=%async_computation.3 | async-start | bytes 1572864 | tf_op jit(solution)/shard_map/all_to_all | solution.py:439
  248.3 23.3 %collective-permute-start.17 = (bf16[128,1536]{1,0:T(8,128)(2,1)}, bf16[128,1536]{1,0:T(8,128)(2,1)S(1)}, u32[]{:S(2)}, u32[]{:S(2)}) collective-permute-start(bf16[128,1536]{1,0:T(8,128)(2,1)} %copy-done.56), channel_id=1, source_target_pairs={{0,2},{1,3},{2,0},{3,1},{4,6},{5,7},{6,4},{7,5},{8,10},{9,11},{10,... | collective-permute-start | bytes 1179656 | tf_op jit(solution)/shard_map/ppermute | solution.py:425
  252.7 19.8 %collective-permute-start.18 = (bf16[128,1536]{1,0:T(8,128)(2,1)S(1)}, bf16[128,1536]{1,0:T(8,128)(2,1)}, u32[]{:S(2)}, u32[]{:S(2)}) collective-permute-start(bf16[128,1536]{1,0:T(8,128)(2,1)S(1)} %copy-done.55), channel_id=1, source_target_pairs={{0,4},{1,5},{2,6},{3,7},{4,0},{5,1},{6,2},{7,3},{8,12},{9,13},{10,... | collective-permute-start | bytes 1179656 | tf_op jit(solution)/shard_map/ppermute | solution.py:425
  252.7 14.9 %collective-permute-start.19 = (bf16[128,384]{1,0:T(8,128)(2,1)}, bf16[128,384]{1,0:T(8,128)(2,1)S(1)}, u32[]{:S(2)}, u32[]{:S(2)}) collective-permute-start(bf16[128,384]{1,0:T(8,128)(2,1)} %get-tuple-element.215), channel_id=1, source_target_pairs={{0,8},{1,9},{2,10},{3,11},{4,12},{5,13},{6,14},{7,15},{8,0},{9,1},... | collective-permute-start | bytes 294920 | tf_op jit(solution)/shard_map/ppermute | solution.py:425
  254.3 13.2 %collective-permute-start.20 = (bf16[128,384]{1,0:T(8,128)(2,1)}, bf16[128,384]{1,0:T(8,128)(2,1)S(1)}, u32[]{:S(2)}, u32[]{:S(2)}) collective-permute-start(bf16[128,384]{1,0:T(8,128)(2,1)} %get-tuple-element.216), channel_id=1, source_target_pairs={{0,16},{1,17},{2,18},{3,19},{4,20},{5,21},{6,22},{7,23},{8,24},{9,... | collective-permute-start | bytes 294920 | tf_op jit(solution)/shard_map/ppermute | solution.py:425
  255.8 15.9 %collective-permute-start.21 = (bf16[128,384]{1,0:T(8,128)(2,1)}, bf16[128,384]{1,0:T(8,128)(2,1)S(1)}, u32[]{:S(2)}, u32[]{:S(2)}) collective-permute-start(bf16[128,384]{1,0:T(8,128)(2,1)} %copy-done.58), channel_id=1, source_target_pairs={{0,24},{1,25},{2,26},{3,27},{4,28},{5,29},{6,30},{7,31},{8,16},{9,... | collective-permute-start | bytes 294920 | tf_op jit(solution)/shard_map/ppermute | solution.py:425
  280.5 11.0 %collective-permute-start.22 = (bf16[4,144,1536]{2,1,0:T(8,128)(2,1)}, bf16[4,144,1536]{2,1,0:T(8,128)(2,1)}, u32[]{:S(2)}, u32[]{:S(2)}) collective-permute-start(bf16[4,144,1536]{2,1,0:T(8,128)(2,1)} %get-tuple-element.235), channel_id=1, source_target_pairs={{0,1},{1,0},{2,3},{3,2},{4,5},{5,4},{6,7},{7,6},{8,9},{9,8},{10,11... | collective-permute-start | bytes 5308424 | tf_op jit(solution)/shard_map/ppermute | solution.py:425
  284.5 14.0 %all-to-all-start.4 = ((f32[32,1,96]{2,1,0:T(1,128)}), f32[32,1,96]{2,1,0:T(1,128)S(1)}, u32[]{:S(2)}, u32[]{:S(2)}) async-start(f32[32,1,96]{2,1,0:T(1,128)} %bitcast.21), calls=%async_computation.4 | async-start | bytes 32768 | tf_op jit(solution)/shard_map/all_to_all | solution.py:439
  298.4 26.7 %all-to-all-start.5 = ((bf16[4,128,1536]{2,1,0:T(8,128)(2,1)}), bf16[4,128,1536]{2,1,0:T(8,128)(2,1)}, u32[]{:S(2)}, u32[]{:S(2)}) async-start(bf16[4,128,1536]{2,1,0:T(8,128)(2,1)} %get-tuple-element.237), calls=%async_computation.5 | async-start | bytes 3145728 | tf_op jit(solution)/shard_map/all_to_all | solution.py:439
  305.3 35.2 %collective-permute-start.23 = (bf16[144,1536]{1,0:T(8,128)(2,1)}, bf16[144,1536]{1,0:T(8,128)(2,1)}, u32[]{:S(2)}, u32[]{:S(2)}) collective-permute-start(bf16[144,1536]{1,0:T(8,128)(2,1)} %get-tuple-element.239), channel_id=1, source_target_pairs={{0,2},{1,3},{2,0},{3,1},{4,6},{5,7},{6,4},{7,5},{8,10},{9,11},{10,... | collective-permute-start | bytes 1327112 | tf_op jit(solution)/shard_map/ppermute | solution.py:425
  305.8 34.7 %collective-permute-start.24 = (bf16[144,1536]{1,0:T(8,128)(2,1)}, bf16[144,1536]{1,0:T(8,128)(2,1)}, u32[]{:S(2)}, u32[]{:S(2)}) collective-permute-start(bf16[144,1536]{1,0:T(8,128)(2,1)} %get-tuple-element.240), channel_id=1, source_target_pairs={{0,4},{1,5},{2,6},{3,7},{4,0},{5,1},{6,2},{7,3},{8,12},{9,13},{10,... | collective-permute-start | bytes 1327112 | tf_op jit(solution)/shard_map/ppermute | solution.py:425
  307.7 32.8 %collective-permute-start.25 = (bf16[144,1536]{1,0:T(8,128)(2,1)}, bf16[144,1536]{1,0:T(8,128)(2,1)}, u32[]{:S(2)}, u32[]{:S(2)}) collective-permute-start(bf16[144,1536]{1,0:T(8,128)(2,1)} %get-tuple-element.241), channel_id=1, source_target_pairs={{0,6},{1,7},{2,4},{3,5},{4,2},{5,3},{6,0},{7,1},{8,14},{9,15},{10,... | collective-permute-start | bytes 1327112 | tf_op jit(solution)/shard_map/ppermute | solution.py:425
  309.8 18.2 %copy-start.72 = (f32[2,48]{1,0:T(2,128)}, f32[2,48]{1,0:T(2,128)S(1)}, u32[]{:S(2)}) copy-start(f32[2,48]{1,0:T(2,128)S(1)} %reshape.172) | copy-start | bytes 1156
  310.4 17.6 %copy-start.65 = (f32[2,48]{1,0:T(2,128)}, f32[2,48]{1,0:T(2,128)S(1)}, u32[]{:S(2)}) copy-start(f32[2,48]{1,0:T(2,128)S(1)} %get-tuple-element.274) | copy-start | bytes 1156
  310.9 17.2 %copy-start.36 = (f32[128,1536]{1,0:T(8,128)S(1)}, f32[128,1536]{1,0:T(8,128)}, u32[]{:S(2)}) copy-start(f32[128,1536]{1,0:T(8,128)} %copy-done.35) | copy-start | bytes 2359300
  (61 other events, 167.7 us)
Sparse Core Ops, SparseCore 0:
  10.2 44.9 all-gather.4
  67.3 73.9 all-gather.6
  143.7 30.9 all-gather.8
  217.4 103.1 reduce-scatter.1

commit v3 on v2

--- a/solution.py
+++ b/solution.py
@@ -29,7 +29,9 @@
 TN = (((0,), (0,)), ((), ()))
 NT = (((1,), (1,)), ((), ()))
 VMEM_SLACK = 12 * 1024 * 1024
+VMEM_ALL = 60 * 1024 * 1024
 TILE = 256
+SHORT = 30_000_000_000
 
 bf16 = jnp.bfloat16
 f32 = jnp.float32
@@ -74,7 +76,12 @@
     return jnp.where(lax.rem(column, HEAD_DIM) < HALF, left, right)
 
 
-def kernel_call(body, outs, ins, smem=(), hbm=(), scratch=(), sems=()):
+def waited(copy, ref):
+    copy.wait()
+    return ref
+
+
+def kernel_call(body, outs, ins, smem=(), hbm=(), late=(), scratch=(), sems=(), shared=False, flops=0):
     moved = [i for i in range(len(ins)) if i not in smem and i not in hbm]
 
     def fetched(*refs):
@@ -85,10 +92,12 @@
         ]
         for copy in copies:
             copy.start()
-        for copy in copies:
-            copy.wait()
         for j, i in enumerate(moved):
             given[i] = held[j]
+            if i in late:
+                given[i] = functools.partial(waited, copies[j], held[j])
+            else:
+                copies[j].wait()
         body(*given, *rest[: -1 - len(moved)])
 
     arrays = [*outs, *((ins[i].shape, ins[i].dtype) for i in moved)]
@@ -108,13 +117,13 @@
             *(pltpu.VMEM(ins[i].shape, ins[i].dtype) for i in moved),
             pltpu.SemaphoreType.DMA((len(moved),)),
         ],
-        compiler_params=pltpu.CompilerParams(vmem_limit_bytes=held_bytes + VMEM_SLACK),
-        cost_estimate=pl.CostEstimate(flops=0, bytes_accessed=0, transcendentals=0),
+        compiler_params=pltpu.CompilerParams(vmem_limit_bytes=held_bytes + VMEM_SLACK if shared else VMEM_ALL),
+        cost_estimate=pl.CostEstimate(flops=flops, bytes_accessed=0, transcendentals=0),
     )(*ins)
     return list(outputs)
 
 
-def project_body(x_ref, w_ref, gains_ref, cos_ref, sine_ref, out_ref, normed_ref, rows_ref):
+def project_body(at_ref, x_ref, w_ref, gains_ref, cos_ref, sine_ref, normed_ref, rows_ref, *refs):
     if gains_ref.shape[1] == D:
         rows_ref[...] = gains_ref[...]
     else:
@@ -128,11 +137,12 @@
                 ],
                 axis=1,
             )
-    for k in range(x_ref.shape[0]):
-        x = wide(x_ref[k])
-        normed_ref[k] = low(x * rms_scale(x) * rows_ref[0:1, :])
-        p = dot(normed_ref[k], w_ref[...], NT)
-        out_ref[k] = low(p * cos_ref[...] + swap_halves(p) * sine_ref[...])
+    for k, ref in enumerate(refs):
+        x = wide(x_ref[at_ref[0] ^ k])
+        normed = low(x * rms_scale(x) * rows_ref[0:1, :])
+        normed_ref[at_ref[0] ^ k] = normed
+        p = dot(normed, w_ref[...], NT)
+        ref[...] = low(p * cos_ref[...] + swap_halves(p) * sine_ref[...])
 
 
 def head_columns(blocks_ref, head):
@@ -141,7 +151,10 @@
     return blocks_ref[head // per, :, at : at + HEAD_DIM]
 
 
-def attend_body(slots, len_ref, qkv_ref, prob_ref, att_ref):
+def attend_body(n, slots, at_ref, len_ref, *refs):
+    in_refs, (qkv_ref, prob_ref, att_ref) = refs[:n], refs[n:]
+    for k in range(n):
+        qkv_ref[at_ref[0] ^ k] = in_refs[k][...]
     rows = qkv_ref.shape[1]
     seq_len = rows // slots
     shape = (GROUPS * rows, rows)
@@ -187,8 +200,7 @@
     normed_ref[...] = low(hidden * rms_scale(hidden) * gain_ref[1:2, :])
 
 
-def units_back_body(n, tile, *refs):
-    dy_refs, (w_ref, rows_ref, out_ref, held_ref, sems) = refs[:n], refs[n:]
+def units_back_body(tile, at_ref, dy_ref, w_ref, rows_ref, out_ref, held_ref, sems):
     tiles = range(0, held_ref.shape[0], tile)
     copies = [
         pltpu.make_async_copy(
@@ -198,9 +210,9 @@
     ]
     for copy in copies:
         copy.start()
-    rows = dy_refs[0].shape[0]
-    for k in range(n):
-        rows_ref[k * rows : (k + 1) * rows, :] = dy_refs[k][...]
+    rows = dy_ref.shape[1]
+    for k in range(dy_ref.shape[0]):
+        rows_ref[k * rows : (k + 1) * rows, :] = dy_ref[at_ref[1] ^ k]
     for copy, j in zip(copies, tiles):
         copy.wait()
         out_ref[:, j : j + tile] = dot(rows_ref[...], held_ref[j : j + tile, :], NT)
@@ -255,22 +267,19 @@
             out_refs[k - 1][:, at] = low(back[k * rows : (k + 1) * rows])
 
 
-def norm_back_body(n_z, n, at_ref, own_ref, *refs):
+def attend_back_body(n, n_z, at_ref, own_ref, *refs):
     got = refs[: n_z - 1]
-    hidden_ref, gain_ref, up_ref = refs[n_z - 1 : n_z + 2]
-    grad_ref, low_ref, gain_grad_ref = refs[n_z + 2 : n_z + 5]
-    col_refs, held_ref, sems = refs[n_z + 5 : -2], refs[-2], refs[-1]
-    width = D // n
-    copies = [pltpu.make_async_copy(r, held_ref.at[k], sems.at[k]) for k, r in enumerate(got)]
-    for copy in copies:
-        copy.start()
+    hidden_ref, gain_ref, up_ref, late_wo, late_qkv, late_prob, late_cos, late_sine = refs[
+        n_z - 1 : n_z + 7
+    ]
+    grad_ref, low_ref, gain_grad_ref, heads_ref = refs[n_z + 7 : n_z + 11]
+    col_refs = refs[n_z + 11 :]
     hidden = hidden_ref[...]
     scale = rms_scale(hidden)
     unit = hidden * scale
     dn = own_ref[...]
-    for k, copy in enumerate(copies):
-        copy.wait()
-        dn = dn + wide(held_ref[k])
+    for late in got:
+        dn = dn + wide(late()[...])
     gain_grad_ref[...] = jnp.sum(dn * unit, axis=0, keepdims=True)
     scaled = dn * gain_ref[1:2, :]
     grad = wide(up_ref[...]) + scale * (
@@ -278,15 +287,15 @@
     )
     grad_ref[...] = grad
     low_ref[...] = low(grad)
-    if col_refs:
-        for k in range(n):
-            at = pl.multiple_of((at_ref[0] ^ k) * width, 128)
-            col_refs[k][...] = low_ref[:, pl.ds(at, width)]
-
-
-def attend_back_body(n, grad_ref, wo_ref, qkv_ref, prob_ref, cos_ref, sine_ref, heads_ref):
-    rows = grad_ref.shape[0]
-    do = low(dot(grad_ref[...], wo_ref[...], NN))
+    width = D // n
+    for k, ref in enumerate(col_refs):
+        at = pl.multiple_of((at_ref[0] ^ k) * width, 128)
+        ref[...] = low_ref[:, pl.ds(at, width)]
+
+    wo_ref = late_wo()
+    do = low(dot(low_ref[...], wo_ref[...], NN))
+    qkv_ref, prob_ref, cos_ref, sine_ref = late_qkv(), late_prob(), late_cos(), late_sine()
+    rows = do.shape[0]
     grads = [None] * ALL_HEADS
     root = HEAD_DIM ** (-0.5)
     for g in range(KV_HEADS):
@@ -341,23 +350,28 @@
             part_refs[k - 1][:, at] = low(out[k * rows : (k + 1) * rows])
 
 
-def columns_grad_body(n, at_ref, in_ref, normed_ref, att_ref, *refs):
-    col_refs, (mine_ref, other_ref, held_ref, sum_ref) = refs[:n], refs[n:]
-    for k in range(n):
-        held_ref[at_ref[0] ^ k] = col_refs[k][...]
+def columns_grad_body(n, at_ref, late_in, late_normed, late_att, *refs):
+    late_cols, (mine_ref, other_ref, held_ref, sum_ref) = refs[:n], refs[n:]
     n_z = mine_ref.shape[0]
     blocks = 2 * n_z
+    in_ref, normed_ref = late_in(), late_normed()
     grads = in_ref[...].reshape(-1, in_ref.shape[2])
-    cols = held_ref[...].reshape(-1, held_ref.shape[2])
     normed = normed_ref[...].reshape(-1, D)
-    att = att_ref[...].reshape(-1, D)
-    first, second = grads.shape[1] // blocks, cols.shape[1] // blocks
+    first = grads.shape[1] // blocks
     for j in range(0, D, 512):
         at = slice(j, j + 512)
         one = dot(grads, normed[:, at], TN)
+        for i in range(blocks):
+            sum_ref[i, :first, at] = one[i * first : (i + 1) * first]
+    for k in range(n):
+        held_ref[at_ref[0] ^ k] = late_cols[k]()[...]
+    cols = held_ref[...].reshape(-1, held_ref.shape[2])
+    att = late_att()[...].reshape(-1, D)
+    second = cols.shape[1] // blocks
+    for j in range(0, D, 512):
+        at = slice(j, j + 512)
         two = dot(cols, att[:, at], TN)
         for i in range(blocks):
-            sum_ref[i, :first, at] = one[i * first : (i + 1) * first]
             sum_ref[i, first:, at] = two[i * second : (i + 1) * second]
     for z in range(n_z):
         i = (at_ref[1] ^ z) * 2
@@ -371,14 +385,22 @@
         ref[...] = low(mine_ref[k + 1] + wide(other_ref[k + 1]))
 
 
-def inputs_grad_body(grad_ref, w_ref, x_ref, out_ref, gain_ref):
+def inputs_grad_body(at_ref, grad_ref, w_ref, x_ref, second_ref, gain_ref, *out_refs):
     total = jnp.zeros((1, D), f32)
-    for k in range(x_ref.shape[0]):
-        back = dot(grad_ref[k], w_ref[...], NN)
-        x = wide(x_ref[k])
+    for k, ref in enumerate(out_refs):
+        back = dot(grad_ref[at_ref[0] ^ k], w_ref[...], NN)
+        x = wide(x_ref[at_ref[0] ^ k])
         total = total + jnp.sum(back * (x * rms_scale(x)), axis=0, keepdims=True)
-        out_ref[k] = low(back)
-    gain_ref[...] = total
+        ref[...] = back.astype(ref.dtype)
+    if gain_ref.shape[1] == D:
+        gain_ref[0:1, :] = total
+        gain_ref[1:2, :] = second_ref[...]
+    else:
+        width = gain_ref.shape[1] // 2
+        for d in range(gain_ref.shape[0]):
+            at = slice(d * width, (d + 1) * width)
+            gain_ref[d : d + 1, :width] = total[:, at]
+            gain_ref[d : d + 1, width:] = second_ref[:, at]
 
 
 def settle_body(rate, n, *refs):
@@ -502,8 +524,8 @@
     gain_all, out_own, in_group = tie(gain_all, out_own, in_group)
     row_valid = (jnp.arange(seq_len)[None, :] < lengths[:, None]).reshape(rows, 1)
     upstream = jnp.where(row_valid, cotangent.reshape(rows, D), jnp.zeros((), bf16))
-    upstream, in_group = tie(upstream, in_group)
-    upstream_parts = links.gather(upstream, links.z)
+    upstream_group, in_group = tie(jnp.tile(upstream[None], (n_z, 1, 1)), in_group)
+    upstream_group = exchange(upstream_group, "z")
     if not aligned:
         gain_all = wide(gain_all).reshape(devices, 2, -1)
         gain_all = jnp.swapaxes(gain_all, 0, 1).reshape(2, D)
@@ -512,16 +534,14 @@
     ff_low, in_group = tie(ff_low, in_group)
     ff = lax.all_gather(ff_low, PLANE, axis=1, tiled=True)
 
-    blocks, normed_group, gain_rows = kernel_call(
+    normed_group, gain_rows, *blocks = kernel_call(
         project_body,
-        [
-            ((n_dp, rows, group), bf16),
-            ((n_dp, rows, D), bf16),
-            ((2, D), f32),
-        ],
-        [token_group, in_group, gain_all, cos_here, sine_here],
-    )
-    qkv = exchange(blocks, "dp")
+        [((n_dp, rows, D), bf16), ((2, D), f32)] + [((rows, group), bf16)] * n_dp,
+        [at, token_group, in_group, gain_all, cos_here, sine_here],
+        smem=(0,),
+    )
+    blocks = links.spread(blocks, links.dp)
+    normed_group, out_own = tie(normed_group, out_own)
 
     out_own = jnp.stack(out_own).reshape(n_dp * n_z, out_width, D)
     out_other = links.send(out_own, 1)
@@ -539,13 +559,17 @@
             )
         ]
 
-    prob, attended = kernel_call(
-        functools.partial(attend_body, slots),
-        [((KV_HEADS, GROUPS * rows, rows), f32), ((rows, D), bf16)],
-        [lengths.astype(jnp.int32), qkv],
-        smem=(0,),
-    )
-    attended, upstream_parts = tie(attended, upstream_parts)
+    qkv, prob, attended = kernel_call(
+        functools.partial(attend_body, n_dp, slots),
+        [
+            ((n_dp, rows, group), bf16),
+            ((KV_HEADS, GROUPS * rows, rows), f32),
+            ((rows, D), bf16),
+        ],
+        [at, lengths.astype(jnp.int32), *blocks],
+        smem=(0, 1),
+    )
+    attended, upstream_group = tie(attended, upstream_group)
     hidden, normed_two, out_full = kernel_call(
         functools.partial(out_body, n_z),
         [((rows, D), f32), ((rows, D), bf16), ((devices, out_width, D), bf16)],
@@ -560,12 +584,14 @@
     attended_group = lax.all_gather(attended, "dp", axis=0)
     group_rows, units = n_z * rows, n_dp * 2 * ff_width
     upstream_group, grad_active = kernel_call(
-        functools.partial(units_back_body, n_z, TILE),
+        functools.partial(units_back_body, TILE),
         [((group_rows, D), bf16), ((group_rows, units), f32)],
-        [*upstream_parts, ff],
-        hbm=(n_z,),
+        [at, upstream_group, ff],
+        smem=(0,),
+        hbm=(2,),
         scratch=[((units, D), bf16)],
         sems=[(units // TILE,)],
+        shared=True,
     )
     normed_parts, grad_active = tie(normed_parts, grad_active)
     normed_rows, active, grad_gate, grad_up, *grad_normed = kernel_call(
@@ -578,6 +604,7 @@
         hbm=range(n_z + 1),
         scratch=[((2, units, D), bf16)],
         sems=[(2, units // TILE), (n_z,)],
+        shared=True,
     )
     grad_normed = links.spread(grad_normed, links.z)
     grad_ff, *partial_out = kernel_call(
@@ -587,38 +614,45 @@
         hbm=(5,),
         scratch=[((units, D), bf16)],
         sems=[()],
-    )
-    grad_ff, partial_out, grad_normed = tie(grad_ff, partial_out, grad_normed)
+        shared=True,
+    )
     grad_ff = lax.psum_scatter(grad_ff, PLANE, scatter_dimension=1, tiled=True)
+    partial_out, grad_normed = tie(partial_out, grad_normed)
     partial_out = links.spread(partial_out, links.z)
 
     col_width = D // n_dp
     col_aligned = col_width % 128 == 0
-    grad_hidden, grad_branch, gain_two_grad, *columns = kernel_call(
-        functools.partial(norm_back_body, n_z, n_dp),
-        [((rows, D), f32), ((rows, D), bf16), ((1, D), f32)]
+    grad_hidden, grad_branch, gain_two_grad, blocks, *columns = kernel_call(
+        functools.partial(attend_back_body, n_dp, n_z),
+        [((rows, D), f32), ((rows, D), bf16), ((1, D), f32), ((n_dp, rows, group), bf16)]
         + ([((rows, col_width), bf16)] * n_dp if col_aligned else []),
-        [at, *grad_normed, hidden, gain_rows, upstream],
+        [
+            at,
+            *grad_normed,
+            hidden,
+            gain_rows,
+            upstream,
+            out_full,
+            qkv,
+            prob,
+            cos_rows,
+            sine_rows,
+        ],
         smem=(0,),
-        hbm=range(2, n_z + 1),
-        scratch=[((n_z - 1, rows, D), bf16)],
-        sems=[(n_z - 1,)],
+        late=(*range(2, n_z + 1), *range(n_z + 4, n_z + 9)),
+        flops=SHORT,
     )
     if not col_aligned:
         split = jnp.swapaxes(grad_branch.reshape(rows, n_dp, col_width), 0, 1)
         columns = [block_of(split, at_dp ^ k) for k in range(n_dp)]
     columns = links.spread(columns, links.dp)
 
-    (blocks,) = kernel_call(
-        functools.partial(attend_back_body, n_dp),
-        [((n_dp, rows, group), bf16)],
-        [grad_branch, out_full, qkv, prob, cos_rows, sine_rows],
-    )
     blocks, partial_out[-1] = tie(blocks, partial_out[-1])
     grad_proj = exchange(blocks, "dp")
-    grad_proj, partial_out, columns = tie(grad_proj, partial_out, columns)
+    grad_proj, columns = tie(grad_proj, columns)
 
     col_rows = in_width + out_width
+
     if aligned:
         mine, other = kernel_call(
             functools.partial(columns_grad_body, n_dp),
@@ -626,6 +660,8 @@
             [at, grad_proj, normed_group, attended_group, *columns],
             scratch=[((n_dp, rows, col_width), bf16), ((n_zc, col_rows, D), f32)],
             smem=(0,),
+            late=range(1, n_dp + 4),
+            flops=SHORT,
         )
     else:
         columns = jnp.stack(columns)
@@ -638,35 +674,38 @@
             axis=1,
         ).reshape(n_z, 2, col_rows, D)
         mine, other = (
-            jnp.stack(
-                [block_of(block_of(total, at_z ^ z), at_core ^ c) for z in range(n_z)]
-            )
+            jnp.stack([block_of(block_of(total, at_z ^ z), at_core ^ c) for z in range(n_z)])
             for c in range(2)
         )
         other = low(other)
     grad_proj, mine = tie(grad_proj, mine)
     other = links.send(other, 1)
+    grad_gains, *grad_normed_one = kernel_call(
+        inputs_grad_body,
+        [((devices, D // devices * 2) if aligned else (2, D), f32), ((rows, D), f32)]
+        + [((rows, D), bf16)] * (n_dp - 1),
+        [at, grad_proj, in_group, token_group, gain_two_grad],
+        smem=(0,),
+        flops=SHORT,
+    )
+    if not aligned:
+        grad_gains = jnp.swapaxes(grad_gains.reshape(2, devices, -1), 0, 1).reshape(devices, -1)
+    other, partial_out = tie(other, partial_out)
     grad_cols = kernel_call(
         add_body,
         [((col_rows, D), f32)] + [((col_rows, D), bf16)] * (n_z - 1),
         [mine, other],
     )
-    grad_normed_one, gain_one_grad = kernel_call(
-        inputs_grad_body,
-        [((n_dp, rows, D), bf16), ((1, D), f32)],
-        [grad_proj, in_group, token_group],
-    )
-    grad_gains = jnp.concatenate([gain_one_grad, gain_two_grad])
-    grad_gains = jnp.swapaxes(grad_gains.reshape(2, devices, -1), 0, 1).reshape(devices, -1)
-    grad_gains = exchange(grad_gains, AXES)
     grad_normed_one, grad_gains, grad_cols[0] = tie(grad_normed_one, grad_gains, grad_cols[0])
     grad_cols = links.spread(grad_cols, links.z)
-    grad_gain = jnp.sum(grad_gains, axis=0).reshape(gains_pair.shape)
-    parts = exchange(grad_normed_one, "dp")
+    parts = [grad_normed_one[0]]
+    for k in range(1, n_dp):
+        parts.append(links.send(grad_normed_one[k], links.dp[k]))
+    grad_gains = exchange(grad_gains, AXES)
     total_out = hidden + partial_out[0] + sum(wide(r) for r in partial_out[1:])
     produced = low(jnp.where(row_valid, total_out, 0.0))
 
-    grad_normed_one = jnp.sum(wide(parts), axis=0)
+    grad_normed_one = parts[0] + sum(wide(r) for r in parts[1:])
     inputs = wide(token_rows)
     scale_one = rms_scale(inputs)
     unit_one = inputs * scale_one
@@ -695,8 +734,11 @@
 
     new_gate_up = update_ff(grad_ff[:2], gate_up, gate_up_mom, gate_up_avg, True)
     new_down = update(down_proj, wide(grad_ff[2]), down_proj_mom, down_proj_avg, step_rate)
+    grad_cols, grad_gains, new_gate_up, new_down = tie(
+        grad_cols, grad_gains, new_gate_up, new_down
+    )
+    grad_gain = jnp.sum(grad_gains, axis=0).reshape(gains_pair.shape)
     new_gains = update(gains_pair, grad_gain, gains_mom, gains_avg, step_rate)
-    grad_cols, new_gate_up, new_down = tie(grad_cols, new_gate_up, new_down)
     new_cols = settle(
         grad_cols, in_proj, in_proj_mom, in_proj_avg, out_proj, out_proj_mom, out_proj_avg
     )

time: 357 us -> 324 us (0.908); the launches traced: 351 us -> 322 us
  local copies, waits for them, and re-layouts: 45 us -> 20.2 us
  Pallas kernels: 66.1 us -> 84.1 us
  starting transfers between devices: 100 us -> 89.2 us
  other arithmetic: 24.8 us -> 18.2 us
  waiting for transfers between devices: 101 us -> 96.2 us
    unnamed x147 -> x93, local copies, waits for them, and re-layouts: 39.6 us -> 13.8 us
    all_to_all x6 -> x5, waiting for transfers between devices: 24.8 us -> 5.94 us  [exchange(): return lax.all_to_all(values, axes, split_axis=0, concat_axis=0, tiled=True)]
    pallas_call x14 -> x13, Pallas kernels: 66.1 us -> 84.1 us  [kernel_call(): pl.pallas_call(fetched, out_shape=[jax.ShapeDtypeStruct(s, t) for s, t in...]
    ppermute x26 -> x29, starting transfers between devices: 63.3 us -> 53.8 us  [send(): lax.ppermute(values, AXES, [(i, i ^ mask) for i in range(self.count)])]
    all_gather x1, waiting for transfers between devices: 0.01 us -> 9.21 us  [on_device(): ff = lax.all_gather(ff_low, PLANE, axis=1, tiled=True)]
    ppermute x26 -> x29, waiting for transfers between devices: 76.2 us -> 80.9 us  [send(): lax.ppermute(values, AXES, [(i, i ^ mask) for i in range(self.count)])]
    all_to_all x6 -> x5, starting transfers between devices: 36.4 us -> 35.1 us  [exchange(): return lax.all_to_all(values, axes, split_axis=0, concat_axis=0, tiled=True)]
  transfers between devices with their start and end apart: 36 -> 38, of which waited for: 13 -> 13; matrix products, arithmetic and copies ran while one was open for 8% -> 6% of each run, Pallas kernels for 18% -> 25%
where the time goes in v3:
time: 324 us; the launch traced here: 322 us
  waiting for transfers between devices  96.2 us (30%)
  starting transfers between devices  89.2 us (28%)
  Pallas kernels  84.1 us (26%)
  local copies, waits for them, and re-layouts  20.2 us (6%)
  other arithmetic  18.2 us (6%)
  between operations  14.4 us (4%)
    pallas_call x13, Pallas kernels, kernel_call(): pl.pallas_call(fetched, out_shape=[jax.ShapeDtypeStruct(s, t) for s, t in...  84.1 us
    ppermute x29, waiting for transfers between devices, send(): lax.ppermute(values, AXES, [(i, i ^ mask) for i in range(self.count)])  80.9 us
    ppermute x29, starting transfers between devices, send(): lax.ppermute(values, AXES, [(i, i ^ mask) for i in range(self.count)])  53.8 us
    all_to_all x5, starting transfers between devices, exchange(): return lax.all_to_all(values, axes, split_axis=0, concat_axis=0, tiled=True)  35.1 us
    unnamed x93, local copies, waits for them, and re-layouts  13.8 us
    all_gather x1, waiting for transfers between devices, on_device(): ff = lax.all_gather(ff_low, PLANE, axis=1, tiled=True)  9.21 us
  transfers between devices with their start and end apart: 38, of which 13 were waited for; matrix products, arithmetic and copies ran while one was open for 6% of the time, Pallas kernels for 25%

profile of v3, /device:TPU:0, one launch (start us, length us, event | category | flops | bytes accessed | tf_op | source)
XLA Modules:
  0.0 322.2 jit_solution(4536323836456175123)
XLA Ops:
  7.2 1.8 bitcast_convert_fusion
  9.1 2.3 tile.47
  11.3 5.3 %all-to-all-start = ((bf16[4,128,1536]{2,1,0:T(8,128)(2,1)}), bf16[4,128,1536]{2,1,0:T(8,128)(2,1)S(1)}, u32[]{:S(2)}, u32[]{:S(2)}) async-start(bf16[4,128,1536]{2,1,0:T(8,128)(2,1)} %tile.47), calls=%async_computation | async-start | bytes 3145728 | tf_op jit(solution)/shard_map/all_to_all | solution.py:461
  18.3 2.6 collective-permute-start.1
  23.0 2.2 collective-permute-done
  25.2 14.2 %collective-permute-done.1 = bf16[48,1536]{1,0:T(8,128)(2,1)S(1)} collective-permute-done((bf16[48,1536]{1,0:T(8,128)(2,1)S(1)}, bf16[48,1536]{1,0:T(8,128)(2,1)S(1)}, u32[]{:S(2)}, u32[]{:S(2)}) %collective-permute-start.1) | collective-permute-done | bytes 147488 | tf_op jit(solution)/shard_map/ppermute | solution.py:447
  40.5 2.3 collective-permute-start.3
  45.6 13.4 %all-to-all-start.1 = ((bf16[32,1,96]{2,1,0:T(2,128)(2,1)}), bf16[32,1,96]{2,1,0:T(2,128)(2,1)S(1)}, u32[]{:S(2)}, u32[]{:S(2)}) async-start(bf16[32,1,96]{2,1,0:T(2,128)(2,1)} %copy.46), calls=%async_computation.1 | async-start | bytes 32768 | tf_op jit(solution)/shard_map/all_to_all | solution.py:461
  60.2 3.1 shard_map.385
  63.3 2.8 all-to-all-done.1
  68.0 9.6 %all-to-all-start.2 = ((bf16[4,128,1536]{2,1,0:T(8,128)(2,1)}), bf16[4,128,1536]{2,1,0:T(8,128)(2,1)S(1)}, u32[]{:S(2)}, u32[]{:S(2)}) async-start(bf16[4,128,1536]{2,1,0:T(8,128)(2,1)} %tile.48), calls=%async_computation.2 | async-start | bytes 3145728 | tf_op jit(solution)/shard_map/all_to_all | solution.py:461
  78.2 8.2 %shard_map.386 = (bf16[4,128,1536]{2,1,0:T(8,128)(2,1)}, f32[2,1536]{1,0:T(2,128)}, bf16[128,768]{1,0:T(8,128)(2,1)}, bf16[128,768]{1,0:T(8,128)(2,1)}, bf16[128...) custom-call(s32[3]{0:T(128)} %pad_add_fusion.refs_0_, bf16[4,128,1536]{2,1,0:T(8,128)(2,1)} %copy-done.9, ...), custom_call_target="tpu_custom_call" | custom-call | tf_op jit(solution)/shard_map/pallas_call | solution.py:106
  86.5 3.0 pad_maximum_fusion
  91.1 1.9 collective-permute-start.8
  93.0 7.8 %collective-permute-done.6.refs_3_ = bf16[128,768]{1,0:T(8,128)(2,1)S(1)} collective-permute-done((bf16[128,768]{1,0:T(8,128)(2,1)S(1)}, bf16[128,768]{1,0:T(8,128)(2,1)S(1)}, u32[]{:S(2)}, u32[]{:S(2)}) %collective-permute-start.6) | collective-permute-done | bytes 196640 | tf_op jit(solution)/shard_map/ppermute | solution.py:447
  101.2 4.6 %collective-permute-done.8.refs_5_ = bf16[128,768]{1,0:T(8,128)(2,1)S(1)} collective-permute-done((bf16[128,768]{1,0:T(8,128)(2,1)S(1)}, bf16[128,768]{1,0:T(8,128)(2,1)S(1)}, u32[]{:S(2)}, u32[]{:S(2)}) %collective-permute-start.8) | collective-permute-done | bytes 196640 | tf_op jit(solution)/shard_map/ppermute | solution.py:447
  106.4 5.3 %shard_map.387 = (bf16[4,128,768]{2,1,0:T(8,128)(2,1)}, f32[8,256,128]{2,1,0:T(8,128)}, bf16[128,1536]{1,0:T(8,128)(2,1)}) custom-call(s32[3]{0:T(128)} %pad_add_fusion.refs_0_, s32[2]{0:T(128)} %refs_1_.4, bf16[128,768]{1,0:T(8,128)(2,1)} %get-tuple-element.176.refs_2_, bf16[128,768]{1,0:T(8,128)(2,1)} %copy-done.26, bf16[128,768]{1,0:T(8,128)(2,1)} %copy-done.27, ...), custom_call_target="tpu_custom_call" | custom-call | tf_op jit(solution)/shard_map/pallas_call | solution.py:106
  111.7 3.1 all-to-all-done.2.refs_1_
  115.1 8.7 %shard_map.388 = (f32[128,1536]{1,0:T(8,128)}, bf16[128,1536]{1,0:T(8,128)(2,1)}, bf16[32,48,1536]{2,1,0:T(8,128)(2,1)}) custom-call(s32[3]{0:T(128)} %pad_add_fusion.refs_0_, bf16[128,1536]{1,0:T(8,128)(2,1)} %get-tuple-element.182.refs_1_, bf16[128,1536]{1,0:T(8,128)(2,1)} %bitcast.63, f32[2,1536]{1,0:T(2,128)} %get-tuple-element.183.refs_3_.refs_6_, ...), custom_call_target="tpu_custom_call" | custom-call | tf_op jit(solution)/shard_map/pallas_call | solution.py:106
  123.9 1.9 collective-permute-start.11
  125.7 2.5 collective-permute-start.12
  128.2 9.2 %all-gather.7.cloned.1.call-done.refs_2_.refs_4_.refs_5_ = bf16[3,1024,1536]{2,1,0:T(8,128)(2,1)} async-done(((bf16[3,128,1536]{2,1,0:T(8,128)(2,1)}), bf16[3,1024,1536]{2,1,0:T(8,128)(2,1)}) %all-gather.7.cloned.1.call-update) | async-done | bytes 9437200 | tf_op jit(solution)/shard_map/all_gather | solution.py:535
  137.4 3.7 %copy-done = bf16[3,1024,1536]{2,1,0:T(8,128)(2,1)S(1)} copy-done((bf16[3,1024,1536]{2,1,0:T(8,128)(2,1)S(1)}, bf16[3,1024,1536]{2,1,0:T(8,128)(2,1)}, u32[]{:S(2)}) %copy-start) | copy-done | bytes 9437208
  141.1 5.0 %shard_map.389 = (bf16[512,1536]{1,0:T(8,128)(2,1)S(1)}, f32[512,1024]{1,0:T(8,128)S(1)}) custom-call(s32[3]{0:T(128)S(1)} %copy-done.4, bf16[4,128,1536]{2,1,0:T(8,128)(2,1)S(1)} %all-to-all-done.2.refs_1_, bf16[3,1024,1536]{2,1,0:T(8,128)(2,1)S(1)} %copy-done), custom_call_target="tpu_custom_call" | custom-call | tf_op jit(solution)/shard_map/pallas_call | solution.py:106
  146.1 7.8 %collective-permute-done.11.refs_2_ = bf16[128,1536]{1,0:T(8,128)(2,1)S(1)} collective-permute-done((bf16[128,1536]{1,0:T(8,128)(2,1)}, bf16[128,1536]{1,0:T(8,128)(2,1)S(1)}, u32[]{:S(2)}, u32[]{:S(2)}) %collective-permute-start.11) | collective-permute-done | bytes 393248 | tf_op jit(solution)/shard_map/ppermute | solution.py:447
  153.9 9.2 %shard_map.390 = (bf16[512,1536]{1,0:T(8,128)(2,1)S(1)}, bf16[512,1024]{1,0:T(8,128)(2,1)S(1)}, bf16[512,1024]{1,0:T(8,128)(2,1)S(1)}, bf16[512,1024]{1,0:T(8,12...) custom-call(bf16[128,1536]{1,0:T(8,128)(2,1)S(1)} %copy-done.3, ...), custom_call_target="tpu_custom_call" | custom-call | tf_op jit(solution)/shard_map/pallas_call | solution.py:106
  164.0 7.6 %shard_map.391 = (bf16[3,1024,1536]{2,1,0:T(8,128)(2,1)S(1)}, f32[128,1536]{1,0:T(8,128)S(1)}, bf16[128,1536]{1,0:T(8,128)(2,1)S(1)}, bf16[128,1536]{1,0:T(8,128)(2,1)S(1)}, bf16[128,1536]{1,0:T(8,128)(2,1)S(1)}) custom-call(bf16[512,1024]{1,0:T(8,128)(2,1)S(1)} %get-tuple-element.203.refs_0_, bf16[512,1024]{1,0:T(8,128)(2,1)S(1)} %get-tuple-element.204.refs_1_, ...), custom_call_target="tpu_custom_call" | custom-call | tf_op jit(solution)/shard_map/pallas_call | solution.py:106
  171.6 3.7 %copy-done.2 = bf16[3,1024,1536]{2,1,0:T(8,128)(2,1)} copy-done((bf16[3,1024,1536]{2,1,0:T(8,128)(2,1)}, bf16[3,1024,1536]{2,1,0:T(8,128)(2,1)S(1)}, u32[]{:S(2)}) %copy-start.2) | copy-done | bytes 9437208
  176.3 7.1 %collective-permute-start.13 = (bf16[128,1536]{1,0:T(8,128)(2,1)S(1)}, bf16[128,1536]{1,0:T(8,128)(2,1)S(1)}, u32[]{:S(2)}, u32[]{:S(2)}) collective-permute-start(bf16[128,1536]{1,0:T(8,128)(2,1)S(1)} %copy-done.7), channel_id=1, source_target_pairs={{0,2},{1,3},{2,0},{3,1},{4,6},{5,7},{6,4},{7,5},{8,10},{9,11},{10,... | collective-permute-start | bytes 1179656 | tf_op jit(solution)/shard_map/ppermute | solution.py:447
  183.4 2.4 collective-permute-start.15
  185.8 11.4 %collective-permute-done.13.refs_2_ = bf16[128,1536]{1,0:T(8,128)(2,1)S(1)} collective-permute-done((bf16[128,1536]{1,0:T(8,128)(2,1)S(1)}, bf16[128,1536]{1,0:T(8,128)(2,1)S(1)}, u32[]{:S(2)}, u32[]{:S(2)}) %collective-permute-start.13) | collective-permute-done | bytes 393248 | tf_op jit(solution)/shard_map/ppermute | solution.py:447
  197.2 20.2 %collective-permute-done.14.refs_3_ = bf16[128,1536]{1,0:T(8,128)(2,1)S(1)} collective-permute-done((bf16[128,1536]{1,0:T(8,128)(2,1)S(1)}, bf16[128,1536]{1,0:T(8,128)(2,1)S(1)}, u32[]{:S(2)}, u32[]{:S(2)}) %collective-permute-start.14) | collective-permute-done | bytes 393248 | tf_op jit(solution)/shard_map/ppermute | solution.py:447
  218.9 9.6 %shard_map.392 = (f32[128,1536]{1,0:T(8,128)}, bf16[128,1536]{1,0:T(8,128)(2,1)}, f32[1,1536]{1,0:T(1,128)}, bf16[4,128,768]{2,1,0:T(8,128)(2,1)}, bf16[128,384]...) custom-call(s32[3]{0:T(128)} %pad_add_fusion.refs_0_, ...), custom_call_target="tpu_custom_call" | custom-call | flops 30000001024 | tf_op jit(solution)/shard_map/pallas_call | solution.py:106
  228.5 3.9 %all-to-all-start.3 = ((bf16[4,128,768]{2,1,0:T(8,128)(2,1)}), bf16[4,128,768]{2,1,0:T(8,128)(2,1)S(1)}, u32[]{:S(2)}, u32[]{:S(2)}) async-start(bf16[4,128,768]{2,1,0:T(8,128)(2,1)} %get-tuple-element.227), calls=%async_computation.3 | async-start | bytes 1572864 | tf_op jit(solution)/shard_map/all_to_all | solution.py:461
  236.2 9.3 %collective-permute-start.21 = (bf16[128,1536]{1,0:T(8,128)(2,1)S(1)}, bf16[128,1536]{1,0:T(8,128)(2,1)S(1)}, u32[]{:S(2)}, u32[]{:S(2)}) collective-permute-start(bf16[128,1536]{1,0:T(8,128)(2,1)S(1)} %get-tuple-element.240), channel_id=1, source_target_pairs={{0,2},{1,3},{2,0},{3,1},{4,6},{5,7},{6,4},{7,5},{8,10},{9,11},{10,... | collective-permute-start | bytes 1179656 | tf_op jit(solution)/shard_map/ppermute | solution.py:447
  248.6 7.3 %shard_map.393 = (f32[4,144,1536]{2,1,0:T(8,128)}, bf16[4,144,1536]{2,1,0:T(8,128)(2,1)}) custom-call(s32[3]{0:T(128)} %pad_add_fusion.refs_0_, bf16[4,128,768]{2,1,0:T(8,128)(2,1)} %copy-done.20, bf16[4,128,1536]{2,1,0:T(8,128)(2,1)} %get-tuple-element.233.refs_2_, bf16[4,128,1536]{2,1,0:T(8,128)(2,1)} %bitcast.81, ...), custom_call_target="tpu_custom_call" | custom-call | flops 30000001024 | tf_op jit(solution)/shard_map/pallas_call | solution.py:106
  256.0 5.3 %shard_map.394 = (f32[32,96]{1,0:T(8,128)}, f32[128,1536]{1,0:T(8,128)}, bf16[128,1536]{1,0:T(8,128)(2,1)}, bf16[128,1536]{1,0:T(8,128)(2,1)}, bf16[128,1536]{1,0:T(8,128)(2,1)}) custom-call(s32[3]{0:T(128)} %pad_add_fusion.refs_0_, bf16[4,128,768]{2,1,0:T(8,128)(2,1)} %copy-done.20, bf16[768,1536]{1,0:T(8,128)(2,1)} %all-gather.5.cloned.1.call-done.refs_2_, ...), custom_call_target="tpu_custom_call" | custom-call | flops 30000001024 | tf_op jit(solution)/shard_map/pallas_call | solution.py:106
  261.4 4.1 %shard_map.395 = (f32[144,1536]{1,0:T(8,128)}, bf16[144,1536]{1,0:T(8,128)(2,1)}, bf16[144,1536]{1,0:T(8,128)(2,1)}, bf16[144,1536]{1,0:T(8,128)(2,1)}) custom-call(f32[4,144,1536]{2,1,0:T(8,128)} %get-tuple-element.256.refs_0_, bf16[4,144,1536]{2,1,0:T(8,128)(2,1)} %collective-permute-done.20.refs_1_), custom_call_target="tpu_custom_call" | custom-call | tf_op jit(solution)/shard_map/pallas_call | solution.py:106
  265.4 4.9 %collective-permute-start.26 = (bf16[144,1536]{1,0:T(8,128)(2,1)}, bf16[144,1536]{1,0:T(8,128)(2,1)S(1)}, u32[]{:S(2)}, u32[]{:S(2)}) collective-permute-start(bf16[144,1536]{1,0:T(8,128)(2,1)} %get-tuple-element.264), channel_id=1, source_target_pairs={{0,2},{1,3},{2,0},{3,1},{4,6},{5,7},{6,4},{7,5},{8,10},{9,11},{10,... | collective-permute-start | bytes 1327112 | tf_op jit(solution)/shard_map/ppermute | solution.py:447
  271.2 2.9 all-to-all-start.4
  274.1 1.8 collective-permute-start.23
  277.7 2.0 select_convert_fusion
  279.7 6.7 %collective-permute-done.23 = bf16[128,1536]{1,0:T(8,128)(2,1)S(1)} collective-permute-done((bf16[128,1536]{1,0:T(8,128)(2,1)}, bf16[128,1536]{1,0:T(8,128)(2,1)S(1)}, u32[]{:S(2)}, u32[]{:S(2)}) %collective-permute-start.23) | collective-permute-done | bytes 393248 | tf_op jit(solution)/shard_map/ppermute | solution.py:447
  286.4 3.6 %collective-permute-start.28 = (bf16[144,1536]{1,0:T(8,128)(2,1)}, bf16[144,1536]{1,0:T(8,128)(2,1)}, u32[]{:S(2)}, u32[]{:S(2)}) collective-permute-start(bf16[144,1536]{1,0:T(8,128)(2,1)} %get-tuple-element.266), channel_id=1, source_target_pairs={{0,6},{1,7},{2,4},{3,5},{4,2},{5,3},{6,0},{7,1},{8,14},{9,15},{10,... | collective-permute-start | bytes 1327112 | tf_op jit(solution)/shard_map/ppermute | solution.py:447
  290.0 5.6 %collective-permute-done.24 = bf16[128,1536]{1,0:T(8,128)(2,1)S(1)} collective-permute-done((bf16[128,1536]{1,0:T(8,128)(2,1)}, bf16[128,1536]{1,0:T(8,128)(2,1)S(1)}, u32[]{:S(2)}, u32[]{:S(2)}) %collective-permute-start.24) | collective-permute-done | bytes 393248 | tf_op jit(solution)/shard_map/ppermute | solution.py:447
  297.5 2.3 fusion.10
  303.5 6.2 %shard_map.396 = (f32[2,1536,128]{2,1,0:T(8,128)}, f32[2,1536,128]{2,1,0:T(8,128)}, f32[2,1536,128]{2,1,0:T(8,128)}, f32[2,1536,128]{2,1,0:T(8,128)}, bf16[2,1536,128]{2,1,0:T(8,128)(2,1)}) custom-call(bf16[2,128,1536]{2,1,0:T(8,128)(2,1)} %slice.12.refs_0_, f32[2,1536,128]{2,1,0:T(8,128)} %refs_1_.5, f32[2,1536,128]{2,1,0:T(8,128)} %refs_2_.1, ...), custom_call_target="tpu_custom_call" | custom-call | tf_op jit(solution)/shard_map/pallas_call | solution.py:106
  311.0 4.7 %shard_map.397 = (f32[96,1536]{1,0:T(8,128)}, f32[96,1536]{1,0:T(8,128)}, f32[96,1536]{1,0:T(8,128)}, f32[96,1536]{1,0:T(8,128)}, bf16[96,1536]{1,0:T(8,128)(2,1...) custom-call(f32[144,1536]{1,0:T(8,128)} %get-tuple-element.274.refs_, ...), custom_call_target="tpu_custom_call" | custom-call | tf_op jit(solution)/shard_map/pallas_call | solution.py:106
  (177 shorter events, 34.1 us)
Async XLA Ops:
  7.2 59.5 %all-gather.5.cloned.1.call-start = ((), (), s32[]{:S(2)}) async-start(), calls=%async_computation.6 | async-start | bytes 2654208 | tf_op jit(solution)/shard_map/all_gather | solution.py:510
  11.3 28.0 %all-to-all-start = ((bf16[4,128,1536]{2,1,0:T(8,128)(2,1)}), bf16[4,128,1536]{2,1,0:T(8,128)(2,1)S(1)}, u32[]{:S(2)}, u32[]{:S(2)}) async-start(bf16[4,128,1536]{2,1,0:T(8,128)(2,1)} %tile.47), calls=%async_computation | async-start | bytes 3145728 | tf_op jit(solution)/shard_map/all_to_all | solution.py:461
  16.7 8.5 %collective-permute-start = (bf16[48,1536]{1,0:T(8,128)(2,1)S(1)}, bf16[48,1536]{1,0:T(8,128)(2,1)S(1)}, u32[]{:S(2)}, u32[]{:S(2)}) collective-permute-start(bf16[48,1536]{1,0:T(8,128)(2,1)S(1)} %bitcast_convert_fusion.1), channel_id=1, source_target_pairs={{0,2},{1,3},{2,0},{3,1},{4,6},{5,7},{6,4},{7,5},{8,10},{9,11},{10,... | collective-permute-start | bytes 442376 | tf_op jit(solution)/shard_map/ppermute | solution.py:447
  18.3 21.0 %collective-permute-start.1 = (bf16[48,1536]{1,0:T(8,128)(2,1)S(1)}, bf16[48,1536]{1,0:T(8,128)(2,1)S(1)}, u32[]{:S(2)}, u32[]{:S(2)}) collective-permute-start(bf16[48,1536]{1,0:T(8,128)(2,1)S(1)} %bitcast_convert_fusion.1), channel_id=1, source_target_pairs={{0,4},{1,5},{2,6},{3,7},{4,0},{5,1},{6,2},{7,3},{8,12},{9,13},{10,... | collective-permute-start | bytes 442376 | tf_op jit(solution)/shard_map/ppermute | solution.py:447
  20.9 18.5 %collective-permute-start.2 = (bf16[48,1536]{1,0:T(8,128)(2,1)S(1)}, bf16[48,1536]{1,0:T(8,128)(2,1)}, u32[]{:S(2)}, u32[]{:S(2)}) collective-permute-start(bf16[48,1536]{1,0:T(8,128)(2,1)S(1)} %bitcast_convert_fusion.1), channel_id=1, source_target_pairs={{0,6},{1,7},{2,4},{3,5},{4,2},{5,3},{6,0},{7,1},{8,14},{9,15},{10,... | collective-permute-start | bytes 442376 | tf_op jit(solution)/shard_map/ppermute | solution.py:447
  21.6 17.7 %copy-start.16 = (f32[128,768]{1,0:T(8,128)}, f32[128,768]{1,0:T(8,128)S(1)}, u32[]{:S(2)}) copy-start(f32[128,768]{1,0:T(8,128)S(1)} %tile.21.refs_11_) | copy-start | bytes 1179652
  21.9 38.3 %copy-start.17 = (f32[128,768]{1,0:T(8,128)}, f32[128,768]{1,0:T(8,128)S(1)}, u32[]{:S(2)}) copy-start(f32[128,768]{1,0:T(8,128)S(1)} %tile.45.refs_12_) | copy-start | bytes 1179652
  21.9 22.4 %copy-start.37 = (s32[2]{0:T(128)S(1)}, s32[2]{0:T(128)}, u32[]{:S(2)}) copy-start(s32[2]{0:T(128)} %refs_1_.4) | copy-start | bytes 28
  39.4 23.9 %copy-start.9 = (bf16[4,128,1536]{2,1,0:T(8,128)(2,1)}, bf16[4,128,1536]{2,1,0:T(8,128)(2,1)S(1)}, u32[]{:S(2)}) copy-start(bf16[4,128,1536]{2,1,0:T(8,128)(2,1)S(1)} %all-to-all-done.refs_1_.refs_3_) | copy-start | bytes 4718596
  40.5 22.7 %copy-start.13 = (bf16[4,48,1536]{2,1,0:T(8,128)(2,1)}, bf16[4,48,1536]{2,1,0:T(8,128)(2,1)S(1)}, u32[]{:S(2)}) copy-start(bf16[4,48,1536]{2,1,0:T(8,128)(2,1)S(1)} %pad_maximum_fusion.1) | copy-start | bytes 1769476
  40.5 26.2 %collective-permute-start.3 = (bf16[4,48,1536]{2,1,0:T(8,128)(2,1)S(1)}, bf16[4,48,1536]{2,1,0:T(8,128)(2,1)S(1)}, u32[]{:S(2)}, u32[]{:S(2)}) collective-permute-start(bf16[4,48,1536]{2,1,0:T(8,128)(2,1)S(1)} %pad_maximum_fusion.1), channel_id=1, source_target_pairs={{0,8},{1,9},{2,10},{3,11},{4,12},{5,13},{6,14},{7,15},{8,0},{9,1},... | collective-permute-start | bytes 1769480 | tf_op jit(solution)/shard_map/ppermute | solution.py:447
  42.8 23.9 %collective-permute-start.4 = (bf16[4,48,1536]{2,1,0:T(8,128)(2,1)S(1)}, bf16[4,48,1536]{2,1,0:T(8,128)(2,1)}, u32[]{:S(2)}, u32[]{:S(2)}) collective-permute-start(bf16[4,48,1536]{2,1,0:T(8,128)(2,1)S(1)} %pad_maximum_fusion.1), channel_id=1, source_target_pairs={{0,16},{1,17},{2,18},{3,19},{4,20},{5,21},{6,22},{7,23},{8,24},{9,... | collective-permute-start | bytes 1769480 | tf_op jit(solution)/shard_map/ppermute | solution.py:447
  44.3 22.4 %collective-permute-start.5 = (bf16[4,48,1536]{2,1,0:T(8,128)(2,1)S(1)}, bf16[4,48,1536]{2,1,0:T(8,128)(2,1)}, u32[]{:S(2)}, u32[]{:S(2)}) collective-permute-start(bf16[4,48,1536]{2,1,0:T(8,128)(2,1)S(1)} %pad_maximum_fusion.1), channel_id=1, source_target_pairs={{0,24},{1,25},{2,26},{3,27},{4,28},{5,29},{6,30},{7,31},{8,16},{9,... | collective-permute-start | bytes 1769480 | tf_op jit(solution)/shard_map/ppermute | solution.py:447
  45.6 20.5 %all-to-all-start.1 = ((bf16[32,1,96]{2,1,0:T(2,128)(2,1)}), bf16[32,1,96]{2,1,0:T(2,128)(2,1)S(1)}, u32[]{:S(2)}, u32[]{:S(2)}) async-start(bf16[32,1,96]{2,1,0:T(2,128)(2,1)} %copy.46), calls=%async_computation.1 | async-start | bytes 32768 | tf_op jit(solution)/shard_map/all_to_all | solution.py:461
  59.0 78.4 %all-gather.7.cloned.1.call-start = ((), (), s32[]{:S(2)}) async-start(), calls=%async_computation.7 | async-start | bytes 10616832 | tf_op jit(solution)/shard_map/all_gather | solution.py:535
  68.0 46.8 %all-to-all-start.2 = ((bf16[4,128,1536]{2,1,0:T(8,128)(2,1)}), bf16[4,128,1536]{2,1,0:T(8,128)(2,1)S(1)}, u32[]{:S(2)}, u32[]{:S(2)}) async-start(bf16[4,128,1536]{2,1,0:T(8,128)(2,1)} %tile.48), calls=%async_computation.2 | async-start | bytes 3145728 | tf_op jit(solution)/shard_map/all_to_all | solution.py:461
  77.6 170.1 %all-gather.9.cloned.1.call-start = ((), (), s32[]{:S(2)}) async-start(), calls=%async_computation.9 | async-start | bytes 1966080 | tf_op jit(solution)/shard_map/all_gather | solution.py:584
  89.5 25.6 %collective-permute-start.9 = (bf16[16,48,1536]{2,1,0:T(8,128)(2,1)}, bf16[16,48,1536]{2,1,0:T(8,128)(2,1)}, u32[]{:S(2)}, u32[]{:S(2)}) collective-permute-start(bf16[16,48,1536]{2,1,0:T(8,128)(2,1)} %bitcast.16.refs_4_), channel_id=1, source_target_pairs={{0,1},{1,0},{2,3},{3,2},{4,5},{5,4},{6,7},{7,6},{8,9},{9,8},{10,11... | collective-permute-start | bytes 7077896 | tf_op jit(solution)/shard_map/ppermute | solution.py:447
  89.5 11.3 %collective-permute-start.6 = (bf16[128,768]{1,0:T(8,128)(2,1)S(1)}, bf16[128,768]{1,0:T(8,128)(2,1)S(1)}, u32[]{:S(2)}, u32[]{:S(2)}) collective-permute-start(bf16[128,768]{1,0:T(8,128)(2,1)S(1)} %copy-done.43), channel_id=1, source_target_pairs={{0,8},{1,9},{2,10},{3,11},{4,12},{5,13},{6,14},{7,15},{8,0},{9,1},... | collective-permute-start | bytes 589832 | tf_op jit(solution)/shard_map/ppermute | solution.py:447
  90.5 10.7 %collective-permute-start.7 = (bf16[128,768]{1,0:T(8,128)(2,1)S(1)}, bf16[128,768]{1,0:T(8,128)(2,1)S(1)}, u32[]{:S(2)}, u32[]{:S(2)}) collective-permute-start(bf16[128,768]{1,0:T(8,128)(2,1)S(1)} %copy-done.42), channel_id=1, source_target_pairs={{0,16},{1,17},{2,18},{3,19},{4,20},{5,21},{6,22},{7,23},{8,24},{9,... | collective-permute-start | bytes 589832 | tf_op jit(solution)/shard_map/ppermute | solution.py:447
  91.1 14.6 %collective-permute-start.8 = (bf16[128,768]{1,0:T(8,128)(2,1)S(1)}, bf16[128,768]{1,0:T(8,128)(2,1)S(1)}, u32[]{:S(2)}, u32[]{:S(2)}) collective-permute-start(bf16[128,768]{1,0:T(8,128)(2,1)S(1)} %copy-done.41), channel_id=1, source_target_pairs={{0,24},{1,25},{2,26},{3,27},{4,28},{5,29},{6,30},{7,31},{8,16},{9,... | collective-permute-start | bytes 589832 | tf_op jit(solution)/shard_map/ppermute | solution.py:447
  114.8 182.5 %reduce-scatter.2.cloned.1.call-start = ((), (), s32[]{:S(2)}) async-start(), calls=%async_computation.8 | async-start | bytes 10616832 | tf_op jit(solution)/shard_map/reduce_scatter | solution.py:619
  115.1 22.4 %copy-start.4 = (s32[3]{0:T(128)S(1)}, s32[3]{0:T(128)}, u32[]{:S(2)}) copy-start(s32[3]{0:T(128)} %pad_add_fusion.refs_0_) | copy-start | bytes 40
  123.8 22.3 %collective-permute-start.10 = (bf16[128,1536]{1,0:T(8,128)(2,1)}, bf16[128,1536]{1,0:T(8,128)(2,1)S(1)}, u32[]{:S(2)}, u32[]{:S(2)}) collective-permute-start(bf16[128,1536]{1,0:T(8,128)(2,1)} %get-tuple-element.198.refs_0_), channel_id=1, source_target_pairs={{0,2},{1,3},{2,0},{3,1},{4,6},{5,7},{6,4},{7,5},{8,10},{9,11},{10,... | collective-permute-start | bytes 1179656 | tf_op jit(solution)/shard_map/ppermute | solution.py:447
  123.9 30.1 %collective-permute-start.11 = (bf16[128,1536]{1,0:T(8,128)(2,1)}, bf16[128,1536]{1,0:T(8,128)(2,1)S(1)}, u32[]{:S(2)}, u32[]{:S(2)}) collective-permute-start(bf16[128,1536]{1,0:T(8,128)(2,1)} %get-tuple-element.198.refs_0_), channel_id=1, source_target_pairs={{0,4},{1,5},{2,6},{3,7},{4,0},{5,1},{6,2},{7,3},{8,12},{9,13},{10,... | collective-permute-start | bytes 1179656 | tf_op jit(solution)/shard_map/ppermute | solution.py:447
  125.7 28.2 %collective-permute-start.12 = (bf16[128,1536]{1,0:T(8,128)(2,1)}, bf16[128,1536]{1,0:T(8,128)(2,1)S(1)}, u32[]{:S(2)}, u32[]{:S(2)}) collective-permute-start(bf16[128,1536]{1,0:T(8,128)(2,1)} %get-tuple-element.198.refs_0_), channel_id=1, source_target_pairs={{0,6},{1,7},{2,4},{3,5},{4,2},{5,3},{6,0},{7,1},{8,14},{9,15},{10,... | collective-permute-start | bytes 1179656 | tf_op jit(solution)/shard_map/ppermute | solution.py:447
  176.3 20.9 %collective-permute-start.13 = (bf16[128,1536]{1,0:T(8,128)(2,1)S(1)}, bf16[128,1536]{1,0:T(8,128)(2,1)S(1)}, u32[]{:S(2)}, u32[]{:S(2)}) collective-permute-start(bf16[128,1536]{1,0:T(8,128)(2,1)S(1)} %copy-done.7), channel_id=1, source_target_pairs={{0,2},{1,3},{2,0},{3,1},{4,6},{5,7},{6,4},{7,5},{8,10},{9,11},{10,... | collective-permute-start | bytes 1179656 | tf_op jit(solution)/shard_map/ppermute | solution.py:447
  183.4 34.0 %collective-permute-start.14 = (bf16[128,1536]{1,0:T(8,128)(2,1)S(1)}, bf16[128,1536]{1,0:T(8,128)(2,1)S(1)}, u32[]{:S(2)}, u32[]{:S(2)}) collective-permute-start(bf16[128,1536]{1,0:T(8,128)(2,1)S(1)} %get-tuple-element.214), channel_id=1, source_target_pairs={{0,4},{1,5},{2,6},{3,7},{4,0},{5,1},{6,2},{7,3},{8,12},{9,13},{10,... | collective-permute-start | bytes 1179656 | tf_op jit(solution)/shard_map/ppermute | solution.py:447
  183.4 34.0 %collective-permute-start.15 = (bf16[128,1536]{1,0:T(8,128)(2,1)S(1)}, bf16[128,1536]{1,0:T(8,128)(2,1)S(1)}, u32[]{:S(2)}, u32[]{:S(2)}) collective-permute-start(bf16[128,1536]{1,0:T(8,128)(2,1)S(1)} %get-tuple-element.215), channel_id=1, source_target_pairs={{0,6},{1,7},{2,4},{3,5},{4,2},{5,3},{6,0},{7,1},{8,14},{9,15},{10,... | collective-permute-start | bytes 1179656 | tf_op jit(solution)/shard_map/ppermute | solution.py:447
  197.2 21.7 %copy-start.38 = (bf16[128,1536]{1,0:T(8,128)(2,1)}, bf16[128,1536]{1,0:T(8,128)(2,1)S(1)}, u32[]{:S(2)}) copy-start(bf16[128,1536]{1,0:T(8,128)(2,1)S(1)} %collective-permute-done.13.refs_2_) | copy-start | bytes 1179652
  217.4 11.1 %collective-permute-start.16 = (bf16[128,1536]{1,0:T(8,128)(2,1)S(1)}, bf16[128,1536]{1,0:T(8,128)(2,1)S(1)}, u32[]{:S(2)}, u32[]{:S(2)}) collective-permute-start(bf16[128,1536]{1,0:T(8,128)(2,1)S(1)} %get-tuple-element.226), channel_id=1, source_target_pairs={{0,6},{1,7},{2,4},{3,5},{4,2},{5,3},{6,0},{7,1},{8,14},{9,15},{10,... | collective-permute-start | bytes 1179656 | tf_op jit(solution)/shard_map/ppermute | solution.py:447
  228.5 19.1 %all-to-all-start.3 = ((bf16[4,128,768]{2,1,0:T(8,128)(2,1)}), bf16[4,128,768]{2,1,0:T(8,128)(2,1)S(1)}, u32[]{:S(2)}, u32[]{:S(2)}) async-start(bf16[4,128,768]{2,1,0:T(8,128)(2,1)} %get-tuple-element.227), calls=%async_computation.3 | async-start | bytes 1572864 | tf_op jit(solution)/shard_map/all_to_all | solution.py:461
  232.7 13.7 %collective-permute-start.17 = (bf16[128,384]{1,0:T(8,128)(2,1)}, bf16[128,384]{1,0:T(8,128)(2,1)S(1)}, u32[]{:S(2)}, u32[]{:S(2)}) collective-permute-start(bf16[128,384]{1,0:T(8,128)(2,1)} %get-tuple-element.229), channel_id=1, source_target_pairs={{0,8},{1,9},{2,10},{3,11},{4,12},{5,13},{6,14},{7,15},{8,0},{9,1},... | collective-permute-start | bytes 294920 | tf_op jit(solution)/shard_map/ppermute | solution.py:447
  234.4 12.0 %collective-permute-start.18 = (bf16[128,384]{1,0:T(8,128)(2,1)}, bf16[128,384]{1,0:T(8,128)(2,1)S(1)}, u32[]{:S(2)}, u32[]{:S(2)}) collective-permute-start(bf16[128,384]{1,0:T(8,128)(2,1)} %get-tuple-element.230), channel_id=1, source_target_pairs={{0,16},{1,17},{2,18},{3,19},{4,20},{5,21},{6,22},{7,23},{8,24},{9,... | collective-permute-start | bytes 294920 | tf_op jit(solution)/shard_map/ppermute | solution.py:447
  235.9 11.8 %collective-permute-start.19 = (bf16[128,384]{1,0:T(8,128)(2,1)}, bf16[128,384]{1,0:T(8,128)(2,1)}, u32[]{:S(2)}, u32[]{:S(2)}) collective-permute-start(bf16[128,384]{1,0:T(8,128)(2,1)} %get-tuple-element.231), channel_id=1, source_target_pairs={{0,24},{1,25},{2,26},{3,27},{4,28},{5,29},{6,30},{7,31},{8,16},{9,... | collective-permute-start | bytes 294920 | tf_op jit(solution)/shard_map/ppermute | solution.py:447
  236.2 25.1 %collective-permute-start.21 = (bf16[128,1536]{1,0:T(8,128)(2,1)S(1)}, bf16[128,1536]{1,0:T(8,128)(2,1)S(1)}, u32[]{:S(2)}, u32[]{:S(2)}) collective-permute-start(bf16[128,1536]{1,0:T(8,128)(2,1)S(1)} %get-tuple-element.240), channel_id=1, source_target_pairs={{0,2},{1,3},{2,0},{3,1},{4,6},{5,7},{6,4},{7,5},{8,10},{9,11},{10,... | collective-permute-start | bytes 1179656 | tf_op jit(solution)/shard_map/ppermute | solution.py:447
  245.6 15.8 %collective-permute-start.22 = (bf16[128,1536]{1,0:T(8,128)(2,1)S(1)}, bf16[128,1536]{1,0:T(8,128)(2,1)}, u32[]{:S(2)}, u32[]{:S(2)}) collective-permute-start(bf16[128,1536]{1,0:T(8,128)(2,1)S(1)} %get-tuple-element.241), channel_id=1, source_target_pairs={{0,4},{1,5},{2,6},{3,7},{4,0},{5,1},{6,2},{7,3},{8,12},{9,13},{10,... | collective-permute-start | bytes 1179656 | tf_op jit(solution)/shard_map/ppermute | solution.py:447
  255.9 5.5 %collective-permute-start.20 = (bf16[4,144,1536]{2,1,0:T(8,128)(2,1)}, bf16[4,144,1536]{2,1,0:T(8,128)(2,1)}, u32[]{:S(2)}, u32[]{:S(2)}) collective-permute-start(bf16[4,144,1536]{2,1,0:T(8,128)(2,1)} %get-tuple-element.238), channel_id=1, source_target_pairs={{0,1},{1,0},{2,3},{3,2},{4,5},{5,4},{6,7},{7,6},{8,9},{9,8},{10,11... | collective-permute-start | bytes 5308424 | tf_op jit(solution)/shard_map/ppermute | solution.py:447
  261.3 16.4 %copy-start.24 = (f32[128,1536]{1,0:T(8,128)S(1)}, f32[128,1536]{1,0:T(8,128)}, u32[]{:S(2)}) copy-start(f32[128,1536]{1,0:T(8,128)} %get-tuple-element.193.refs_5_) | copy-start | bytes 2359300
  261.3 16.4 %copy-start.31 = (pred[128]{0:T(512)(128)(4,1)S(1)}, pred[128]{0:T(512)(128)(4,1)}, u32[]{:S(2)}) copy-start(pred[128]{0:T(512)(128)(4,1)} %lt.33) | copy-start | bytes 388
  265.4 44.3 %collective-permute-start.26 = (bf16[144,1536]{1,0:T(8,128)(2,1)}, bf16[144,1536]{1,0:T(8,128)(2,1)S(1)}, u32[]{:S(2)}, u32[]{:S(2)}) collective-permute-start(bf16[144,1536]{1,0:T(8,128)(2,1)} %get-tuple-element.264), channel_id=1, source_target_pairs={{0,2},{1,3},{2,0},{3,1},{4,6},{5,7},{6,4},{7,5},{8,10},{9,11},{10,... | collective-permute-start | bytes 1327112 | tf_op jit(solution)/shard_map/ppermute | solution.py:447
  270.4 39.4 %collective-permute-start.27 = (bf16[144,1536]{1,0:T(8,128)(2,1)}, bf16[144,1536]{1,0:T(8,128)(2,1)}, u32[]{:S(2)}, u32[]{:S(2)}) collective-permute-start(bf16[144,1536]{1,0:T(8,128)(2,1)} %get-tuple-element.265), channel_id=1, source_target_pairs={{0,4},{1,5},{2,6},{3,7},{4,0},{5,1},{6,2},{7,3},{8,12},{9,13},{10,... | collective-permute-start | bytes 1327112 | tf_op jit(solution)/shard_map/ppermute | solution.py:447
  271.2 38.5 %all-to-all-start.4 = ((f32[32,1,96]{2,1,0:T(1,128)}), f32[32,1,96]{2,1,0:T(1,128)S(1)}, u32[]{:S(2)}, u32[]{:S(2)}) async-start(f32[32,1,96]{2,1,0:T(1,128)} %bitcast.22), calls=%async_computation.4 | async-start | bytes 32768 | tf_op jit(solution)/shard_map/all_to_all | solution.py:461
  274.1 21.5 %copy-start.11 = (f32[128,1536]{1,0:T(8,128)S(1)}, f32[128,1536]{1,0:T(8,128)}, u32[]{:S(2)}) copy-start(f32[128,1536]{1,0:T(8,128)} %get-tuple-element.259) | copy-start | bytes 2359300
  274.1 12.2 %collective-permute-start.23 = (bf16[128,1536]{1,0:T(8,128)(2,1)}, bf16[128,1536]{1,0:T(8,128)(2,1)S(1)}, u32[]{:S(2)}, u32[]{:S(2)}) collective-permute-start(bf16[128,1536]{1,0:T(8,128)(2,1)} %get-tuple-element.260), channel_id=1, source_target_pairs={{0,8},{1,9},{2,10},{3,11},{4,12},{5,13},{6,14},{7,15},{8,0},{9,1},... | collective-permute-start | bytes 1179656 | tf_op jit(solution)/shard_map/ppermute | solution.py:447
  276.0 19.6 %collective-permute-start.24 = (bf16[128,1536]{1,0:T(8,128)(2,1)}, bf16[128,1536]{1,0:T(8,128)(2,1)S(1)}, u32[]{:S(2)}, u32[]{:S(2)}) collective-permute-start(bf16[128,1536]{1,0:T(8,128)(2,1)} %get-tuple-element.261), channel_id=1, source_target_pairs={{0,16},{1,17},{2,18},{3,19},{4,20},{5,21},{6,22},{7,23},{8,24},{9,... | collective-permute-start | bytes 1179656 | tf_op jit(solution)/shard_map/ppermute | solution.py:447
  277.4 18.2 %collective-permute-start.25 = (bf16[128,1536]{1,0:T(8,128)(2,1)}, bf16[128,1536]{1,0:T(8,128)(2,1)S(1)}, u32[]{:S(2)}, u32[]{:S(2)}) collective-permute-start(bf16[128,1536]{1,0:T(8,128)(2,1)} %get-tuple-element.262), channel_id=1, source_target_pairs={{0,24},{1,25},{2,26},{3,27},{4,28},{5,29},{6,30},{7,31},{8,16},{9,... | collective-permute-start | bytes 1179656 | tf_op jit(solution)/shard_map/ppermute | solution.py:447
  286.4 23.3 %collective-permute-start.28 = (bf16[144,1536]{1,0:T(8,128)(2,1)}, bf16[144,1536]{1,0:T(8,128)(2,1)}, u32[]{:S(2)}, u32[]{:S(2)}) collective-permute-start(bf16[144,1536]{1,0:T(8,128)(2,1)} %get-tuple-element.266), channel_id=1, source_target_pairs={{0,6},{1,7},{2,4},{3,5},{4,2},{5,3},{6,0},{7,1},{8,14},{9,15},{10,... | collective-permute-start | bytes 1327112 | tf_op jit(solution)/shard_map/ppermute | solution.py:447
  (36 other events, 160.1 us)
Sparse Core Ops, SparseCore 0:
  10.3 44.1 all-gather.4
  68.1 69.2 all-gather.6
  139.9 30.9 all-gather.8
  175.5 89.2 reduce-scatter.1

commit v4 on v3

--- a/solution.py
+++ b/solution.py
@@ -32,6 +32,7 @@
 VMEM_ALL = 60 * 1024 * 1024
 TILE = 256
 SHORT = 30_000_000_000
+LONG = 300_000_000_000
 
 bf16 = jnp.bfloat16
 f32 = jnp.float32
@@ -81,7 +82,9 @@
     return ref
 
 
-def kernel_call(body, outs, ins, smem=(), hbm=(), late=(), scratch=(), sems=(), shared=False, flops=0):
+def kernel_call(
+    body, outs, ins, smem=(), hbm=(), late=(), far=(), scratch=(), sems=(), shared=False, flops=0
+):
     moved = [i for i in range(len(ins)) if i not in smem and i not in hbm]
 
     def fetched(*refs):
@@ -100,7 +103,8 @@
                 copies[j].wait()
         body(*given, *rest[: -1 - len(moved)])
 
-    arrays = [*outs, *((ins[i].shape, ins[i].dtype) for i in moved)]
+    arrays = [v for i, v in enumerate(outs) if i not in far]
+    arrays += [*((ins[i].shape, ins[i].dtype) for i in moved)]
     arrays += scratch
     held_bytes = sum(math.prod(s) * jnp.dtype(t).itemsize for s, t in arrays)
     outputs = pl.pallas_call(
@@ -110,7 +114,10 @@
             pl.BlockSpec(memory_space=pltpu.SMEM if i in smem else pltpu.HBM)
             for i in range(len(ins))
         ],
-        out_specs=[pl.BlockSpec(memory_space=pltpu.VMEM)] * len(outs),
+        out_specs=[
+            pl.BlockSpec(memory_space=pltpu.HBM if i in far else pltpu.VMEM)
+            for i in range(len(outs))
+        ],
         scratch_shapes=[
             *(pltpu.VMEM(s, t) for s, t in scratch),
             *(pltpu.SemaphoreType.DMA(s) for s in sems),
@@ -179,18 +186,29 @@
     att_ref[...] = low(jnp.concatenate(outs, axis=1))
 
 
+def place_copies(n_z, at_ref, parts, wo_ref, sem):
+    if len(parts) == 1:
+        return [pltpu.make_async_copy(parts[0], wo_ref, sem)]
+    copies = []
+    for c, part in enumerate(parts):
+        for k in range(part.shape[0]):
+            to = (at_ref[0] ^ (k // n_z)) * n_z + (at_ref[1] ^ (k % n_z))
+            to = to * 2 + (at_ref[2] ^ c)
+            copies.append(pltpu.make_async_copy(part.at[k], wo_ref.at[to], sem))
+    return copies
+
+
+def place_body(n_z, at_ref, *refs):
+    copies = place_copies(n_z, at_ref, refs[:-2], refs[-2], refs[-1])
+    for copy in copies:
+        copy.start()
+    for copy in copies:
+        copy.wait()
+
+
 def out_body(n_z, at_ref, att_ref, x_ref, gain_ref, *refs):
-    hidden_ref, normed_ref, wo_ref, sem = refs[-4:]
-    parts = refs[:-4]
-    copies = []
-    if len(parts) == 1:
-        copies.append(pltpu.make_async_copy(parts[0], wo_ref, sem))
-    else:
-        for c, part in enumerate(parts):
-            for k in range(part.shape[0]):
-                to = (at_ref[0] ^ (k // n_z)) * n_z + (at_ref[1] ^ (k % n_z))
-                to = to * 2 + (at_ref[2] ^ c)
-                copies.append(pltpu.make_async_copy(part.at[k], wo_ref.at[to], sem))
+    parts, (hidden_ref, normed_ref, wo_ref, sem) = refs[:-4], refs[-4:]
+    copies = place_copies(n_z, at_ref, parts, wo_ref, sem)
     for copy in copies:
         copy.start()
     for copy in copies:
@@ -414,19 +432,24 @@
             ref[...] = value
 
 
-def pack_body(gate_ref, down_ref, out_ref):
+def pack_body(gate_ref, down_ref, up_ref, out_ref, copies_ref):
+    for k in range(copies_ref.shape[0]):
+        copies_ref[k] = up_ref[...]
     out_ref[0] = low(gate_ref[0].T)
     out_ref[1] = low(gate_ref[1].T)
     out_ref[2] = low(down_ref[...])
 
 
-def update_body(rate, flip, n, *refs):
-    grad_ref, refs = refs[0], refs[1:]
-    for i in range(n):
-        weight, moment, average = (r[i] for r in refs[:3])
-        gradient = wide(grad_ref[i].T if flip else grad_ref[i])
-        for ref, value in zip(refs[3:], update(weight, gradient, moment, average, rate)):
-            ref[i] = value
+def update_body(rate, grad_ref, *refs):
+    ins, outs = refs[:6], refs[6:]
+    for p in range(2):
+        weight, moment, average = (r[p] for r in ins[:3])
+        gradient = wide(grad_ref[p].T)
+        for ref, value in zip(outs[:5], update(weight, gradient, moment, average, rate)):
+            ref[p] = value
+    weight, moment, average = (r[...] for r in ins[3:])
+    for ref, value in zip(outs[5:], update(weight, wide(grad_ref[2]), moment, average, rate)):
+        ref[...] = value
 
 
 def update(weight, gradient, moment, average, step_rate):
@@ -447,10 +470,11 @@
         return lax.ppermute(values, AXES, [(i, i ^ mask) for i in range(self.count)])
 
     def gather(self, values, masks):
-        return [values] + [self.send(values, m) for m in masks[1:]]
+        return self.spread([values] * len(masks), masks)
 
     def spread(self, blocks, masks):
-        return [blocks[0]] + [self.send(b, m) for b, m in zip(blocks[1:], masks[1:])]
+        sent = [self.send(b, m) for b, m in reversed(list(zip(blocks[1:], masks[1:])))]
+        return [blocks[0]] + sent[::-1]
 
 
 def block_of(values, index):
@@ -518,27 +542,32 @@
     gain_all, cos_here, sine_here, cos_rows, sine_rows = tie(
         gain_all, cos_here, sine_here, cos_rows, sine_rows
     )
-    gain_all, token_group, out_z = tie(gain_all, token_group, out_z)
+    row_valid = (jnp.arange(seq_len)[None, :] < lengths[:, None]).reshape(rows, 1)
+    upstream = jnp.where(row_valid, cotangent.reshape(rows, D), jnp.zeros((), bf16))
+    ff_low, upstream_group = kernel_call(
+        pack_body,
+        [((3, ff_width, D), bf16), ((n_z, rows, D), bf16)],
+        [gate_up, down_proj, upstream],
+    )
+    gain_all, token_group, upstream_group = tie(gain_all, token_group, upstream_group)
     gain_all = exchange(gain_all, AXES)
     out_own = links.gather(jnp.stack(out_z), links.dp)
-    gain_all, out_own, in_group = tie(gain_all, out_own, in_group)
-    row_valid = (jnp.arange(seq_len)[None, :] < lengths[:, None]).reshape(rows, 1)
-    upstream = jnp.where(row_valid, cotangent.reshape(rows, D), jnp.zeros((), bf16))
-    upstream_group, in_group = tie(jnp.tile(upstream[None], (n_z, 1, 1)), in_group)
+    gain_all, in_group = tie(gain_all, in_group)
+    ff_low, in_group = tie(ff_low, in_group)
+    ff = lax.all_gather(ff_low, PLANE, axis=1, tiled=True)
+    upstream_group, in_group = tie(upstream_group, in_group)
     upstream_group = exchange(upstream_group, "z")
     if not aligned:
         gain_all = wide(gain_all).reshape(devices, 2, -1)
         gain_all = jnp.swapaxes(gain_all, 0, 1).reshape(2, D)
 
-    (ff_low,) = kernel_call(pack_body, [((3, ff_width, D), bf16)], [gate_up, down_proj])
-    ff_low, in_group = tie(ff_low, in_group)
-    ff = lax.all_gather(ff_low, PLANE, axis=1, tiled=True)
 
     normed_group, gain_rows, *blocks = kernel_call(
         project_body,
         [((n_dp, rows, D), bf16), ((2, D), f32)] + [((rows, group), bf16)] * n_dp,
         [at, token_group, in_group, gain_all, cos_here, sine_here],
         smem=(0,),
+        flops=LONG,
     )
     blocks = links.spread(blocks, links.dp)
     normed_group, out_own = tie(normed_group, out_own)
@@ -570,15 +599,15 @@
         smem=(0, 1),
     )
     attended, upstream_group = tie(attended, upstream_group)
-    hidden, normed_two, out_full = kernel_call(
+    hidden, normed_two = kernel_call(
         functools.partial(out_body, n_z),
-        [((rows, D), f32), ((rows, D), bf16), ((devices, out_width, D), bf16)],
+        [((rows, D), f32), ((rows, D), bf16)],
         [at, attended, token_rows, gain_rows, *out_parts],
         smem=(0,),
         hbm=range(4, 4 + len(out_parts)),
+        scratch=[((devices, out_width, D), bf16)],
         sems=[()],
     )
-    out_full = out_full.reshape(D, D)
 
     normed_parts = links.gather(normed_two, links.z)
     attended_group = lax.all_gather(attended, "dp", axis=0)
@@ -593,7 +622,17 @@
         sems=[(units // TILE,)],
         shared=True,
     )
-    normed_parts, grad_active = tie(normed_parts, grad_active)
+    out_parts, normed_two = tie(out_parts, normed_two)
+    (out_full,) = kernel_call(
+        functools.partial(place_body, n_z),
+        [((devices, out_width, D), bf16)],
+        [at, *out_parts],
+        smem=(0,),
+        hbm=range(1, 1 + len(out_parts)),
+        sems=[()],
+    )
+    out_full = out_full.reshape(D, D)
+    normed_parts, grad_active, out_full = tie(normed_parts, grad_active, out_full)
     normed_rows, active, grad_gate, grad_up, *grad_normed = kernel_call(
         functools.partial(units_body, n_z, TILE),
         [((group_rows, D), bf16)]
@@ -715,14 +754,6 @@
     )
 
 
-    def update_ff(grad, weight, moment, average, flip):
-        outs = [(weight.shape, f32)] * 4 + [(weight.shape, bf16)]
-        return kernel_call(
-            functools.partial(update_body, step_rate, flip, weight.shape[0]),
-            outs,
-            [grad, weight, moment, average],
-        )
-
     def settle(grads, *state):
         state = [jnp.transpose(v) for v in state]
         outs = kernel_call(
@@ -732,11 +763,13 @@
         )
         return [jnp.transpose(v) for v in outs]
 
-    new_gate_up = update_ff(grad_ff[:2], gate_up, gate_up_mom, gate_up_avg, True)
-    new_down = update(down_proj, wide(grad_ff[2]), down_proj_mom, down_proj_avg, step_rate)
-    grad_cols, grad_gains, new_gate_up, new_down = tie(
-        grad_cols, grad_gains, new_gate_up, new_down
-    )
+    state = [gate_up, gate_up_mom, gate_up_avg, down_proj, down_proj_mom, down_proj_avg]
+    new_ff = kernel_call(
+        functools.partial(update_body, step_rate),
+        [(v.shape, t) for v in state[::3] for t in (f32, f32, f32, f32, bf16)],
+        [grad_ff, *state],
+    )
+    grad_cols, grad_gains, new_ff = tie(grad_cols, grad_gains, new_ff)
     grad_gain = jnp.sum(grad_gains, axis=0).reshape(gains_pair.shape)
     new_gains = update(gains_pair, grad_gain, gains_mom, gains_avg, step_rate)
     new_cols = settle(
@@ -746,8 +779,7 @@
         produced.reshape(tokens.shape),
         grad_inputs.reshape(tokens.shape),
         *new_cols,
-        *new_gate_up,
-        *new_down,
+        *new_ff,
         *new_gains,
     )
 

time: 324 us -> 313 us (0.966); the launches traced: 322 us -> 307 us
  starting transfers between devices: 89.2 us -> 75.9 us
  Pallas kernels: 84.1 us -> 90.7 us
  local copies, waits for them, and re-layouts: 20.2 us -> 14.1 us
    all_to_all x5, starting transfers between devices: 35.1 us -> 18.9 us  [exchange(): return lax.all_to_all(values, axes, split_axis=0, concat_axis=0, tiled=True)]
    pallas_call x13 -> x14, Pallas kernels: 84.1 us -> 90.7 us  [kernel_call(): pl.pallas_call(fetched, out_shape=[jax.ShapeDtypeStruct(s, t) for s, t in...]
    all_to_all x5, waiting for transfers between devices: 5.94 us -> 12.4 us  [exchange(): return lax.all_to_all(values, axes, split_axis=0, concat_axis=0, tiled=True)]
    ppermute x29, waiting for transfers between devices: 80.9 us -> 76.8 us  [send(): lax.ppermute(values, AXES, [(i, i ^ mask) for i in range(self.count)])]
    all_gather x1, waiting for transfers between devices: 9.21 us -> 5.4 us  [on_device(): ff = lax.all_gather(ff_low, PLANE, axis=1, tiled=True)]
    unnamed x93 -> x91, local copies, waits for them, and re-layouts: 13.8 us -> 11.4 us
  transfers between devices with their start and end apart: 38 -> 38, of which waited for: 13 -> 13; matrix products, arithmetic and copies ran while one was open for 6% -> 5% of each run, Pallas kernels for 25% -> 28%
where the time goes in v4:
time: 313 us; the launch traced here: 307 us
  waiting for transfers between devices  95.3 us (30%)
  Pallas kernels  90.7 us (29%)
  starting transfers between devices  75.9 us (24%)
  other arithmetic  16.4 us (5%)
  between operations  14.5 us (5%)
  local copies, waits for them, and re-layouts  14.1 us (5%)
    pallas_call x14, Pallas kernels, kernel_call(): pl.pallas_call(fetched, out_shape=[jax.ShapeDtypeStruct(s, t) for s, t in...  90.7 us
    ppermute x29, waiting for transfers between devices, send(): lax.ppermute(values, AXES, [(i, i ^ mask) for i in range(self.count)])  76.8 us
    ppermute x29, starting transfers between devices, send(): lax.ppermute(values, AXES, [(i, i ^ mask) for i in range(self.count)])  56.7 us
    all_to_all x5, starting transfers between devices, exchange(): return lax.all_to_all(values, axes, split_axis=0, concat_axis=0, tiled=True)  18.9 us
    all_to_all x5, waiting for transfers between devices, exchange(): return lax.all_to_all(values, axes, split_axis=0, concat_axis=0, tiled=True)  12.4 us
    unnamed x91, local copies, waits for them, and re-layouts  11.4 us
  transfers between devices with their start and end apart: 38, of which 13 were waited for; matrix products, arithmetic and copies ran while one was open for 5% of the time, Pallas kernels for 28%

profile of v4, /device:TPU:0, one launch (start us, length us, event | category | flops | bytes accessed | tf_op | source)
XLA Modules:
  0.0 306.9 jit_solution(1937931891494770609)
XLA Ops:
  7.3 1.9 bitcast_convert_fusion.1
  10.8 4.0 %collective-permute-start.4 = (bf16[48,1536]{1,0:T(8,128)(2,1)}, bf16[48,1536]{1,0:T(8,128)(2,1)S(1)}, u32[]{:S(2)}, u32[]{:S(2)}) collective-permute-start(bf16[48,1536]{1,0:T(8,128)(2,1)} %bitcast_convert_fusion), channel_id=1, source_target_pairs={{0,4},{1,5},{2,6},{3,7},{4,0},{5,1},{6,2},{7,3},{8,12},{9,13},{10,... | collective-permute-start | bytes 442376 | tf_op jit(solution)/shard_map/ppermute | solution.py:470
  17.7 3.7 %all-to-all-start = ((bf16[4,128,1536]{2,1,0:T(8,128)(2,1)}), bf16[4,128,1536]{2,1,0:T(8,128)(2,1)S(1)}, u32[]{:S(2)}, u32[]{:S(2)}) async-start(bf16[4,128,1536]{2,1,0:T(8,128)(2,1)} %tile.41), calls=%async_computation | async-start | bytes 3145728 | tf_op jit(solution)/shard_map/all_to_all | solution.py:485
  22.4 1.8 bitcast_select_fusion.refs_2_.refs_7_
  25.3 3.6 %shard_map.385 = (bf16[3,128,1536]{2,1,0:T(8,128)(2,1)}, bf16[4,128,1536]{2,1,0:T(8,128)(2,1)}) custom-call(f32[2,1536,128]{2,1,0:T(8,128)} %refs_1_.5, f32[128,1536]{1,0:T(8,128)} %refs_4_.1, bf16[128,1536]{1,0:T(8,128)(2,1)} %bitcast_select_fusion.refs_2_.refs_7_), custom_call_target="tpu_custom_call" | custom-call | tf_op jit(solution)/shard_map/pallas_call | solution.py:110
  29.5 10.7 %all-to-all-done.refs_1_.refs_3_ = bf16[4,128,1536]{2,1,0:T(8,128)(2,1)S(1)} async-done(((bf16[4,128,1536]{2,1,0:T(8,128)(2,1)}), bf16[4,128,1536]{2,1,0:T(8,128)(2,1)S(1)}, u32[]{:S(2)}, u32[]{:S(2)}) %all-to-all-start) | async-done | bytes 1572896 | tf_op jit(solution)/shard_map/all_to_all | solution.py:485
  40.8 3.9 %all-to-all-start.1 = ((bf16[32,1,96]{2,1,0:T(2,128)(2,1)}), bf16[32,1,96]{2,1,0:T(2,128)(2,1)S(1)}, u32[]{:S(2)}, u32[]{:S(2)}) async-start(bf16[32,1,96]{2,1,0:T(2,128)(2,1)} %copy.46), calls=%async_computation.1 | async-start | bytes 32768 | tf_op jit(solution)/shard_map/all_to_all | solution.py:485
  44.8 1.9 pad_maximum_fusion.1
  46.7 1.8 collective-permute-start.6
  52.4 4.4 %all-to-all-start.2 = ((bf16[4,128,1536]{2,1,0:T(8,128)(2,1)}), bf16[4,128,1536]{2,1,0:T(8,128)(2,1)}, u32[]{:S(2)}, u32[]{:S(2)}) async-start(bf16[4,128,1536]{2,1,0:T(8,128)(2,1)} %get-tuple-element.182), calls=%async_computation.2 | async-start | bytes 3145728 | tf_op jit(solution)/shard_map/all_to_all | solution.py:485
  57.6 7.4 %shard_map.386 = (bf16[4,128,1536]{2,1,0:T(8,128)(2,1)}, f32[2,1536]{1,0:T(2,128)}, bf16[128,768]{1,0:T(8,128)(2,1)}, bf16[128,768]{1,0:T(8,128)(2,1)}, bf16[128...) custom-call(s32[3]{0:T(128)} %pad_add_fusion.refs_0_, bf16[4,128,1536]{2,1,0:T(8,128)(2,1)} %copy-done.11, ...), custom_call_target="tpu_custom_call" | custom-call | flops 299999985664 | tf_op jit(solution)/shard_map/pallas_call | solution.py:110
  65.1 11.3 %collective-permute-done.7 = bf16[4,48,1536]{2,1,0:T(8,128)(2,1)} collective-permute-done((bf16[4,48,1536]{2,1,0:T(8,128)(2,1)}, bf16[4,48,1536]{2,1,0:T(8,128)(2,1)}, u32[]{:S(2)}, u32[]{:S(2)}) %collective-permute-start.7) | collective-permute-done | bytes 589856 | tf_op jit(solution)/shard_map/ppermute | solution.py:470
  76.4 4.8 %collective-permute-done.8 = bf16[4,48,1536]{2,1,0:T(8,128)(2,1)} collective-permute-done((bf16[4,48,1536]{2,1,0:T(8,128)(2,1)}, bf16[4,48,1536]{2,1,0:T(8,128)(2,1)}, u32[]{:S(2)}, u32[]{:S(2)}) %collective-permute-start.8) | collective-permute-done | bytes 589856 | tf_op jit(solution)/shard_map/ppermute | solution.py:470
  81.2 2.0 pad_maximum_fusion
  83.2 2.3 collective-permute-start
  87.1 5.0 %collective-permute-done.refs_3_ = bf16[128,768]{1,0:T(8,128)(2,1)S(1)} collective-permute-done((bf16[128,768]{1,0:T(8,128)(2,1)S(1)}, bf16[128,768]{1,0:T(8,128)(2,1)S(1)}, u32[]{:S(2)}, u32[]{:S(2)}) %collective-permute-start) | collective-permute-done | bytes 196640 | tf_op jit(solution)/shard_map/ppermute | solution.py:470
  92.0 5.4 %collective-permute-done.1.refs_4_ = bf16[128,768]{1,0:T(8,128)(2,1)S(1)} collective-permute-done((bf16[128,768]{1,0:T(8,128)(2,1)S(1)}, bf16[128,768]{1,0:T(8,128)(2,1)S(1)}, u32[]{:S(2)}, u32[]{:S(2)}) %collective-permute-start.1) | collective-permute-done | bytes 196640 | tf_op jit(solution)/shard_map/ppermute | solution.py:470
  98.2 5.0 %shard_map.387 = (bf16[4,128,768]{2,1,0:T(8,128)(2,1)}, f32[8,256,128]{2,1,0:T(8,128)}, bf16[128,1536]{1,0:T(8,128)(2,1)}) custom-call(s32[3]{0:T(128)} %pad_add_fusion.refs_0_, s32[2]{0:T(128)} %refs_1_.4, bf16[128,768]{1,0:T(8,128)(2,1)} %get-tuple-element.177.refs_2_, bf16[128,768]{1,0:T(8,128)(2,1)} %copy-done.20, bf16[128,768]{1,0:T(8,128)(2,1)} %copy-done.21, ...), custom_call_target="tpu_custom_call" | custom-call | tf_op jit(solution)/shard_map/pallas_call | solution.py:110
  103.5 7.0 %shard_map.388 = (f32[128,1536]{1,0:T(8,128)}, bf16[128,1536]{1,0:T(8,128)(2,1)}) custom-call(s32[3]{0:T(128)} %pad_add_fusion.refs_0_, bf16[128,1536]{1,0:T(8,128)(2,1)} %get-tuple-element.183.refs_1_, bf16[128,1536]{1,0:T(8,128)(2,1)} %bitcast.57, f32[2,1536]{1,0:T(2,128)} %get-tuple-element.184.refs_3_.refs_6_, bf16[16,48,1536]{2,1,0:T(8,128)(2,1)} %bitcast.55, ...), custom_call_target="tpu_custom_call" | custom-call | tf_op jit(solution)/shard_map/pallas_call | solution.py:110
  112.1 2.4 collective-permute-start.11
  115.0 5.3 %shard_map.390 = bf16[32,48,1536]{2,1,0:T(8,128)(2,1)} custom-call(s32[3]{0:T(128)} %pad_add_fusion.refs_0_, bf16[16,48,1536]{2,1,0:T(8,128)(2,1)} %bitcast.56, bf16[16,48,1536]{2,1,0:T(8,128)(2,1)} %collective-permute-done.9.refs_5_.refs_2_), custom_call_target="tpu_custom_call" | custom-call | tf_op jit(solution)/shard_map/pallas_call | solution.py:110
  120.3 5.4 %all-gather.7.cloned.1.call-done.refs_2_.refs_4_.refs_5_ = bf16[3,1024,1536]{2,1,0:T(8,128)(2,1)} async-done(((bf16[3,128,1536]{2,1,0:T(8,128)(2,1)}), bf16[3,1024,1536]{2,1,0:T(8,128)(2,1)}) %all-gather.7.cloned.1.call-update) | async-done | bytes 9437200 | tf_op jit(solution)/shard_map/all_gather | solution.py:557
  125.7 3.7 %copy-done = bf16[3,1024,1536]{2,1,0:T(8,128)(2,1)S(1)} copy-done((bf16[3,1024,1536]{2,1,0:T(8,128)(2,1)S(1)}, bf16[3,1024,1536]{2,1,0:T(8,128)(2,1)}, u32[]{:S(2)}) %copy-start) | copy-done | bytes 9437208
  129.4 6.5 %shard_map.389 = (bf16[512,1536]{1,0:T(8,128)(2,1)S(1)}, f32[512,1024]{1,0:T(8,128)S(1)}) custom-call(s32[3]{0:T(128)S(1)} %copy-done.4, bf16[4,128,1536]{2,1,0:T(8,128)(2,1)} %all-to-all-done.2.refs_1_, bf16[3,1024,1536]{2,1,0:T(8,128)(2,1)S(1)} %copy-done), custom_call_target="tpu_custom_call" | custom-call | tf_op jit(solution)/shard_map/pallas_call | solution.py:110
  135.9 6.2 %collective-permute-done.11.refs_2_ = bf16[128,1536]{1,0:T(8,128)(2,1)S(1)} collective-permute-done((bf16[128,1536]{1,0:T(8,128)(2,1)}, bf16[128,1536]{1,0:T(8,128)(2,1)S(1)}, u32[]{:S(2)}, u32[]{:S(2)}) %collective-permute-start.11) | collective-permute-done | bytes 393248 | tf_op jit(solution)/shard_map/ppermute | solution.py:470
  142.1 9.2 %shard_map.391 = (bf16[512,1536]{1,0:T(8,128)(2,1)S(1)}, bf16[512,1024]{1,0:T(8,128)(2,1)S(1)}, bf16[512,1024]{1,0:T(8,128)(2,1)S(1)}, bf16[512,1024]{1,0:T(8,12...) custom-call(bf16[128,1536]{1,0:T(8,128)(2,1)S(1)} %copy-done.3, ...), custom_call_target="tpu_custom_call" | custom-call | tf_op jit(solution)/shard_map/pallas_call | solution.py:110
  152.1 7.6 %shard_map.392 = (bf16[3,1024,1536]{2,1,0:T(8,128)(2,1)S(1)}, f32[128,1536]{1,0:T(8,128)S(1)}, bf16[128,1536]{1,0:T(8,128)(2,1)S(1)}, bf16[128,1536]{1,0:T(8,128)(2,1)S(1)}, bf16[128,1536]{1,0:T(8,128)(2,1)S(1)}) custom-call(bf16[512,1024]{1,0:T(8,128)(2,1)S(1)} %get-tuple-element.202.refs_0_, bf16[512,1024]{1,0:T(8,128)(2,1)S(1)} %get-tuple-element.203.refs_1_, ...), custom_call_target="tpu_custom_call" | custom-call | tf_op jit(solution)/shard_map/pallas_call | solution.py:110
  159.7 3.7 %copy-done.2 = bf16[3,1024,1536]{2,1,0:T(8,128)(2,1)} copy-done((bf16[3,1024,1536]{2,1,0:T(8,128)(2,1)}, bf16[3,1024,1536]{2,1,0:T(8,128)(2,1)S(1)}, u32[]{:S(2)}) %copy-start.2) | copy-done | bytes 9437208
  163.5 7.5 %collective-permute-start.13 = (bf16[128,1536]{1,0:T(8,128)(2,1)S(1)}, bf16[128,1536]{1,0:T(8,128)(2,1)S(1)}, u32[]{:S(2)}, u32[]{:S(2)}) collective-permute-start(bf16[128,1536]{1,0:T(8,128)(2,1)S(1)} %get-tuple-element.212), channel_id=1, source_target_pairs={{0,2},{1,3},{2,0},{3,1},{4,6},{5,7},{6,4},{7,5},{8,10},{9,11},{10,... | collective-permute-start | bytes 1179656 | tf_op jit(solution)/shard_map/ppermute | solution.py:470
  173.4 12.3 %collective-permute-done.13.refs_2_ = bf16[128,1536]{1,0:T(8,128)(2,1)S(1)} collective-permute-done((bf16[128,1536]{1,0:T(8,128)(2,1)S(1)}, bf16[128,1536]{1,0:T(8,128)(2,1)S(1)}, u32[]{:S(2)}, u32[]{:S(2)}) %collective-permute-start.13) | collective-permute-done | bytes 393248 | tf_op jit(solution)/shard_map/ppermute | solution.py:470
  185.7 19.3 %collective-permute-done.14.refs_3_ = bf16[128,1536]{1,0:T(8,128)(2,1)S(1)} collective-permute-done((bf16[128,1536]{1,0:T(8,128)(2,1)S(1)}, bf16[128,1536]{1,0:T(8,128)(2,1)S(1)}, u32[]{:S(2)}, u32[]{:S(2)}) %collective-permute-start.14) | collective-permute-done | bytes 393248 | tf_op jit(solution)/shard_map/ppermute | solution.py:470
  205.0 2.4 collective-permute-start.16
  207.4 9.4 %shard_map.393 = (f32[128,1536]{1,0:T(8,128)}, bf16[128,1536]{1,0:T(8,128)(2,1)}, f32[1,1536]{1,0:T(1,128)}, bf16[4,128,768]{2,1,0:T(8,128)(2,1)}, bf16[128,384]...) custom-call(s32[3]{0:T(128)} %pad_add_fusion.refs_0_, ...), custom_call_target="tpu_custom_call" | custom-call | flops 30000001024 | tf_op jit(solution)/shard_map/pallas_call | solution.py:110
  217.6 3.8 %all-to-all-start.3 = ((bf16[4,128,768]{2,1,0:T(8,128)(2,1)}), bf16[4,128,768]{2,1,0:T(8,128)(2,1)S(1)}, u32[]{:S(2)}, u32[]{:S(2)}) async-start(bf16[4,128,768]{2,1,0:T(8,128)(2,1)} %get-tuple-element.226), calls=%async_computation.3 | async-start | bytes 1572864 | tf_op jit(solution)/shard_map/all_to_all | solution.py:485
  221.7 1.7 collective-permute-start.17
  225.2 9.6 %collective-permute-start.21 = (bf16[128,1536]{1,0:T(8,128)(2,1)S(1)}, bf16[128,1536]{1,0:T(8,128)(2,1)}, u32[]{:S(2)}, u32[]{:S(2)}) collective-permute-start(bf16[128,1536]{1,0:T(8,128)(2,1)S(1)} %get-tuple-element.239), channel_id=1, source_target_pairs={{0,2},{1,3},{2,0},{3,1},{4,6},{5,7},{6,4},{7,5},{8,10},{9,11},{10,... | collective-permute-start | bytes 1179656 | tf_op jit(solution)/shard_map/ppermute | solution.py:470
  236.4 7.6 %shard_map.394 = (f32[4,144,1536]{2,1,0:T(8,128)}, bf16[4,144,1536]{2,1,0:T(8,128)(2,1)}) custom-call(s32[3]{0:T(128)} %pad_add_fusion.refs_0_, bf16[4,128,768]{2,1,0:T(8,128)(2,1)} %copy-done.14, bf16[4,128,1536]{2,1,0:T(8,128)(2,1)} %get-tuple-element.232.refs_2_, bf16[4,128,1536]{2,1,0:T(8,128)(2,1)} %bitcast.72, ...), custom_call_target="tpu_custom_call" | custom-call | flops 30000001024 | tf_op jit(solution)/shard_map/pallas_call | solution.py:110
  244.1 5.3 %shard_map.395 = (f32[32,96]{1,0:T(8,128)}, f32[128,1536]{1,0:T(8,128)}, bf16[128,1536]{1,0:T(8,128)(2,1)}, bf16[128,1536]{1,0:T(8,128)(2,1)}, bf16[128,1536]{1,0:T(8,128)(2,1)}) custom-call(s32[3]{0:T(128)} %pad_add_fusion.refs_0_, bf16[4,128,768]{2,1,0:T(8,128)(2,1)} %copy-done.14, bf16[768,1536]{1,0:T(8,128)(2,1)} %all-gather.5.cloned.1.call-done.refs_2_, ...), custom_call_target="tpu_custom_call" | custom-call | flops 30000001024 | tf_op jit(solution)/shard_map/pallas_call | solution.py:110
  249.5 4.1 %shard_map.396 = (f32[144,1536]{1,0:T(8,128)}, bf16[144,1536]{1,0:T(8,128)(2,1)}, bf16[144,1536]{1,0:T(8,128)(2,1)}, bf16[144,1536]{1,0:T(8,128)(2,1)}) custom-call(f32[4,144,1536]{2,1,0:T(8,128)} %get-tuple-element.255.refs_0_, bf16[4,144,1536]{2,1,0:T(8,128)(2,1)} %collective-permute-done.20.refs_1_), custom_call_target="tpu_custom_call" | custom-call | tf_op jit(solution)/shard_map/pallas_call | solution.py:110
  253.6 6.0 %collective-permute-start.26 = (bf16[144,1536]{1,0:T(8,128)(2,1)}, bf16[144,1536]{1,0:T(8,128)(2,1)S(1)}, u32[]{:S(2)}, u32[]{:S(2)}) collective-permute-start(bf16[144,1536]{1,0:T(8,128)(2,1)} %get-tuple-element.263), channel_id=1, source_target_pairs={{0,2},{1,3},{2,0},{3,1},{4,6},{5,7},{6,4},{7,5},{8,10},{9,11},{10,... | collective-permute-start | bytes 1327112 | tf_op jit(solution)/shard_map/ppermute | solution.py:470
  259.8 3.2 %all-to-all-start.4 = ((f32[32,1,96]{2,1,0:T(1,128)}), f32[32,1,96]{2,1,0:T(1,128)S(1)}, u32[]{:S(2)}, u32[]{:S(2)}) async-start(f32[32,1,96]{2,1,0:T(1,128)} %bitcast.22), calls=%async_computation.4 | async-start | bytes 32768 | tf_op jit(solution)/shard_map/all_to_all | solution.py:485
  263.0 1.8 collective-permute-start.23
  266.6 2.2 select_convert_fusion
  268.8 6.4 %collective-permute-done.23 = bf16[128,1536]{1,0:T(8,128)(2,1)S(1)} collective-permute-done((bf16[128,1536]{1,0:T(8,128)(2,1)}, bf16[128,1536]{1,0:T(8,128)(2,1)S(1)}, u32[]{:S(2)}, u32[]{:S(2)}) %collective-permute-start.23) | collective-permute-done | bytes 393248 | tf_op jit(solution)/shard_map/ppermute | solution.py:470
  275.2 3.7 %collective-permute-start.28 = (bf16[144,1536]{1,0:T(8,128)(2,1)}, bf16[144,1536]{1,0:T(8,128)(2,1)S(1)}, u32[]{:S(2)}, u32[]{:S(2)}) collective-permute-start(bf16[144,1536]{1,0:T(8,128)(2,1)} %get-tuple-element.265), channel_id=1, source_target_pairs={{0,6},{1,7},{2,4},{3,5},{4,2},{5,3},{6,0},{7,1},{8,14},{9,15},{10,... | collective-permute-start | bytes 1327112 | tf_op jit(solution)/shard_map/ppermute | solution.py:470
  278.9 5.6 %collective-permute-done.24 = bf16[128,1536]{1,0:T(8,128)(2,1)S(1)} collective-permute-done((bf16[128,1536]{1,0:T(8,128)(2,1)}, bf16[128,1536]{1,0:T(8,128)(2,1)S(1)}, u32[]{:S(2)}, u32[]{:S(2)}) %collective-permute-start.24) | collective-permute-done | bytes 393248 | tf_op jit(solution)/shard_map/ppermute | solution.py:470
  286.2 8.0 %shard_map.397 = (f32[2,1536,128]{2,1,0:T(8,128)}, f32[2,1536,128]{2,1,0:T(8,128)}, f32[2,1536,128]{2,1,0:T(8,128)}, f32[2,1536,128]{2,1,0:T(8,128)}, bf16[2,153...) custom-call(bf16[3,128,1536]{2,1,0:T(8,128)(2,1)} %reduce-scatter.2., ...), custom_call_target="tpu_custom_call" | custom-call | tf_op jit(solution)/shard_map/pallas_call | solution.py:110
  295.6 4.7 %shard_map.398 = (f32[96,1536]{1,0:T(8,128)}, f32[96,1536]{1,0:T(8,128)}, f32[96,1536]{1,0:T(8,128)}, f32[96,1536]{1,0:T(8,128)}, bf16[96,1536]{1,0:T(8,128)(2,1...) custom-call(f32[144,1536]{1,0:T(8,128)} %get-tuple-element.278.refs_, ...), custom_call_target="tpu_custom_call" | custom-call | tf_op jit(solution)/shard_map/pallas_call | solution.py:110
  (172 shorter events, 30.2 us)
Async XLA Ops:
  7.2 45.2 %all-gather.5.cloned.1.call-start = ((), (), s32[]{:S(2)}) async-start(), calls=%async_computation.6 | async-start | bytes 2654208 | tf_op jit(solution)/shard_map/all_gather | solution.py:534
  10.8 34.0 %collective-permute-start.4 = (bf16[48,1536]{1,0:T(8,128)(2,1)}, bf16[48,1536]{1,0:T(8,128)(2,1)S(1)}, u32[]{:S(2)}, u32[]{:S(2)}) collective-permute-start(bf16[48,1536]{1,0:T(8,128)(2,1)} %bitcast_convert_fusion), channel_id=1, source_target_pairs={{0,4},{1,5},{2,6},{3,7},{4,0},{5,1},{6,2},{7,3},{8,12},{9,13},{10,... | collective-permute-start | bytes 442376 | tf_op jit(solution)/shard_map/ppermute | solution.py:470
  14.8 30.0 %collective-permute-start.5 = (bf16[48,1536]{1,0:T(8,128)(2,1)}, bf16[48,1536]{1,0:T(8,128)(2,1)}, u32[]{:S(2)}, u32[]{:S(2)}) collective-permute-start(bf16[48,1536]{1,0:T(8,128)(2,1)} %bitcast_convert_fusion), channel_id=1, source_target_pairs={{0,6},{1,7},{2,4},{3,5},{4,2},{5,3},{6,0},{7,1},{8,14},{9,15},{10,... | collective-permute-start | bytes 442376 | tf_op jit(solution)/shard_map/ppermute | solution.py:470
  16.2 28.6 %collective-permute-start.3 = (bf16[48,1536]{1,0:T(8,128)(2,1)}, bf16[48,1536]{1,0:T(8,128)(2,1)}, u32[]{:S(2)}, u32[]{:S(2)}) collective-permute-start(bf16[48,1536]{1,0:T(8,128)(2,1)} %bitcast_convert_fusion), channel_id=1, source_target_pairs={{0,2},{1,3},{2,0},{3,1},{4,6},{5,7},{6,4},{7,5},{8,10},{9,11},{10,... | collective-permute-start | bytes 442376 | tf_op jit(solution)/shard_map/ppermute | solution.py:470
  17.7 22.5 %all-to-all-start = ((bf16[4,128,1536]{2,1,0:T(8,128)(2,1)}), bf16[4,128,1536]{2,1,0:T(8,128)(2,1)S(1)}, u32[]{:S(2)}, u32[]{:S(2)}) async-start(bf16[4,128,1536]{2,1,0:T(8,128)(2,1)} %tile.41), calls=%async_computation | async-start | bytes 3145728 | tf_op jit(solution)/shard_map/all_to_all | solution.py:485
  40.2 12.2 %copy-start.11 = (bf16[4,128,1536]{2,1,0:T(8,128)(2,1)}, bf16[4,128,1536]{2,1,0:T(8,128)(2,1)S(1)}, u32[]{:S(2)}) copy-start(bf16[4,128,1536]{2,1,0:T(8,128)(2,1)S(1)} %all-to-all-done.refs_1_.refs_3_) | copy-start | bytes 4718596
  40.8 11.0 %all-to-all-start.1 = ((bf16[32,1,96]{2,1,0:T(2,128)(2,1)}), bf16[32,1,96]{2,1,0:T(2,128)(2,1)S(1)}, u32[]{:S(2)}, u32[]{:S(2)}) async-start(bf16[32,1,96]{2,1,0:T(2,128)(2,1)} %copy.46), calls=%async_computation.1 | async-start | bytes 32768 | tf_op jit(solution)/shard_map/all_to_all | solution.py:485
  46.7 18.4 %collective-permute-start.6 = (bf16[4,48,1536]{2,1,0:T(8,128)(2,1)}, bf16[4,48,1536]{2,1,0:T(8,128)(2,1)}, u32[]{:S(2)}, u32[]{:S(2)}) collective-permute-start(bf16[4,48,1536]{2,1,0:T(8,128)(2,1)} %pad_maximum_fusion.1), channel_id=1, source_target_pairs={{0,8},{1,9},{2,10},{3,11},{4,12},{5,13},{6,14},{7,15},{8,0},{9,1},... | collective-permute-start | bytes 1769480 | tf_op jit(solution)/shard_map/ppermute | solution.py:470
  48.4 28.0 %collective-permute-start.7 = (bf16[4,48,1536]{2,1,0:T(8,128)(2,1)}, bf16[4,48,1536]{2,1,0:T(8,128)(2,1)}, u32[]{:S(2)}, u32[]{:S(2)}) collective-permute-start(bf16[4,48,1536]{2,1,0:T(8,128)(2,1)} %pad_maximum_fusion.1), channel_id=1, source_target_pairs={{0,16},{1,17},{2,18},{3,19},{4,20},{5,21},{6,22},{7,23},{8,24},{9,... | collective-permute-start | bytes 1769480 | tf_op jit(solution)/shard_map/ppermute | solution.py:470
  49.9 31.3 %collective-permute-start.8 = (bf16[4,48,1536]{2,1,0:T(8,128)(2,1)}, bf16[4,48,1536]{2,1,0:T(8,128)(2,1)}, u32[]{:S(2)}, u32[]{:S(2)}) collective-permute-start(bf16[4,48,1536]{2,1,0:T(8,128)(2,1)} %pad_maximum_fusion.1), channel_id=1, source_target_pairs={{0,24},{1,25},{2,26},{3,27},{4,28},{5,29},{6,30},{7,31},{8,16},{9,... | collective-permute-start | bytes 1769480 | tf_op jit(solution)/shard_map/ppermute | solution.py:470
  52.4 50.8 %all-to-all-start.2 = ((bf16[4,128,1536]{2,1,0:T(8,128)(2,1)}), bf16[4,128,1536]{2,1,0:T(8,128)(2,1)}, u32[]{:S(2)}, u32[]{:S(2)}) async-start(bf16[4,128,1536]{2,1,0:T(8,128)(2,1)} %get-tuple-element.182), calls=%async_computation.2 | async-start | bytes 3145728 | tf_op jit(solution)/shard_map/all_to_all | solution.py:485
  56.8 68.9 %all-gather.7.cloned.1.call-start = ((), (), s32[]{:S(2)}) async-start(), calls=%async_computation.7 | async-start | bytes 10616832 | tf_op jit(solution)/shard_map/all_gather | solution.py:557
  57.5 178.0 %all-gather.9.cloned.1.call-start = ((), (), s32[]{:S(2)}) async-start(), calls=%async_computation.9 | async-start | bytes 1966080 | tf_op jit(solution)/shard_map/all_gather | solution.py:613
  83.1 20.4 %copy-start.6 = (bf16[4,4,48,1536]{3,2,1,0:T(8,128)(2,1)}, bf16[4,4,48,1536]{3,2,1,0:T(8,128)(2,1)S(1)}, u32[]{:S(2)}) copy-start(bf16[4,4,48,1536]{3,2,1,0:T(8,128)(2,1)S(1)} %pad_maximum_fusion) | copy-start | bytes 7077892
  83.1 20.4 %collective-permute-start.9 = (bf16[16,48,1536]{2,1,0:T(8,128)(2,1)S(1)}, bf16[16,48,1536]{2,1,0:T(8,128)(2,1)}, u32[]{:S(2)}, u32[]{:S(2)}) collective-permute-start(bf16[16,48,1536]{2,1,0:T(8,128)(2,1)S(1)} %bitcast.54), channel_id=1, source_target_pairs={{0,1},{1,0},{2,3},{3,2},{4,5},{5,4},{6,7},{7,6},{8,9},{9,8},{10,11... | collective-permute-start | bytes 7077896 | tf_op jit(solution)/shard_map/ppermute | solution.py:470
  83.2 8.8 %collective-permute-start = (bf16[128,768]{1,0:T(8,128)(2,1)S(1)}, bf16[128,768]{1,0:T(8,128)(2,1)S(1)}, u32[]{:S(2)}, u32[]{:S(2)}) collective-permute-start(bf16[128,768]{1,0:T(8,128)(2,1)S(1)} %copy-done.38), channel_id=1, source_target_pairs={{0,8},{1,9},{2,10},{3,11},{4,12},{5,13},{6,14},{7,15},{8,0},{9,1},... | collective-permute-start | bytes 589832 | tf_op jit(solution)/shard_map/ppermute | solution.py:470
  85.5 12.0 %collective-permute-start.1 = (bf16[128,768]{1,0:T(8,128)(2,1)S(1)}, bf16[128,768]{1,0:T(8,128)(2,1)S(1)}, u32[]{:S(2)}, u32[]{:S(2)}) collective-permute-start(bf16[128,768]{1,0:T(8,128)(2,1)S(1)} %copy-done.37), channel_id=1, source_target_pairs={{0,16},{1,17},{2,18},{3,19},{4,20},{5,21},{6,22},{7,23},{8,24},{9,... | collective-permute-start | bytes 589832 | tf_op jit(solution)/shard_map/ppermute | solution.py:470
  86.4 11.1 %collective-permute-start.2 = (bf16[128,768]{1,0:T(8,128)(2,1)S(1)}, bf16[128,768]{1,0:T(8,128)(2,1)S(1)}, u32[]{:S(2)}, u32[]{:S(2)}) collective-permute-start(bf16[128,768]{1,0:T(8,128)(2,1)S(1)} %copy-done.36), channel_id=1, source_target_pairs={{0,24},{1,25},{2,26},{3,27},{4,28},{5,29},{6,30},{7,31},{8,16},{9,... | collective-permute-start | bytes 589832 | tf_op jit(solution)/shard_map/ppermute | solution.py:470
  103.3 182.9 %reduce-scatter.2.cloned.1.call-start = ((), (), s32[]{:S(2)}) async-start(), calls=%async_computation.8 | async-start | bytes 10616832 | tf_op jit(solution)/shard_map/reduce_scatter | solution.py:658
  110.5 15.2 %copy-start.4 = (s32[3]{0:T(128)S(1)}, s32[3]{0:T(128)}, u32[]{:S(2)}) copy-start(s32[3]{0:T(128)} %pad_add_fusion.refs_0_) | copy-start | bytes 40
  110.5 25.4 %collective-permute-start.10 = (bf16[128,1536]{1,0:T(8,128)(2,1)}, bf16[128,1536]{1,0:T(8,128)(2,1)S(1)}, u32[]{:S(2)}, u32[]{:S(2)}) collective-permute-start(bf16[128,1536]{1,0:T(8,128)(2,1)} %get-tuple-element.197.refs_0_), channel_id=1, source_target_pairs={{0,2},{1,3},{2,0},{3,1},{4,6},{5,7},{6,4},{7,5},{8,10},{9,11},{10,... | collective-permute-start | bytes 1179656 | tf_op jit(solution)/shard_map/ppermute | solution.py:470
  112.1 30.0 %collective-permute-start.11 = (bf16[128,1536]{1,0:T(8,128)(2,1)}, bf16[128,1536]{1,0:T(8,128)(2,1)S(1)}, u32[]{:S(2)}, u32[]{:S(2)}) collective-permute-start(bf16[128,1536]{1,0:T(8,128)(2,1)} %get-tuple-element.197.refs_0_), channel_id=1, source_target_pairs={{0,4},{1,5},{2,6},{3,7},{4,0},{5,1},{6,2},{7,3},{8,12},{9,13},{10,... | collective-permute-start | bytes 1179656 | tf_op jit(solution)/shard_map/ppermute | solution.py:470
  114.5 27.6 %collective-permute-start.12 = (bf16[128,1536]{1,0:T(8,128)(2,1)}, bf16[128,1536]{1,0:T(8,128)(2,1)S(1)}, u32[]{:S(2)}, u32[]{:S(2)}) collective-permute-start(bf16[128,1536]{1,0:T(8,128)(2,1)} %get-tuple-element.197.refs_0_), channel_id=1, source_target_pairs={{0,6},{1,7},{2,4},{3,5},{4,2},{5,3},{6,0},{7,1},{8,14},{9,15},{10,... | collective-permute-start | bytes 1179656 | tf_op jit(solution)/shard_map/ppermute | solution.py:470
  129.4 12.7 %copy-start.1 = (bf16[3,1024,1536]{2,1,0:T(8,128)(2,1)S(1)}, bf16[3,1024,1536]{2,1,0:T(8,128)(2,1)}, u32[]{:S(2)}) copy-start(bf16[3,1024,1536]{2,1,0:T(8,128)(2,1)} %all-gather.7.cloned.1.call-done.refs_2_.refs_4_.refs_5_) | copy-start | bytes 28311556
  129.4 12.7 %copy-start.3 = (bf16[128,1536]{1,0:T(8,128)(2,1)S(1)}, bf16[128,1536]{1,0:T(8,128)(2,1)}, u32[]{:S(2)}) copy-start(bf16[128,1536]{1,0:T(8,128)(2,1)} %get-tuple-element.197.refs_0_) | copy-start | bytes 1179652
  163.5 22.2 %collective-permute-start.13 = (bf16[128,1536]{1,0:T(8,128)(2,1)S(1)}, bf16[128,1536]{1,0:T(8,128)(2,1)S(1)}, u32[]{:S(2)}, u32[]{:S(2)}) collective-permute-start(bf16[128,1536]{1,0:T(8,128)(2,1)S(1)} %get-tuple-element.212), channel_id=1, source_target_pairs={{0,2},{1,3},{2,0},{3,1},{4,6},{5,7},{6,4},{7,5},{8,10},{9,11},{10,... | collective-permute-start | bytes 1179656 | tf_op jit(solution)/shard_map/ppermute | solution.py:470
  170.9 34.0 %collective-permute-start.14 = (bf16[128,1536]{1,0:T(8,128)(2,1)S(1)}, bf16[128,1536]{1,0:T(8,128)(2,1)S(1)}, u32[]{:S(2)}, u32[]{:S(2)}) collective-permute-start(bf16[128,1536]{1,0:T(8,128)(2,1)S(1)} %get-tuple-element.213), channel_id=1, source_target_pairs={{0,4},{1,5},{2,6},{3,7},{4,0},{5,1},{6,2},{7,3},{8,12},{9,13},{10,... | collective-permute-start | bytes 1179656 | tf_op jit(solution)/shard_map/ppermute | solution.py:470
  171.9 33.0 %collective-permute-start.15 = (bf16[128,1536]{1,0:T(8,128)(2,1)S(1)}, bf16[128,1536]{1,0:T(8,128)(2,1)S(1)}, u32[]{:S(2)}, u32[]{:S(2)}) collective-permute-start(bf16[128,1536]{1,0:T(8,128)(2,1)S(1)} %get-tuple-element.214), channel_id=1, source_target_pairs={{0,6},{1,7},{2,4},{3,5},{4,2},{5,3},{6,0},{7,1},{8,14},{9,15},{10,... | collective-permute-start | bytes 1179656 | tf_op jit(solution)/shard_map/ppermute | solution.py:470
  185.7 21.7 %copy-start.33 = (bf16[128,1536]{1,0:T(8,128)(2,1)}, bf16[128,1536]{1,0:T(8,128)(2,1)S(1)}, u32[]{:S(2)}) copy-start(bf16[128,1536]{1,0:T(8,128)(2,1)S(1)} %collective-permute-done.13.refs_2_) | copy-start | bytes 1179652
  205.0 11.9 %collective-permute-start.16 = (bf16[128,1536]{1,0:T(8,128)(2,1)S(1)}, bf16[128,1536]{1,0:T(8,128)(2,1)S(1)}, u32[]{:S(2)}, u32[]{:S(2)}) collective-permute-start(bf16[128,1536]{1,0:T(8,128)(2,1)S(1)} %get-tuple-element.225), channel_id=1, source_target_pairs={{0,6},{1,7},{2,4},{3,5},{4,2},{5,3},{6,0},{7,1},{8,14},{9,15},{10,... | collective-permute-start | bytes 1179656 | tf_op jit(solution)/shard_map/ppermute | solution.py:470
  217.6 17.9 %all-to-all-start.3 = ((bf16[4,128,768]{2,1,0:T(8,128)(2,1)}), bf16[4,128,768]{2,1,0:T(8,128)(2,1)S(1)}, u32[]{:S(2)}, u32[]{:S(2)}) async-start(bf16[4,128,768]{2,1,0:T(8,128)(2,1)} %get-tuple-element.226), calls=%async_computation.3 | async-start | bytes 1572864 | tf_op jit(solution)/shard_map/all_to_all | solution.py:485
  221.7 13.4 %collective-permute-start.17 = (bf16[128,384]{1,0:T(8,128)(2,1)S(1)}, bf16[128,384]{1,0:T(8,128)(2,1)S(1)}, u32[]{:S(2)}, u32[]{:S(2)}) collective-permute-start(bf16[128,384]{1,0:T(8,128)(2,1)S(1)} %copy-done.41), channel_id=1, source_target_pairs={{0,8},{1,9},{2,10},{3,11},{4,12},{5,13},{6,14},{7,15},{8,0},{9,1},... | collective-permute-start | bytes 294920 | tf_op jit(solution)/shard_map/ppermute | solution.py:470
  223.4 11.7 %collective-permute-start.18 = (bf16[128,384]{1,0:T(8,128)(2,1)S(1)}, bf16[128,384]{1,0:T(8,128)(2,1)S(1)}, u32[]{:S(2)}, u32[]{:S(2)}) collective-permute-start(bf16[128,384]{1,0:T(8,128)(2,1)S(1)} %copy-done.40), channel_id=1, source_target_pairs={{0,16},{1,17},{2,18},{3,19},{4,20},{5,21},{6,22},{7,23},{8,24},{9,... | collective-permute-start | bytes 294920 | tf_op jit(solution)/shard_map/ppermute | solution.py:470
  224.9 10.7 %collective-permute-start.19 = (bf16[128,384]{1,0:T(8,128)(2,1)S(1)}, bf16[128,384]{1,0:T(8,128)(2,1)S(1)}, u32[]{:S(2)}, u32[]{:S(2)}) collective-permute-start(bf16[128,384]{1,0:T(8,128)(2,1)S(1)} %copy-done.39), channel_id=1, source_target_pairs={{0,24},{1,25},{2,26},{3,27},{4,28},{5,29},{6,30},{7,31},{8,16},{9,... | collective-permute-start | bytes 294920 | tf_op jit(solution)/shard_map/ppermute | solution.py:470
  225.2 24.3 %collective-permute-start.21 = (bf16[128,1536]{1,0:T(8,128)(2,1)S(1)}, bf16[128,1536]{1,0:T(8,128)(2,1)}, u32[]{:S(2)}, u32[]{:S(2)}) collective-permute-start(bf16[128,1536]{1,0:T(8,128)(2,1)S(1)} %get-tuple-element.239), channel_id=1, source_target_pairs={{0,2},{1,3},{2,0},{3,1},{4,6},{5,7},{6,4},{7,5},{8,10},{9,11},{10,... | collective-permute-start | bytes 1179656 | tf_op jit(solution)/shard_map/ppermute | solution.py:470
  234.8 14.7 %collective-permute-start.22 = (bf16[128,1536]{1,0:T(8,128)(2,1)S(1)}, bf16[128,1536]{1,0:T(8,128)(2,1)}, u32[]{:S(2)}, u32[]{:S(2)}) collective-permute-start(bf16[128,1536]{1,0:T(8,128)(2,1)S(1)} %get-tuple-element.240), channel_id=1, source_target_pairs={{0,4},{1,5},{2,6},{3,7},{4,0},{5,1},{6,2},{7,3},{8,12},{9,13},{10,... | collective-permute-start | bytes 1179656 | tf_op jit(solution)/shard_map/ppermute | solution.py:470
  244.0 5.5 %collective-permute-start.20 = (bf16[4,144,1536]{2,1,0:T(8,128)(2,1)}, bf16[4,144,1536]{2,1,0:T(8,128)(2,1)}, u32[]{:S(2)}, u32[]{:S(2)}) collective-permute-start(bf16[4,144,1536]{2,1,0:T(8,128)(2,1)} %get-tuple-element.237), channel_id=1, source_target_pairs={{0,1},{1,0},{2,3},{3,2},{4,5},{5,4},{6,7},{7,6},{8,9},{9,8},{10,11... | collective-permute-start | bytes 5308424 | tf_op jit(solution)/shard_map/ppermute | solution.py:470
  249.4 17.2 %copy-start.16 = (f32[128,1536]{1,0:T(8,128)S(1)}, f32[128,1536]{1,0:T(8,128)}, u32[]{:S(2)}) copy-start(f32[128,1536]{1,0:T(8,128)} %get-tuple-element.190.refs_5_) | copy-start | bytes 2359300
  249.4 17.1 %copy-start.26 = (pred[128]{0:T(512)(128)(4,1)S(1)}, pred[128]{0:T(512)(128)(4,1)}, u32[]{:S(2)}) copy-start(pred[128]{0:T(512)(128)(4,1)} %copy-done.25) | copy-start | bytes 388
  253.6 30.9 %copy-start.9 = (f32[128,1536]{1,0:T(8,128)S(1)}, f32[128,1536]{1,0:T(8,128)}, u32[]{:S(2)}) copy-start(f32[128,1536]{1,0:T(8,128)} %get-tuple-element.258) | copy-start | bytes 2359300
  253.6 40.6 %collective-permute-start.26 = (bf16[144,1536]{1,0:T(8,128)(2,1)}, bf16[144,1536]{1,0:T(8,128)(2,1)S(1)}, u32[]{:S(2)}, u32[]{:S(2)}) collective-permute-start(bf16[144,1536]{1,0:T(8,128)(2,1)} %get-tuple-element.263), channel_id=1, source_target_pairs={{0,2},{1,3},{2,0},{3,1},{4,6},{5,7},{6,4},{7,5},{8,10},{9,11},{10,... | collective-permute-start | bytes 1327112 | tf_op jit(solution)/shard_map/ppermute | solution.py:470
  259.6 34.7 %collective-permute-start.27 = (bf16[144,1536]{1,0:T(8,128)(2,1)}, bf16[144,1536]{1,0:T(8,128)(2,1)}, u32[]{:S(2)}, u32[]{:S(2)}) collective-permute-start(bf16[144,1536]{1,0:T(8,128)(2,1)} %get-tuple-element.264), channel_id=1, source_target_pairs={{0,4},{1,5},{2,6},{3,7},{4,0},{5,1},{6,2},{7,3},{8,12},{9,13},{10,... | collective-permute-start | bytes 1327112 | tf_op jit(solution)/shard_map/ppermute | solution.py:470
  259.8 34.3 %all-to-all-start.4 = ((f32[32,1,96]{2,1,0:T(1,128)}), f32[32,1,96]{2,1,0:T(1,128)S(1)}, u32[]{:S(2)}, u32[]{:S(2)}) async-start(f32[32,1,96]{2,1,0:T(1,128)} %bitcast.22), calls=%async_computation.4 | async-start | bytes 32768 | tf_op jit(solution)/shard_map/all_to_all | solution.py:485
  263.0 12.2 %collective-permute-start.23 = (bf16[128,1536]{1,0:T(8,128)(2,1)}, bf16[128,1536]{1,0:T(8,128)(2,1)S(1)}, u32[]{:S(2)}, u32[]{:S(2)}) collective-permute-start(bf16[128,1536]{1,0:T(8,128)(2,1)} %get-tuple-element.259), channel_id=1, source_target_pairs={{0,8},{1,9},{2,10},{3,11},{4,12},{5,13},{6,14},{7,15},{8,0},{9,1},... | collective-permute-start | bytes 1179656 | tf_op jit(solution)/shard_map/ppermute | solution.py:470
  264.9 19.6 %collective-permute-start.24 = (bf16[128,1536]{1,0:T(8,128)(2,1)}, bf16[128,1536]{1,0:T(8,128)(2,1)S(1)}, u32[]{:S(2)}, u32[]{:S(2)}) collective-permute-start(bf16[128,1536]{1,0:T(8,128)(2,1)} %get-tuple-element.260), channel_id=1, source_target_pairs={{0,16},{1,17},{2,18},{3,19},{4,20},{5,21},{6,22},{7,23},{8,24},{9,... | collective-permute-start | bytes 1179656 | tf_op jit(solution)/shard_map/ppermute | solution.py:470
  266.3 18.2 %collective-permute-start.25 = (bf16[128,1536]{1,0:T(8,128)(2,1)}, bf16[128,1536]{1,0:T(8,128)(2,1)S(1)}, u32[]{:S(2)}, u32[]{:S(2)}) collective-permute-start(bf16[128,1536]{1,0:T(8,128)(2,1)} %get-tuple-element.261), channel_id=1, source_target_pairs={{0,24},{1,25},{2,26},{3,27},{4,28},{5,29},{6,30},{7,31},{8,16},{9,... | collective-permute-start | bytes 1179656 | tf_op jit(solution)/shard_map/ppermute | solution.py:470
  268.8 16.1 %copy-start.15 = (f32[128,1536]{1,0:T(8,128)S(1)}, f32[128,1536]{1,0:T(8,128)}, u32[]{:S(2)}) copy-start(f32[128,1536]{1,0:T(8,128)} %get-tuple-element.246) | copy-start | bytes 2359300
  275.2 19.0 %collective-permute-start.28 = (bf16[144,1536]{1,0:T(8,128)(2,1)}, bf16[144,1536]{1,0:T(8,128)(2,1)S(1)}, u32[]{:S(2)}, u32[]{:S(2)}) collective-permute-start(bf16[144,1536]{1,0:T(8,128)(2,1)} %get-tuple-element.265), channel_id=1, source_target_pairs={{0,6},{1,7},{2,4},{3,5},{4,2},{5,3},{6,0},{7,1},{8,14},{9,15},{10,... | collective-permute-start | bytes 1327112 | tf_op jit(solution)/shard_map/ppermute | solution.py:470
  (35 other events, 137.6 us)
Sparse Core Ops, SparseCore 0:
  10.3 37.8 all-gather.4
  60.1 65.5 all-gather.6
  128.1 30.9 all-gather.8
  163.6 91.2 reduce-scatter.1

commit v5 on v4

--- a/solution.py
+++ b/solution.py
@@ -530,9 +530,11 @@
     gain_low = low(gains_pair)
     token_rows = tokens.reshape(rows, D)
 
+    token_copies = jnp.tile(token_rows[None], (n_dp, 1, 1))
+    out_low, token_copies = tie(out_low, token_copies)
     out_z = links.gather(out_low, links.z)
     in_group = lax.all_gather(in_low, ("z", "core"), axis=0, tiled=True)
-    token_group = exchange(jnp.tile(token_rows[None], (n_dp, 1, 1)), "dp")
+    token_group = exchange(token_copies, "dp")
     cos_rows, sine_rows = rotary_rows(seq_len, slots, heads_here)
     head = at_dp * heads_here + jnp.arange(group) // HEAD_DIM
     turned = (head < HEADS + KV_HEADS)[None, :]

time: 313 us -> 312 us (level)
  no operation moved by 1% of the time
where the time goes in v5:
time: 312 us; the launch traced here: 306 us
  waiting for transfers between devices  96.2 us (31%)
  Pallas kernels  90.6 us (29%)
  starting transfers between devices  75.9 us (24%)
  other arithmetic  14.8 us (5%)
  between operations  14.5 us (5%)
  local copies, waits for them, and re-layouts  14.2 us (5%)
    pallas_call x14, Pallas kernels, kernel_call(): pl.pallas_call(fetched, out_shape=[jax.ShapeDtypeStruct(s, t) for s, t in...  90.6 us
    ppermute x29, waiting for transfers between devices, send(): lax.ppermute(values, AXES, [(i, i ^ mask) for i in range(self.count)])  76.8 us
    ppermute x29, starting transfers between devices, send(): lax.ppermute(values, AXES, [(i, i ^ mask) for i in range(self.count)])  56.7 us
    all_to_all x5, starting transfers between devices, exchange(): return lax.all_to_all(values, axes, split_axis=0, concat_axis=0, tiled=True)  18.9 us
    all_to_all x5, waiting for transfers between devices, exchange(): return lax.all_to_all(values, axes, split_axis=0, concat_axis=0, tiled=True)  13.2 us
    unnamed x91, local copies, waits for them, and re-layouts  11.5 us
  transfers between devices with their start and end apart: 38, of which 13 were waited for; matrix products, arithmetic and copies ran while one was open for 5% of the time, Pallas kernels for 28%

profile of v5, /device:TPU:0, one launch (start us, length us, event | category | flops | bytes accessed | tf_op | source)
XLA Modules:
  0.0 306.3 jit_solution(8690182932177645224)
XLA Ops:
  7.3 1.9 bitcast_convert_fusion
  11.4 4.0 %collective-permute-start.4 = (bf16[48,1536]{1,0:T(8,128)(2,1)S(1)}, bf16[48,1536]{1,0:T(8,128)(2,1)}, u32[]{:S(2)}, u32[]{:S(2)}) collective-permute-start(bf16[48,1536]{1,0:T(8,128)(2,1)S(1)} %bitcast_convert_fusion.1), channel_id=1, source_target_pairs={{0,4},{1,5},{2,6},{3,7},{4,0},{5,1},{6,2},{7,3},{8,12},{9,13},{10,... | collective-permute-start | bytes 442376 | tf_op jit(solution)/shard_map/ppermute | solution.py:470
  17.0 3.7 %all-to-all-start = ((bf16[4,128,1536]{2,1,0:T(8,128)(2,1)}), bf16[4,128,1536]{2,1,0:T(8,128)(2,1)S(1)}, u32[]{:S(2)}, u32[]{:S(2)}) async-start(bf16[4,128,1536]{2,1,0:T(8,128)(2,1)} %tile.41), calls=%async_computation | async-start | bytes 3145728 | tf_op jit(solution)/shard_map/all_to_all | solution.py:485
  23.6 3.6 %shard_map.385 = (bf16[3,128,1536]{2,1,0:T(8,128)(2,1)}, bf16[4,128,1536]{2,1,0:T(8,128)(2,1)}) custom-call(f32[2,1536,128]{2,1,0:T(8,128)} %refs_1_.5, f32[128,1536]{1,0:T(8,128)} %refs_4_.1, bf16[128,1536]{1,0:T(8,128)(2,1)} %bitcast_select_fusion.refs_2_.refs_7_), custom_call_target="tpu_custom_call" | custom-call | tf_op jit(solution)/shard_map/pallas_call | solution.py:110
  27.9 11.6 %all-to-all-done.refs_1_.refs_3_ = bf16[4,128,1536]{2,1,0:T(8,128)(2,1)S(1)} async-done(((bf16[4,128,1536]{2,1,0:T(8,128)(2,1)}), bf16[4,128,1536]{2,1,0:T(8,128)(2,1)S(1)}, u32[]{:S(2)}, u32[]{:S(2)}) %all-to-all-start) | async-done | bytes 1572896 | tf_op jit(solution)/shard_map/all_to_all | solution.py:485
  40.2 3.9 %all-to-all-start.1 = ((bf16[32,1,96]{2,1,0:T(2,128)(2,1)}), bf16[32,1,96]{2,1,0:T(2,128)(2,1)S(1)}, u32[]{:S(2)}, u32[]{:S(2)}) async-start(bf16[32,1,96]{2,1,0:T(2,128)(2,1)} %copy.46), calls=%async_computation.1 | async-start | bytes 32768 | tf_op jit(solution)/shard_map/all_to_all | solution.py:485
  44.1 2.0 pad_maximum_fusion.1
  46.1 1.7 collective-permute-start.6
  49.6 1.6 all-to-all-done.1
  51.8 4.4 %all-to-all-start.2 = ((bf16[4,128,1536]{2,1,0:T(8,128)(2,1)}), bf16[4,128,1536]{2,1,0:T(8,128)(2,1)}, u32[]{:S(2)}, u32[]{:S(2)}) async-start(bf16[4,128,1536]{2,1,0:T(8,128)(2,1)} %get-tuple-element.185), calls=%async_computation.2 | async-start | bytes 3145728 | tf_op jit(solution)/shard_map/all_to_all | solution.py:485
  56.9 7.5 %shard_map.386 = (bf16[4,128,1536]{2,1,0:T(8,128)(2,1)}, f32[2,1536]{1,0:T(2,128)}, bf16[128,768]{1,0:T(8,128)(2,1)}, bf16[128,768]{1,0:T(8,128)(2,1)}, bf16[128...) custom-call(s32[3]{0:T(128)} %pad_add_fusion.refs_0_, bf16[4,128,1536]{2,1,0:T(8,128)(2,1)} %copy-done.10, ...), custom_call_target="tpu_custom_call" | custom-call | flops 299999985664 | tf_op jit(solution)/shard_map/pallas_call | solution.py:110
  64.4 11.4 %collective-permute-done.7 = bf16[4,48,1536]{2,1,0:T(8,128)(2,1)} collective-permute-done((bf16[4,48,1536]{2,1,0:T(8,128)(2,1)}, bf16[4,48,1536]{2,1,0:T(8,128)(2,1)}, u32[]{:S(2)}, u32[]{:S(2)}) %collective-permute-start.7) | collective-permute-done | bytes 589856 | tf_op jit(solution)/shard_map/ppermute | solution.py:470
  75.8 4.8 %collective-permute-done.8 = bf16[4,48,1536]{2,1,0:T(8,128)(2,1)} collective-permute-done((bf16[4,48,1536]{2,1,0:T(8,128)(2,1)}, bf16[4,48,1536]{2,1,0:T(8,128)(2,1)}, u32[]{:S(2)}, u32[]{:S(2)}) %collective-permute-start.8) | collective-permute-done | bytes 589856 | tf_op jit(solution)/shard_map/ppermute | solution.py:470
  80.6 2.0 pad_maximum_fusion
  82.6 2.3 collective-permute-start
  86.5 5.0 %collective-permute-done.refs_3_ = bf16[128,768]{1,0:T(8,128)(2,1)S(1)} collective-permute-done((bf16[128,768]{1,0:T(8,128)(2,1)S(1)}, bf16[128,768]{1,0:T(8,128)(2,1)S(1)}, u32[]{:S(2)}, u32[]{:S(2)}) %collective-permute-start) | collective-permute-done | bytes 196640 | tf_op jit(solution)/shard_map/ppermute | solution.py:470
  91.5 5.4 %collective-permute-done.1.refs_4_ = bf16[128,768]{1,0:T(8,128)(2,1)S(1)} collective-permute-done((bf16[128,768]{1,0:T(8,128)(2,1)S(1)}, bf16[128,768]{1,0:T(8,128)(2,1)S(1)}, u32[]{:S(2)}, u32[]{:S(2)}) %collective-permute-start.1) | collective-permute-done | bytes 196640 | tf_op jit(solution)/shard_map/ppermute | solution.py:470
  97.6 5.0 %shard_map.387 = (bf16[4,128,768]{2,1,0:T(8,128)(2,1)}, f32[8,256,128]{2,1,0:T(8,128)}, bf16[128,1536]{1,0:T(8,128)(2,1)}) custom-call(s32[3]{0:T(128)} %pad_add_fusion.refs_0_, s32[2]{0:T(128)} %refs_1_.4, bf16[128,768]{1,0:T(8,128)(2,1)} %get-tuple-element.180.refs_2_, bf16[128,768]{1,0:T(8,128)(2,1)} %copy-done.20, bf16[128,768]{1,0:T(8,128)(2,1)} %copy-done.21, ...), custom_call_target="tpu_custom_call" | custom-call | tf_op jit(solution)/shard_map/pallas_call | solution.py:110
  103.0 7.0 %shard_map.388 = (f32[128,1536]{1,0:T(8,128)}, bf16[128,1536]{1,0:T(8,128)(2,1)}) custom-call(s32[3]{0:T(128)} %pad_add_fusion.refs_0_, bf16[128,1536]{1,0:T(8,128)(2,1)} %get-tuple-element.186.refs_1_, bf16[128,1536]{1,0:T(8,128)(2,1)} %bitcast.54, f32[2,1536]{1,0:T(2,128)} %get-tuple-element.187.refs_3_.refs_6_, bf16[16,48,1536]{2,1,0:T(8,128)(2,1)} %bitcast.52, ...), custom_call_target="tpu_custom_call" | custom-call | tf_op jit(solution)/shard_map/pallas_call | solution.py:110
  111.5 2.4 collective-permute-start.11
  114.4 5.3 %shard_map.390 = bf16[32,48,1536]{2,1,0:T(8,128)(2,1)} custom-call(s32[3]{0:T(128)} %pad_add_fusion.refs_0_, bf16[16,48,1536]{2,1,0:T(8,128)(2,1)} %bitcast.53, bf16[16,48,1536]{2,1,0:T(8,128)(2,1)} %collective-permute-done.9.refs_5_.refs_2_), custom_call_target="tpu_custom_call" | custom-call | tf_op jit(solution)/shard_map/pallas_call | solution.py:110
  119.7 5.4 %all-gather.7.cloned.1.call-done.refs_2_.refs_4_.refs_5_ = bf16[3,1024,1536]{2,1,0:T(8,128)(2,1)} async-done(((bf16[3,128,1536]{2,1,0:T(8,128)(2,1)}), bf16[3,1024,1536]{2,1,0:T(8,128)(2,1)}) %all-gather.7.cloned.1.call-update) | async-done | bytes 9437200 | tf_op jit(solution)/shard_map/all_gather | solution.py:559
  125.1 3.7 %copy-done = bf16[3,1024,1536]{2,1,0:T(8,128)(2,1)S(1)} copy-done((bf16[3,1024,1536]{2,1,0:T(8,128)(2,1)S(1)}, bf16[3,1024,1536]{2,1,0:T(8,128)(2,1)}, u32[]{:S(2)}) %copy-start) | copy-done | bytes 9437208
  128.8 6.5 %shard_map.389 = (bf16[512,1536]{1,0:T(8,128)(2,1)S(1)}, f32[512,1024]{1,0:T(8,128)S(1)}) custom-call(s32[3]{0:T(128)S(1)} %copy-done.4, bf16[4,128,1536]{2,1,0:T(8,128)(2,1)} %all-to-all-done.2.refs_1_, bf16[3,1024,1536]{2,1,0:T(8,128)(2,1)S(1)} %copy-done), custom_call_target="tpu_custom_call" | custom-call | tf_op jit(solution)/shard_map/pallas_call | solution.py:110
  135.3 6.2 %collective-permute-done.11.refs_2_ = bf16[128,1536]{1,0:T(8,128)(2,1)S(1)} collective-permute-done((bf16[128,1536]{1,0:T(8,128)(2,1)}, bf16[128,1536]{1,0:T(8,128)(2,1)S(1)}, u32[]{:S(2)}, u32[]{:S(2)}) %collective-permute-start.11) | collective-permute-done | bytes 393248 | tf_op jit(solution)/shard_map/ppermute | solution.py:470
  141.5 9.2 %shard_map.391 = (bf16[512,1536]{1,0:T(8,128)(2,1)S(1)}, bf16[512,1024]{1,0:T(8,128)(2,1)S(1)}, bf16[512,1024]{1,0:T(8,128)(2,1)S(1)}, bf16[512,1024]{1,0:T(8,12...) custom-call(bf16[128,1536]{1,0:T(8,128)(2,1)S(1)} %copy-done.3, ...), custom_call_target="tpu_custom_call" | custom-call | tf_op jit(solution)/shard_map/pallas_call | solution.py:110
  151.6 7.6 %shard_map.392 = (bf16[3,1024,1536]{2,1,0:T(8,128)(2,1)S(1)}, f32[128,1536]{1,0:T(8,128)S(1)}, bf16[128,1536]{1,0:T(8,128)(2,1)S(1)}, bf16[128,1536]{1,0:T(8,128)(2,1)S(1)}, bf16[128,1536]{1,0:T(8,128)(2,1)S(1)}) custom-call(bf16[512,1024]{1,0:T(8,128)(2,1)S(1)} %get-tuple-element.206.refs_0_, bf16[512,1024]{1,0:T(8,128)(2,1)S(1)} %get-tuple-element.207.refs_1_, ...), custom_call_target="tpu_custom_call" | custom-call | tf_op jit(solution)/shard_map/pallas_call | solution.py:110
  159.2 3.7 %copy-done.2 = bf16[3,1024,1536]{2,1,0:T(8,128)(2,1)} copy-done((bf16[3,1024,1536]{2,1,0:T(8,128)(2,1)}, bf16[3,1024,1536]{2,1,0:T(8,128)(2,1)S(1)}, u32[]{:S(2)}) %copy-start.2) | copy-done | bytes 9437208
  162.9 7.5 %collective-permute-start.13 = (bf16[128,1536]{1,0:T(8,128)(2,1)S(1)}, bf16[128,1536]{1,0:T(8,128)(2,1)S(1)}, u32[]{:S(2)}, u32[]{:S(2)}) collective-permute-start(bf16[128,1536]{1,0:T(8,128)(2,1)S(1)} %get-tuple-element.216), channel_id=1, source_target_pairs={{0,2},{1,3},{2,0},{3,1},{4,6},{5,7},{6,4},{7,5},{8,10},{9,11},{10,... | collective-permute-start | bytes 1179656 | tf_op jit(solution)/shard_map/ppermute | solution.py:470
  172.8 12.3 %collective-permute-done.13.refs_2_ = bf16[128,1536]{1,0:T(8,128)(2,1)S(1)} collective-permute-done((bf16[128,1536]{1,0:T(8,128)(2,1)S(1)}, bf16[128,1536]{1,0:T(8,128)(2,1)S(1)}, u32[]{:S(2)}, u32[]{:S(2)}) %collective-permute-start.13) | collective-permute-done | bytes 393248 | tf_op jit(solution)/shard_map/ppermute | solution.py:470
  185.1 19.3 %collective-permute-done.14.refs_3_ = bf16[128,1536]{1,0:T(8,128)(2,1)S(1)} collective-permute-done((bf16[128,1536]{1,0:T(8,128)(2,1)S(1)}, bf16[128,1536]{1,0:T(8,128)(2,1)S(1)}, u32[]{:S(2)}, u32[]{:S(2)}) %collective-permute-start.14) | collective-permute-done | bytes 393248 | tf_op jit(solution)/shard_map/ppermute | solution.py:470
  204.4 2.4 collective-permute-start.16
  206.8 9.4 %shard_map.393 = (f32[128,1536]{1,0:T(8,128)}, bf16[128,1536]{1,0:T(8,128)(2,1)}, f32[1,1536]{1,0:T(1,128)}, bf16[4,128,768]{2,1,0:T(8,128)(2,1)}, bf16[128,384]...) custom-call(s32[3]{0:T(128)} %pad_add_fusion.refs_0_, ...), custom_call_target="tpu_custom_call" | custom-call | flops 30000001024 | tf_op jit(solution)/shard_map/pallas_call | solution.py:110
  217.0 3.8 %all-to-all-start.3 = ((bf16[4,128,768]{2,1,0:T(8,128)(2,1)}), bf16[4,128,768]{2,1,0:T(8,128)(2,1)S(1)}, u32[]{:S(2)}, u32[]{:S(2)}) async-start(bf16[4,128,768]{2,1,0:T(8,128)(2,1)} %get-tuple-element.230), calls=%async_computation.3 | async-start | bytes 1572864 | tf_op jit(solution)/shard_map/all_to_all | solution.py:485
  221.1 1.7 collective-permute-start.17
  224.6 9.6 %collective-permute-start.21 = (bf16[128,1536]{1,0:T(8,128)(2,1)S(1)}, bf16[128,1536]{1,0:T(8,128)(2,1)}, u32[]{:S(2)}, u32[]{:S(2)}) collective-permute-start(bf16[128,1536]{1,0:T(8,128)(2,1)S(1)} %get-tuple-element.243), channel_id=1, source_target_pairs={{0,2},{1,3},{2,0},{3,1},{4,6},{5,7},{6,4},{7,5},{8,10},{9,11},{10,... | collective-permute-start | bytes 1179656 | tf_op jit(solution)/shard_map/ppermute | solution.py:470
  235.8 7.5 %shard_map.394 = (f32[4,144,1536]{2,1,0:T(8,128)}, bf16[4,144,1536]{2,1,0:T(8,128)(2,1)}) custom-call(s32[3]{0:T(128)} %pad_add_fusion.refs_0_, bf16[4,128,768]{2,1,0:T(8,128)(2,1)} %copy-done.13, bf16[4,128,1536]{2,1,0:T(8,128)(2,1)} %get-tuple-element.236.refs_2_, bf16[4,128,1536]{2,1,0:T(8,128)(2,1)} %bitcast.69, ...), custom_call_target="tpu_custom_call" | custom-call | flops 30000001024 | tf_op jit(solution)/shard_map/pallas_call | solution.py:110
  243.5 5.3 %shard_map.395 = (f32[32,96]{1,0:T(8,128)}, f32[128,1536]{1,0:T(8,128)}, bf16[128,1536]{1,0:T(8,128)(2,1)}, bf16[128,1536]{1,0:T(8,128)(2,1)}, bf16[128,1536]{1,0:T(8,128)(2,1)}) custom-call(s32[3]{0:T(128)} %pad_add_fusion.refs_0_, bf16[4,128,768]{2,1,0:T(8,128)(2,1)} %copy-done.13, bf16[768,1536]{1,0:T(8,128)(2,1)} %all-gather.5.cloned.1.call-done.refs_2_, ...), custom_call_target="tpu_custom_call" | custom-call | flops 30000001024 | tf_op jit(solution)/shard_map/pallas_call | solution.py:110
  248.9 4.1 %shard_map.396 = (f32[144,1536]{1,0:T(8,128)}, bf16[144,1536]{1,0:T(8,128)(2,1)}, bf16[144,1536]{1,0:T(8,128)(2,1)}, bf16[144,1536]{1,0:T(8,128)(2,1)}) custom-call(f32[4,144,1536]{2,1,0:T(8,128)} %get-tuple-element.259.refs_0_, bf16[4,144,1536]{2,1,0:T(8,128)(2,1)} %collective-permute-done.20.refs_1_), custom_call_target="tpu_custom_call" | custom-call | tf_op jit(solution)/shard_map/pallas_call | solution.py:110
  253.0 6.0 %collective-permute-start.26 = (bf16[144,1536]{1,0:T(8,128)(2,1)}, bf16[144,1536]{1,0:T(8,128)(2,1)S(1)}, u32[]{:S(2)}, u32[]{:S(2)}) collective-permute-start(bf16[144,1536]{1,0:T(8,128)(2,1)} %get-tuple-element.267), channel_id=1, source_target_pairs={{0,2},{1,3},{2,0},{3,1},{4,6},{5,7},{6,4},{7,5},{8,10},{9,11},{10,... | collective-permute-start | bytes 1327112 | tf_op jit(solution)/shard_map/ppermute | solution.py:470
  259.3 3.2 %all-to-all-start.4 = ((f32[32,1,96]{2,1,0:T(1,128)}), f32[32,1,96]{2,1,0:T(1,128)S(1)}, u32[]{:S(2)}, u32[]{:S(2)}) async-start(f32[32,1,96]{2,1,0:T(1,128)} %bitcast.22), calls=%async_computation.4 | async-start | bytes 32768 | tf_op jit(solution)/shard_map/all_to_all | solution.py:485
  262.4 1.8 collective-permute-start.23
  266.0 2.2 select_convert_fusion
  268.2 6.4 %collective-permute-done.23 = bf16[128,1536]{1,0:T(8,128)(2,1)S(1)} collective-permute-done((bf16[128,1536]{1,0:T(8,128)(2,1)}, bf16[128,1536]{1,0:T(8,128)(2,1)S(1)}, u32[]{:S(2)}, u32[]{:S(2)}) %collective-permute-start.23) | collective-permute-done | bytes 393248 | tf_op jit(solution)/shard_map/ppermute | solution.py:470
  274.6 3.7 %collective-permute-start.28 = (bf16[144,1536]{1,0:T(8,128)(2,1)}, bf16[144,1536]{1,0:T(8,128)(2,1)S(1)}, u32[]{:S(2)}, u32[]{:S(2)}) collective-permute-start(bf16[144,1536]{1,0:T(8,128)(2,1)} %get-tuple-element.269), channel_id=1, source_target_pairs={{0,6},{1,7},{2,4},{3,5},{4,2},{5,3},{6,0},{7,1},{8,14},{9,15},{10,... | collective-permute-start | bytes 1327112 | tf_op jit(solution)/shard_map/ppermute | solution.py:470
  278.3 5.6 %collective-permute-done.24 = bf16[128,1536]{1,0:T(8,128)(2,1)S(1)} collective-permute-done((bf16[128,1536]{1,0:T(8,128)(2,1)}, bf16[128,1536]{1,0:T(8,128)(2,1)S(1)}, u32[]{:S(2)}, u32[]{:S(2)}) %collective-permute-start.24) | collective-permute-done | bytes 393248 | tf_op jit(solution)/shard_map/ppermute | solution.py:470
  285.6 8.0 %shard_map.397 = (f32[2,1536,128]{2,1,0:T(8,128)}, f32[2,1536,128]{2,1,0:T(8,128)}, f32[2,1536,128]{2,1,0:T(8,128)}, f32[2,1536,128]{2,1,0:T(8,128)}, bf16[2,153...) custom-call(bf16[3,128,1536]{2,1,0:T(8,128)(2,1)} %reduce-scatter.2., ...), custom_call_target="tpu_custom_call" | custom-call | tf_op jit(solution)/shard_map/pallas_call | solution.py:110
  295.0 4.7 %shard_map.398 = (f32[96,1536]{1,0:T(8,128)}, f32[96,1536]{1,0:T(8,128)}, f32[96,1536]{1,0:T(8,128)}, f32[96,1536]{1,0:T(8,128)}, bf16[96,1536]{1,0:T(8,128)(2,1...) custom-call(f32[144,1536]{1,0:T(8,128)} %get-tuple-element.282.refs_, ...), custom_call_target="tpu_custom_call" | custom-call | tf_op jit(solution)/shard_map/pallas_call | solution.py:110
  (171 shorter events, 28.8 us)
Async XLA Ops:
  7.2 44.6 %all-gather.5.cloned.1.call-start = ((), (), s32[]{:S(2)}) async-start(), calls=%async_computation.6 | async-start | bytes 2654208 | tf_op jit(solution)/shard_map/all_gather | solution.py:536
  11.4 32.7 %collective-permute-start.4 = (bf16[48,1536]{1,0:T(8,128)(2,1)S(1)}, bf16[48,1536]{1,0:T(8,128)(2,1)}, u32[]{:S(2)}, u32[]{:S(2)}) collective-permute-start(bf16[48,1536]{1,0:T(8,128)(2,1)S(1)} %bitcast_convert_fusion.1), channel_id=1, source_target_pairs={{0,4},{1,5},{2,6},{3,7},{4,0},{5,1},{6,2},{7,3},{8,12},{9,13},{10,... | collective-permute-start | bytes 442376 | tf_op jit(solution)/shard_map/ppermute | solution.py:470
  15.4 28.7 %collective-permute-start.5 = (bf16[48,1536]{1,0:T(8,128)(2,1)S(1)}, bf16[48,1536]{1,0:T(8,128)(2,1)}, u32[]{:S(2)}, u32[]{:S(2)}) collective-permute-start(bf16[48,1536]{1,0:T(8,128)(2,1)S(1)} %bitcast_convert_fusion.1), channel_id=1, source_target_pairs={{0,6},{1,7},{2,4},{3,5},{4,2},{5,3},{6,0},{7,1},{8,14},{9,15},{10,... | collective-permute-start | bytes 442376 | tf_op jit(solution)/shard_map/ppermute | solution.py:470
  16.8 27.3 %collective-permute-start.3 = (bf16[48,1536]{1,0:T(8,128)(2,1)S(1)}, bf16[48,1536]{1,0:T(8,128)(2,1)}, u32[]{:S(2)}, u32[]{:S(2)}) collective-permute-start(bf16[48,1536]{1,0:T(8,128)(2,1)S(1)} %bitcast_convert_fusion.1), channel_id=1, source_target_pairs={{0,2},{1,3},{2,0},{3,1},{4,6},{5,7},{6,4},{7,5},{8,10},{9,11},{10,... | collective-permute-start | bytes 442376 | tf_op jit(solution)/shard_map/ppermute | solution.py:470
  17.0 22.5 %all-to-all-start = ((bf16[4,128,1536]{2,1,0:T(8,128)(2,1)}), bf16[4,128,1536]{2,1,0:T(8,128)(2,1)S(1)}, u32[]{:S(2)}, u32[]{:S(2)}) async-start(bf16[4,128,1536]{2,1,0:T(8,128)(2,1)} %tile.41), calls=%async_computation | async-start | bytes 3145728 | tf_op jit(solution)/shard_map/all_to_all | solution.py:485
  39.5 12.3 %copy-start.10 = (bf16[4,128,1536]{2,1,0:T(8,128)(2,1)}, bf16[4,128,1536]{2,1,0:T(8,128)(2,1)S(1)}, u32[]{:S(2)}) copy-start(bf16[4,128,1536]{2,1,0:T(8,128)(2,1)S(1)} %all-to-all-done.refs_1_.refs_3_) | copy-start | bytes 4718596
  40.2 11.0 %all-to-all-start.1 = ((bf16[32,1,96]{2,1,0:T(2,128)(2,1)}), bf16[32,1,96]{2,1,0:T(2,128)(2,1)S(1)}, u32[]{:S(2)}, u32[]{:S(2)}) async-start(bf16[32,1,96]{2,1,0:T(2,128)(2,1)} %copy.46), calls=%async_computation.1 | async-start | bytes 32768 | tf_op jit(solution)/shard_map/all_to_all | solution.py:485
  46.1 18.3 %collective-permute-start.6 = (bf16[4,48,1536]{2,1,0:T(8,128)(2,1)}, bf16[4,48,1536]{2,1,0:T(8,128)(2,1)}, u32[]{:S(2)}, u32[]{:S(2)}) collective-permute-start(bf16[4,48,1536]{2,1,0:T(8,128)(2,1)} %pad_maximum_fusion.1), channel_id=1, source_target_pairs={{0,8},{1,9},{2,10},{3,11},{4,12},{5,13},{6,14},{7,15},{8,0},{9,1},... | collective-permute-start | bytes 1769480 | tf_op jit(solution)/shard_map/ppermute | solution.py:470
  47.8 28.0 %collective-permute-start.7 = (bf16[4,48,1536]{2,1,0:T(8,128)(2,1)}, bf16[4,48,1536]{2,1,0:T(8,128)(2,1)}, u32[]{:S(2)}, u32[]{:S(2)}) collective-permute-start(bf16[4,48,1536]{2,1,0:T(8,128)(2,1)} %pad_maximum_fusion.1), channel_id=1, source_target_pairs={{0,16},{1,17},{2,18},{3,19},{4,20},{5,21},{6,22},{7,23},{8,24},{9,... | collective-permute-start | bytes 1769480 | tf_op jit(solution)/shard_map/ppermute | solution.py:470
  49.3 31.3 %collective-permute-start.8 = (bf16[4,48,1536]{2,1,0:T(8,128)(2,1)}, bf16[4,48,1536]{2,1,0:T(8,128)(2,1)}, u32[]{:S(2)}, u32[]{:S(2)}) collective-permute-start(bf16[4,48,1536]{2,1,0:T(8,128)(2,1)} %pad_maximum_fusion.1), channel_id=1, source_target_pairs={{0,24},{1,25},{2,26},{3,27},{4,28},{5,29},{6,30},{7,31},{8,16},{9,... | collective-permute-start | bytes 1769480 | tf_op jit(solution)/shard_map/ppermute | solution.py:470
  51.8 50.9 %all-to-all-start.2 = ((bf16[4,128,1536]{2,1,0:T(8,128)(2,1)}), bf16[4,128,1536]{2,1,0:T(8,128)(2,1)}, u32[]{:S(2)}, u32[]{:S(2)}) async-start(bf16[4,128,1536]{2,1,0:T(8,128)(2,1)} %get-tuple-element.185), calls=%async_computation.2 | async-start | bytes 3145728 | tf_op jit(solution)/shard_map/all_to_all | solution.py:485
  56.1 69.0 %all-gather.7.cloned.1.call-start = ((), (), s32[]{:S(2)}) async-start(), calls=%async_computation.7 | async-start | bytes 10616832 | tf_op jit(solution)/shard_map/all_gather | solution.py:559
  56.9 178.1 %all-gather.9.cloned.1.call-start = ((), (), s32[]{:S(2)}) async-start(), calls=%async_computation.9 | async-start | bytes 1966080 | tf_op jit(solution)/shard_map/all_gather | solution.py:615
  82.5 20.4 %copy-start.6 = (bf16[4,4,48,1536]{3,2,1,0:T(8,128)(2,1)}, bf16[4,4,48,1536]{3,2,1,0:T(8,128)(2,1)S(1)}, u32[]{:S(2)}) copy-start(bf16[4,4,48,1536]{3,2,1,0:T(8,128)(2,1)S(1)} %pad_maximum_fusion) | copy-start | bytes 7077892
  82.6 20.4 %collective-permute-start.9 = (bf16[16,48,1536]{2,1,0:T(8,128)(2,1)S(1)}, bf16[16,48,1536]{2,1,0:T(8,128)(2,1)}, u32[]{:S(2)}, u32[]{:S(2)}) collective-permute-start(bf16[16,48,1536]{2,1,0:T(8,128)(2,1)S(1)} %bitcast.51), channel_id=1, source_target_pairs={{0,1},{1,0},{2,3},{3,2},{4,5},{5,4},{6,7},{7,6},{8,9},{9,8},{10,11... | collective-permute-start | bytes 7077896 | tf_op jit(solution)/shard_map/ppermute | solution.py:470
  82.6 8.8 %collective-permute-start = (bf16[128,768]{1,0:T(8,128)(2,1)S(1)}, bf16[128,768]{1,0:T(8,128)(2,1)S(1)}, u32[]{:S(2)}, u32[]{:S(2)}) collective-permute-start(bf16[128,768]{1,0:T(8,128)(2,1)S(1)} %copy-done.38), channel_id=1, source_target_pairs={{0,8},{1,9},{2,10},{3,11},{4,12},{5,13},{6,14},{7,15},{8,0},{9,1},... | collective-permute-start | bytes 589832 | tf_op jit(solution)/shard_map/ppermute | solution.py:470
  84.9 11.9 %collective-permute-start.1 = (bf16[128,768]{1,0:T(8,128)(2,1)S(1)}, bf16[128,768]{1,0:T(8,128)(2,1)S(1)}, u32[]{:S(2)}, u32[]{:S(2)}) collective-permute-start(bf16[128,768]{1,0:T(8,128)(2,1)S(1)} %copy-done.37), channel_id=1, source_target_pairs={{0,16},{1,17},{2,18},{3,19},{4,20},{5,21},{6,22},{7,23},{8,24},{9,... | collective-permute-start | bytes 589832 | tf_op jit(solution)/shard_map/ppermute | solution.py:470
  85.8 11.1 %collective-permute-start.2 = (bf16[128,768]{1,0:T(8,128)(2,1)S(1)}, bf16[128,768]{1,0:T(8,128)(2,1)S(1)}, u32[]{:S(2)}, u32[]{:S(2)}) collective-permute-start(bf16[128,768]{1,0:T(8,128)(2,1)S(1)} %copy-done.36), channel_id=1, source_target_pairs={{0,24},{1,25},{2,26},{3,27},{4,28},{5,29},{6,30},{7,31},{8,16},{9,... | collective-permute-start | bytes 589832 | tf_op jit(solution)/shard_map/ppermute | solution.py:470
  102.7 182.9 %reduce-scatter.2.cloned.1.call-start = ((), (), s32[]{:S(2)}) async-start(), calls=%async_computation.8 | async-start | bytes 10616832 | tf_op jit(solution)/shard_map/reduce_scatter | solution.py:660
  109.9 15.2 %copy-start.4 = (s32[3]{0:T(128)S(1)}, s32[3]{0:T(128)}, u32[]{:S(2)}) copy-start(s32[3]{0:T(128)} %pad_add_fusion.refs_0_) | copy-start | bytes 40
  109.9 25.4 %collective-permute-start.10 = (bf16[128,1536]{1,0:T(8,128)(2,1)}, bf16[128,1536]{1,0:T(8,128)(2,1)S(1)}, u32[]{:S(2)}, u32[]{:S(2)}) collective-permute-start(bf16[128,1536]{1,0:T(8,128)(2,1)} %get-tuple-element.201.refs_0_), channel_id=1, source_target_pairs={{0,2},{1,3},{2,0},{3,1},{4,6},{5,7},{6,4},{7,5},{8,10},{9,11},{10,... | collective-permute-start | bytes 1179656 | tf_op jit(solution)/shard_map/ppermute | solution.py:470
  111.5 30.0 %collective-permute-start.11 = (bf16[128,1536]{1,0:T(8,128)(2,1)}, bf16[128,1536]{1,0:T(8,128)(2,1)S(1)}, u32[]{:S(2)}, u32[]{:S(2)}) collective-permute-start(bf16[128,1536]{1,0:T(8,128)(2,1)} %get-tuple-element.201.refs_0_), channel_id=1, source_target_pairs={{0,4},{1,5},{2,6},{3,7},{4,0},{5,1},{6,2},{7,3},{8,12},{9,13},{10,... | collective-permute-start | bytes 1179656 | tf_op jit(solution)/shard_map/ppermute | solution.py:470
  113.9 27.6 %collective-permute-start.12 = (bf16[128,1536]{1,0:T(8,128)(2,1)}, bf16[128,1536]{1,0:T(8,128)(2,1)S(1)}, u32[]{:S(2)}, u32[]{:S(2)}) collective-permute-start(bf16[128,1536]{1,0:T(8,128)(2,1)} %get-tuple-element.201.refs_0_), channel_id=1, source_target_pairs={{0,6},{1,7},{2,4},{3,5},{4,2},{5,3},{6,0},{7,1},{8,14},{9,15},{10,... | collective-permute-start | bytes 1179656 | tf_op jit(solution)/shard_map/ppermute | solution.py:470
  128.8 12.7 %copy-start.1 = (bf16[3,1024,1536]{2,1,0:T(8,128)(2,1)S(1)}, bf16[3,1024,1536]{2,1,0:T(8,128)(2,1)}, u32[]{:S(2)}) copy-start(bf16[3,1024,1536]{2,1,0:T(8,128)(2,1)} %all-gather.7.cloned.1.call-done.refs_2_.refs_4_.refs_5_) | copy-start | bytes 28311556
  128.8 12.7 %copy-start.3 = (bf16[128,1536]{1,0:T(8,128)(2,1)S(1)}, bf16[128,1536]{1,0:T(8,128)(2,1)}, u32[]{:S(2)}) copy-start(bf16[128,1536]{1,0:T(8,128)(2,1)} %get-tuple-element.201.refs_0_) | copy-start | bytes 1179652
  162.9 22.2 %collective-permute-start.13 = (bf16[128,1536]{1,0:T(8,128)(2,1)S(1)}, bf16[128,1536]{1,0:T(8,128)(2,1)S(1)}, u32[]{:S(2)}, u32[]{:S(2)}) collective-permute-start(bf16[128,1536]{1,0:T(8,128)(2,1)S(1)} %get-tuple-element.216), channel_id=1, source_target_pairs={{0,2},{1,3},{2,0},{3,1},{4,6},{5,7},{6,4},{7,5},{8,10},{9,11},{10,... | collective-permute-start | bytes 1179656 | tf_op jit(solution)/shard_map/ppermute | solution.py:470
  170.3 34.0 %collective-permute-start.14 = (bf16[128,1536]{1,0:T(8,128)(2,1)S(1)}, bf16[128,1536]{1,0:T(8,128)(2,1)S(1)}, u32[]{:S(2)}, u32[]{:S(2)}) collective-permute-start(bf16[128,1536]{1,0:T(8,128)(2,1)S(1)} %get-tuple-element.217), channel_id=1, source_target_pairs={{0,4},{1,5},{2,6},{3,7},{4,0},{5,1},{6,2},{7,3},{8,12},{9,13},{10,... | collective-permute-start | bytes 1179656 | tf_op jit(solution)/shard_map/ppermute | solution.py:470
  171.3 33.0 %collective-permute-start.15 = (bf16[128,1536]{1,0:T(8,128)(2,1)S(1)}, bf16[128,1536]{1,0:T(8,128)(2,1)S(1)}, u32[]{:S(2)}, u32[]{:S(2)}) collective-permute-start(bf16[128,1536]{1,0:T(8,128)(2,1)S(1)} %get-tuple-element.218), channel_id=1, source_target_pairs={{0,6},{1,7},{2,4},{3,5},{4,2},{5,3},{6,0},{7,1},{8,14},{9,15},{10,... | collective-permute-start | bytes 1179656 | tf_op jit(solution)/shard_map/ppermute | solution.py:470
  185.1 21.7 %copy-start.33 = (bf16[128,1536]{1,0:T(8,128)(2,1)}, bf16[128,1536]{1,0:T(8,128)(2,1)S(1)}, u32[]{:S(2)}) copy-start(bf16[128,1536]{1,0:T(8,128)(2,1)S(1)} %collective-permute-done.13.refs_2_) | copy-start | bytes 1179652
  204.4 11.9 %collective-permute-start.16 = (bf16[128,1536]{1,0:T(8,128)(2,1)S(1)}, bf16[128,1536]{1,0:T(8,128)(2,1)S(1)}, u32[]{:S(2)}, u32[]{:S(2)}) collective-permute-start(bf16[128,1536]{1,0:T(8,128)(2,1)S(1)} %get-tuple-element.229), channel_id=1, source_target_pairs={{0,6},{1,7},{2,4},{3,5},{4,2},{5,3},{6,0},{7,1},{8,14},{9,15},{10,... | collective-permute-start | bytes 1179656 | tf_op jit(solution)/shard_map/ppermute | solution.py:470
  217.0 17.9 %all-to-all-start.3 = ((bf16[4,128,768]{2,1,0:T(8,128)(2,1)}), bf16[4,128,768]{2,1,0:T(8,128)(2,1)S(1)}, u32[]{:S(2)}, u32[]{:S(2)}) async-start(bf16[4,128,768]{2,1,0:T(8,128)(2,1)} %get-tuple-element.230), calls=%async_computation.3 | async-start | bytes 1572864 | tf_op jit(solution)/shard_map/all_to_all | solution.py:485
  221.1 13.3 %collective-permute-start.17 = (bf16[128,384]{1,0:T(8,128)(2,1)S(1)}, bf16[128,384]{1,0:T(8,128)(2,1)S(1)}, u32[]{:S(2)}, u32[]{:S(2)}) collective-permute-start(bf16[128,384]{1,0:T(8,128)(2,1)S(1)} %copy-done.41), channel_id=1, source_target_pairs={{0,8},{1,9},{2,10},{3,11},{4,12},{5,13},{6,14},{7,15},{8,0},{9,1},... | collective-permute-start | bytes 294920 | tf_op jit(solution)/shard_map/ppermute | solution.py:470
  222.8 11.6 %collective-permute-start.18 = (bf16[128,384]{1,0:T(8,128)(2,1)S(1)}, bf16[128,384]{1,0:T(8,128)(2,1)S(1)}, u32[]{:S(2)}, u32[]{:S(2)}) collective-permute-start(bf16[128,384]{1,0:T(8,128)(2,1)S(1)} %copy-done.40), channel_id=1, source_target_pairs={{0,16},{1,17},{2,18},{3,19},{4,20},{5,21},{6,22},{7,23},{8,24},{9,... | collective-permute-start | bytes 294920 | tf_op jit(solution)/shard_map/ppermute | solution.py:470
  224.3 10.6 %collective-permute-start.19 = (bf16[128,384]{1,0:T(8,128)(2,1)S(1)}, bf16[128,384]{1,0:T(8,128)(2,1)S(1)}, u32[]{:S(2)}, u32[]{:S(2)}) collective-permute-start(bf16[128,384]{1,0:T(8,128)(2,1)S(1)} %copy-done.39), channel_id=1, source_target_pairs={{0,24},{1,25},{2,26},{3,27},{4,28},{5,29},{6,30},{7,31},{8,16},{9,... | collective-permute-start | bytes 294920 | tf_op jit(solution)/shard_map/ppermute | solution.py:470
  224.6 24.2 %collective-permute-start.21 = (bf16[128,1536]{1,0:T(8,128)(2,1)S(1)}, bf16[128,1536]{1,0:T(8,128)(2,1)}, u32[]{:S(2)}, u32[]{:S(2)}) collective-permute-start(bf16[128,1536]{1,0:T(8,128)(2,1)S(1)} %get-tuple-element.243), channel_id=1, source_target_pairs={{0,2},{1,3},{2,0},{3,1},{4,6},{5,7},{6,4},{7,5},{8,10},{9,11},{10,... | collective-permute-start | bytes 1179656 | tf_op jit(solution)/shard_map/ppermute | solution.py:470
  234.2 14.7 %collective-permute-start.22 = (bf16[128,1536]{1,0:T(8,128)(2,1)S(1)}, bf16[128,1536]{1,0:T(8,128)(2,1)}, u32[]{:S(2)}, u32[]{:S(2)}) collective-permute-start(bf16[128,1536]{1,0:T(8,128)(2,1)S(1)} %get-tuple-element.244), channel_id=1, source_target_pairs={{0,4},{1,5},{2,6},{3,7},{4,0},{5,1},{6,2},{7,3},{8,12},{9,13},{10,... | collective-permute-start | bytes 1179656 | tf_op jit(solution)/shard_map/ppermute | solution.py:470
  243.4 5.5 %collective-permute-start.20 = (bf16[4,144,1536]{2,1,0:T(8,128)(2,1)}, bf16[4,144,1536]{2,1,0:T(8,128)(2,1)}, u32[]{:S(2)}, u32[]{:S(2)}) collective-permute-start(bf16[4,144,1536]{2,1,0:T(8,128)(2,1)} %get-tuple-element.241), channel_id=1, source_target_pairs={{0,1},{1,0},{2,3},{3,2},{4,5},{5,4},{6,7},{7,6},{8,9},{9,8},{10,11... | collective-permute-start | bytes 5308424 | tf_op jit(solution)/shard_map/ppermute | solution.py:470
  248.8 17.2 %copy-start.15 = (f32[128,1536]{1,0:T(8,128)S(1)}, f32[128,1536]{1,0:T(8,128)}, u32[]{:S(2)}) copy-start(f32[128,1536]{1,0:T(8,128)} %get-tuple-element.194.refs_5_) | copy-start | bytes 2359300
  248.8 17.2 %copy-start.26 = (pred[128]{0:T(512)(128)(4,1)S(1)}, pred[128]{0:T(512)(128)(4,1)}, u32[]{:S(2)}) copy-start(pred[128]{0:T(512)(128)(4,1)} %copy-done.25) | copy-start | bytes 388
  253.0 30.9 %copy-start.9 = (f32[128,1536]{1,0:T(8,128)S(1)}, f32[128,1536]{1,0:T(8,128)}, u32[]{:S(2)}) copy-start(f32[128,1536]{1,0:T(8,128)} %get-tuple-element.262) | copy-start | bytes 2359300
  253.0 40.6 %collective-permute-start.26 = (bf16[144,1536]{1,0:T(8,128)(2,1)}, bf16[144,1536]{1,0:T(8,128)(2,1)S(1)}, u32[]{:S(2)}, u32[]{:S(2)}) collective-permute-start(bf16[144,1536]{1,0:T(8,128)(2,1)} %get-tuple-element.267), channel_id=1, source_target_pairs={{0,2},{1,3},{2,0},{3,1},{4,6},{5,7},{6,4},{7,5},{8,10},{9,11},{10,... | collective-permute-start | bytes 1327112 | tf_op jit(solution)/shard_map/ppermute | solution.py:470
  258.9 34.7 %collective-permute-start.27 = (bf16[144,1536]{1,0:T(8,128)(2,1)}, bf16[144,1536]{1,0:T(8,128)(2,1)}, u32[]{:S(2)}, u32[]{:S(2)}) collective-permute-start(bf16[144,1536]{1,0:T(8,128)(2,1)} %get-tuple-element.268), channel_id=1, source_target_pairs={{0,4},{1,5},{2,6},{3,7},{4,0},{5,1},{6,2},{7,3},{8,12},{9,13},{10,... | collective-permute-start | bytes 1327112 | tf_op jit(solution)/shard_map/ppermute | solution.py:470
  259.3 34.3 %all-to-all-start.4 = ((f32[32,1,96]{2,1,0:T(1,128)}), f32[32,1,96]{2,1,0:T(1,128)S(1)}, u32[]{:S(2)}, u32[]{:S(2)}) async-start(f32[32,1,96]{2,1,0:T(1,128)} %bitcast.22), calls=%async_computation.4 | async-start | bytes 32768 | tf_op jit(solution)/shard_map/all_to_all | solution.py:485
  262.4 12.2 %collective-permute-start.23 = (bf16[128,1536]{1,0:T(8,128)(2,1)}, bf16[128,1536]{1,0:T(8,128)(2,1)S(1)}, u32[]{:S(2)}, u32[]{:S(2)}) collective-permute-start(bf16[128,1536]{1,0:T(8,128)(2,1)} %get-tuple-element.263), channel_id=1, source_target_pairs={{0,8},{1,9},{2,10},{3,11},{4,12},{5,13},{6,14},{7,15},{8,0},{9,1},... | collective-permute-start | bytes 1179656 | tf_op jit(solution)/shard_map/ppermute | solution.py:470
  264.3 19.6 %collective-permute-start.24 = (bf16[128,1536]{1,0:T(8,128)(2,1)}, bf16[128,1536]{1,0:T(8,128)(2,1)S(1)}, u32[]{:S(2)}, u32[]{:S(2)}) collective-permute-start(bf16[128,1536]{1,0:T(8,128)(2,1)} %get-tuple-element.264), channel_id=1, source_target_pairs={{0,16},{1,17},{2,18},{3,19},{4,20},{5,21},{6,22},{7,23},{8,24},{9,... | collective-permute-start | bytes 1179656 | tf_op jit(solution)/shard_map/ppermute | solution.py:470
  265.7 18.2 %collective-permute-start.25 = (bf16[128,1536]{1,0:T(8,128)(2,1)}, bf16[128,1536]{1,0:T(8,128)(2,1)S(1)}, u32[]{:S(2)}, u32[]{:S(2)}) collective-permute-start(bf16[128,1536]{1,0:T(8,128)(2,1)} %get-tuple-element.265), channel_id=1, source_target_pairs={{0,24},{1,25},{2,26},{3,27},{4,28},{5,29},{6,30},{7,31},{8,16},{9,... | collective-permute-start | bytes 1179656 | tf_op jit(solution)/shard_map/ppermute | solution.py:470
  268.2 16.1 %copy-start.14 = (f32[128,1536]{1,0:T(8,128)S(1)}, f32[128,1536]{1,0:T(8,128)}, u32[]{:S(2)}) copy-start(f32[128,1536]{1,0:T(8,128)} %get-tuple-element.250) | copy-start | bytes 2359300
  274.6 19.0 %collective-permute-start.28 = (bf16[144,1536]{1,0:T(8,128)(2,1)}, bf16[144,1536]{1,0:T(8,128)(2,1)S(1)}, u32[]{:S(2)}, u32[]{:S(2)}) collective-permute-start(bf16[144,1536]{1,0:T(8,128)(2,1)} %get-tuple-element.269), channel_id=1, source_target_pairs={{0,6},{1,7},{2,4},{3,5},{4,2},{5,3},{6,0},{7,1},{8,14},{9,15},{10,... | collective-permute-start | bytes 1327112 | tf_op jit(solution)/shard_map/ppermute | solution.py:470
  (35 other events, 127.6 us)
Sparse Core Ops, SparseCore 0:
  10.3 38.2 all-gather.4
  59.5 65.5 all-gather.6
  127.5 30.9 all-gather.8
  163.0 91.2 reduce-scatter.1
